TPU v7x, 32 devices: a whole 2x2x4 slice. The times are simulated.
32 devices in a mesh: grp: 2 (over x), tp: 16 (over z, y, core).
Axes of the slice: x: 2, y: 2, z: 4, core: 2. Of those that a mesh axis runs over, the one named last changes fastest.
Arguments:
- activations: bfloat16 [16384, 8192], P('grp', 'tp'), parts along dimension 0, may hold values from -6 to 6
- out_grads: bfloat16 [16384, 28672], P('grp', 'tp'), parts along dimension 0, may hold values from -6 to 6
- proj_in: bfloat16 [8192, 64], P('tp'), may hold values from -0.0625 to 0.0625
- proj_out: bfloat16 [28672, 64], P('tp'), may hold values from -0.03125 to 0.03125
- seg_ids: int32 [16384], P('grp'), parts along dimension 0, may hold values from 0 to 7, never falling along the last dimension, each value on 1 to 4096 neighbouring positions
- queries: float32 [1024, 4096], P('tp'), may hold values from -6 to 6
Outputs:
- scores: float32 [16, 1024], P('grp', 'tp'), parts along dimension 0
There are 2 independent parts, one for each index of `grp`. A program takes and returns all parts, laid end to end along the dimension named above; an argument that names none is the same for every part. Nothing has to cross between parts.
Inputs may be any that keep to these rules, and one draw needn't show every extreme that they name: `seg_ids`: never falling along the tokens; every sequence has one token or more, and one has exactly 4096.
All inputs are finite; a program needn't handle non-finite values.
Results may differ from a plain program's by a relative error of at most 0.0003.
Values sent between devices are 32-bit elements; how exact they have to be, the bound alone decides.
No kernel may reach another device: no remote copies, remote signals or barrier semaphores. Data moves between devices by JAX's collectives and lax.ppermute only.
A program may use at most 128 MiB of HBM per device.

v0:
```python
import jax
import jax.numpy as jnp
from jax import lax
from jax.sharding import PartitionSpec as P

SEQS = 8


def sequence_sums(projected, seg_rows, seq_count, rank_size):
    proj_x = projected[:, :rank_size]
    proj_g = projected[:, rank_size:]
    onehot = (seg_rows[:, None] == jnp.arange(seq_count, dtype=jnp.int32)[None, :]).astype(
        jnp.float32
    )
    weighted = (onehot[:, :, None] * proj_g[:, None, :]).reshape(
        projected.shape[0], seq_count * rank_size
    )
    totals = jnp.dot(
        weighted.T, proj_x, precision=lax.Precision.HIGHEST, preferred_element_type=jnp.float32
    )
    return totals.reshape(seq_count, rank_size * rank_size)


def shards(activations, out_grads, proj_in, proj_out, seg_ids, queries):
    rank_size = proj_in.shape[1]
    seq_count = SEQS
    onehot_all = (seg_ids[:, None] == jnp.arange(seq_count, dtype=jnp.int32)[None, :]).astype(
        jnp.float32
    )
    counts = jnp.sum(onehot_all, axis=0)
    side_x = jnp.dot(activations, proj_in, preferred_element_type=jnp.float32)
    side_g = jnp.dot(out_grads, proj_out, preferred_element_type=jnp.float32)
    partial_terms = jnp.concatenate([side_x, side_g], axis=1)
    summed = lax.psum(partial_terms, "tp")
    seq_grads = sequence_sums(summed, seg_ids, seq_count, rank_size)
    seq_grads = seq_grads / counts[:, None]
    return jnp.dot(
        seq_grads, queries.T, precision=lax.Precision.HIGHEST, preferred_element_type=jnp.float32
    )


def solution(mesh):
    placed = (P("grp", "tp"), P("grp", "tp"), P("tp", None), P("tp", None), P("grp"), P("tp", None))
    return jax.shard_map(
        shards, mesh=mesh, in_specs=placed, out_specs=P("grp", "tp"), check_vma=False
    )
```

profile of v0, /device:TPU:0, one launch (start us, length us, event | category | flops | bytes accessed | tf_op | source)
XLA Modules:
  0.0 177.0 jit_solution(17927276641077331849)
XLA Ops:
  6.5 0.0 copy-start
  6.5 0.0 copy-start.2
  6.5 0.0 all-reduce.2.cloned.1.call-start
  6.5 6.1 %fusion.7 = f32[8192,64]{0,1:T(8,128)S(1)} fusion(bf16[8192,512]{1,0:T(8,128)(2,1)} %param.6, bf16[512,64]{0,1:T(8,128)(2,1)} %param.8), kind=kOutput, calls=%fused_computation.10 | convolution fusion | flops 536870912 | bytes 10551296 | tf_op jit(solution)/shard_map/dot_general | solution.py:31
  12.6 0.0 copy-done.2
  12.7 14.2 %fusion.8 = f32[8192,64]{0,1:T(8,128)S(1)} fusion(bf16[8192,1792]{1,0:T(8,128)(2,1)} %param.7, bf16[1792,64]{0,1:T(8,128)(2,1)S(1)} %copy-done.2), kind=kOutput, calls=%fused_computation.11 | convolution fusion | flops 1879048192 | bytes 31686656 | tf_op jit(solution)/shard_map/dot_general | solution.py:32
  26.9 2.2 %pad_maximum_fusion = f32[8192,128]{0,1:T(8,128)} fusion(f32[8192,64]{0,1:T(8,128)S(1)} %fusion.8, f32[8192,64]{0,1:T(8,128)S(1)} %fusion.7), kind=kLoop, calls=%fused_computation.1 | loop fusion | flops 1048576 | bytes 8388608 | tf_op jit(solution)/shard_map/concatenate | solution.py:33
  29.1 0.0 copy-start.3
  29.1 0.0 all-reduce.2.cloned.1.call-update
  29.1 0.7 copy-done.3
  29.8 0.2 fusion.5
  30.1 113.3 %all-reduce.2.cloned.1.call-done = f32[8192,128]{0,1:T(8,128)} async-done(((f32[8192,128]{0,1:T(8,128)}), f32[8192,128]{0,1:T(8,128)}) %all-reduce.2.cloned.1.call-update) | async-done | bytes 4194320 | tf_op jit(solution)/shard_map/psum | solution.py:34
  143.3 0.0 slice-start
  143.3 1.6 slice-done
  144.9 0.0 copy-start.1
  144.9 7.7 %broadcast_multiply_fusion = f32[8192,8,64]{0,2,1:T(8,128)} fusion(f32[8192,64]{0,1:T(8,128)S(1)} %slice-done, f32[8192,8]{0,1:T(8,128)S(1)} %fusion.2), kind=kLoop, calls=%fused_computation | loop fusion | flops 4194304 | bytes 19136512 | tf_op jit(solution)/shard_map/mul | solution.py:15
  152.7 0.0 copy-done.1
  152.7 15.8 %fusion = f32[512,64]{1,0:T(8,128)S(1)} fusion(f32[8192,512]{0,1:T(8,128)} %bitcast.7, f32[8192,128]{0,1:T(8,128)S(1)} %copy-done.1), kind=kOutput, calls=%fused_computation.2 | convolution fusion | flops 3221225472 | bytes 19005440 | tf_op jit(solution)/shard_map/dot_general | solution.py:18
  168.5 0.1 reshape.31
  168.6 0.0 copy-done
  168.6 1.6 fusion.3
  (1 shorter events, 0.0 us)
Async XLA Ops:
  6.5 162.1 %copy-start = (f32[64,4096]{1,0:T(8,128)S(1)}, f32[64,4096]{1,0:T(8,128)}, u32[]{:S(2)}) copy-start(f32[64,4096]{1,0:T(8,128)} %param.11) | copy-start | bytes 3145732
  6.5 6.1 %copy-start.2 = (bf16[1792,64]{0,1:T(8,128)(2,1)S(1)}, bf16[1792,64]{0,1:T(8,128)(2,1)}, u32[]{:S(2)}) copy-start(bf16[1792,64]{0,1:T(8,128)(2,1)} %param.9) | copy-start | bytes 688132
  6.5 136.8 %all-reduce.2.cloned.1.call-start = ((), (), s32[]{:S(2)}) async-start(), calls=%async_computation | async-start | bytes 8388608 | tf_op jit(solution)/shard_map/psum | solution.py:34
  29.1 0.8 copy-start.3
  143.3 1.6 slice-start
  144.9 7.8 %copy-start.1 = (f32[8192,128]{0,1:T(8,128)S(1)}, f32[8192,128]{0,1:T(8,128)}, u32[]{:S(2)}) copy-start(f32[8192,128]{0,1:T(8,128)} %all-reduce.2.cloned.1.call-done) | copy-start | bytes 12582916
Sparse Core Ops, SparseCore 0:
  29.2 114.0 all-reduce.1
where the time goes:
time: 177 us
  waiting for transfers between devices  113 us (64%)
  matrix products  37.7 us (21%)
  between operations  13.4 us (8%)
  other arithmetic  10.2 us (6%)
  local copies, waits for them, and re-layouts  2.45 us (1%)
    psum x1, waiting for transfers between devices, shards(): summed = lax.psum(partial_terms, 'tp')  113 us
    dot_general x1, matrix products, sequence_sums(): jnp.dot(weighted.T, proj_x, precision=lax.Precision.HIGHEST, preferred_el...  15.8 us
    dot_general x1, matrix products, shards(): side_g = jnp.dot(out_grads, proj_out, preferred_element_type=jnp.float32)  14.2 us
    mul x1, other arithmetic, sequence_sums(): onehot[:, :, None] * proj_g[:, None, :]  7.75 us
    dot_general x1, matrix products, shards(): side_x = jnp.dot(activations, proj_in, preferred_element_type=jnp.float32)  6.1 us
  transfers between devices with their start and end apart: 1, of which 1 were waited for; matrix products, arithmetic and copies ran while one was open for 0% of the time, Pallas kernels for 0%

commit v1 on v0

v1 whole, which is shorter than its diff:
```python
import functools

import jax
import jax.numpy as jnp
from jax import lax
from jax.experimental import pallas as pl
from jax.experimental.pallas import tpu as pltpu
from jax.sharding import PartitionSpec as P

SEQS = 8
CHUNKS = 4
STEPS = 4


def project_kernel(low_bits, me_ref, a_ref, g_ref, pi_ref, po_ref, send_ref, keep_ref):
    step = pl.program_id(0)
    count = 1 << low_bits
    low = me_ref[0] & (count - 1)
    rows = a_ref.shape[0] // count
    side_x = jnp.dot(a_ref[...], pi_ref[...], preferred_element_type=jnp.float32)
    side_g = jnp.dot(g_ref[...], po_ref[...], preferred_element_type=jnp.float32)
    both = jnp.concatenate([side_x, side_g], axis=1)

    def store(out_ref):
        for part in range(count):
            start = pl.multiple_of((part ^ low) * rows, rows)
            out_ref[pl.ds(start, rows), :] = both[part * rows : (part + 1) * rows]

    @pl.when(step < STEPS // 2)
    def _():
        store(send_ref)

    @pl.when(step >= STEPS // 2)
    def _():
        store(keep_ref)


def project(chunk, bits, me_rev, activations, out_grads, proj_in, proj_out):
    tokens, width = activations.shape
    hidden = out_grads.shape[1]
    rank = proj_in.shape[1]
    rows = tokens // CHUNKS // STEPS
    low_bits = bits - 2
    half = STEPS // 2

    def source(j, me):
        return (chunk * STEPS + (((j + half) % STEPS) ^ (me[0] >> low_bits)), 0)

    out = jax.ShapeDtypeStruct((tokens // CHUNKS // 2, 2 * rank), jnp.float32)
    return pl.pallas_call(
        functools.partial(project_kernel, low_bits),
        grid_spec=pltpu.PrefetchScalarGridSpec(
            num_scalar_prefetch=1,
            grid=(STEPS,),
            in_specs=[
                pl.BlockSpec((rows, width), source),
                pl.BlockSpec((rows, hidden), source),
                pl.BlockSpec((width, rank), lambda j, me: (0, 0)),
                pl.BlockSpec((hidden, rank), lambda j, me: (0, 0)),
            ],
            out_specs=[
                pl.BlockSpec((rows, 2 * rank), lambda j, me: (jnp.minimum(j, half - 1), 0)),
                pl.BlockSpec((rows, 2 * rank), lambda j, me: (jnp.maximum(j - half, 0), 0)),
            ],
        ),
        out_shape=[out, out],
        compiler_params=pltpu.CompilerParams(vmem_limit_bytes=32 * 1024 * 1024),
        cost_estimate=pl.CostEstimate(
            flops=2 * rows * STEPS * (width + hidden) * rank,
            bytes_accessed=2 * rows * STEPS * (width + hidden),
            transcendentals=0,
        ),
        name="project",
    )(me_rev, activations, out_grads, proj_in, proj_out)


def product_kernel(seq_count, terms_ref, seg_ref, scale_ref, out_ref):
    terms = terms_ref[...]
    rank = terms.shape[1] // 2
    proj_x = terms[:, :rank]
    proj_g = terms[:, rank:]
    seg = seg_ref[...]
    x_hi = proj_x.astype(jnp.bfloat16)
    x_lo = (proj_x - x_hi.astype(jnp.float32)).astype(jnp.bfloat16)
    g_hi = proj_g.astype(jnp.bfloat16)
    g_lo = (proj_g - g_hi.astype(jnp.float32)).astype(jnp.bfloat16)
    x_both = jnp.concatenate([x_hi, x_lo], axis=1)
    g_both = jnp.concatenate([g_hi, g_lo], axis=1)
    half = rank // 2
    for s in range(seq_count):
        masked = jnp.where(seg == s, g_both, jnp.zeros_like(g_both))
        quad = lax.dot_general(
            masked, x_both, (((0,), (0,)), ((), ())), preferred_element_type=jnp.float32
        )
        total = (
            quad[:rank, :rank] + quad[rank:, :rank] + (quad[:rank, rank:] + quad[rank:, rank:])
        ) * scale_ref[s]
        out_ref[s * rank : (s + 1) * rank, :] = total


def product(terms, seg_rows, scale, seq_count):
    rows, width = terms.shape
    rank = width // 2
    return pl.pallas_call(
        functools.partial(product_kernel, seq_count),
        in_specs=[
            pl.BlockSpec(memory_space=pltpu.VMEM),
            pl.BlockSpec(memory_space=pltpu.VMEM),
            pl.BlockSpec(memory_space=pltpu.SMEM),
        ],
        out_specs=pl.BlockSpec(memory_space=pltpu.VMEM),
        out_shape=jax.ShapeDtypeStruct((seq_count * rank, rank), jnp.float32),
        compiler_params=pltpu.CompilerParams(vmem_limit_bytes=32 * 1024 * 1024),
        name="product",
    )(terms, seg_rows, scale)


def shards(devices, activations, out_grads, proj_in, proj_out, seg_ids, queries):
    bits = devices.bit_length() - 1
    tokens = activations.shape[0]
    rank = proj_in.shape[1]
    me = lax.axis_index("tp")
    me_rev = jnp.int32(0)
    for b in range(bits):
        me_rev = me_rev | (((me >> b) & 1) << (bits - 1 - b))

    def swap(value, bit):
        return lax.ppermute(value, "tp", [(i, i ^ (1 << bit)) for i in range(devices)])

    counts = jnp.sum(
        (seg_ids[None, :] == jnp.arange(SEQS, dtype=jnp.int32)[:, None]).astype(jnp.float32), axis=1
    )
    scale = 1.0 / counts
    own = tokens // CHUNKS // devices
    seg_own = lax.dynamic_slice_in_dim(
        seg_ids.reshape(CHUNKS, devices, own), me_rev, 1, axis=1
    ).reshape(CHUNKS * own)
    seg_rows = jnp.broadcast_to(seg_own[:, None], (CHUNKS * own, 2 * rank))

    done = []
    for chunk in range(CHUNKS):
        send, keep = project(
            chunk, bits, me_rev.reshape(1), activations, out_grads, proj_in, proj_out
        )
        for b in range(bits):
            received = swap(send, b)
            half = keep.shape[0] // 2
            if b < bits - 1:
                send = keep[half:] + received[half:]
                keep = keep[:half] + received[:half]
            else:
                keep = keep + received
        done.append(keep)
    terms = jnp.concatenate(done, axis=0)
    grads = product(terms, seg_rows, scale, SEQS).reshape(SEQS, rank * rank)
    for b in range(bits):
        grads = grads + swap(grads, b)
    return jnp.dot(
        grads, queries.T, precision=lax.Precision.HIGHEST, preferred_element_type=jnp.float32
    )


def solution(mesh):
    placed = (P("grp", "tp"), P("grp", "tp"), P("tp", None), P("tp", None), P("grp"), P("tp", None))
    return jax.shard_map(
        functools.partial(shards, mesh.shape["tp"]),
        mesh=mesh,
        in_specs=placed,
        out_specs=P("grp", "tp"),
        check_vma=False,
    )
```

time: 177 us -> 100 us (0.56)
  waiting for transfers between devices: 113 us -> 36 us
  matrix products: 37.7 us -> 1.52 us
  Pallas kernels: 0 us -> 27.2 us
  starting transfers between devices: 0.01 us -> 24.3 us
  between operations: 13.4 us -> 0.17 us
  other arithmetic: 10.2 us -> 3.93 us
  local copies, waits for them, and re-layouts: 2.45 us -> 6.68 us
    psum x1 -> x0, waiting for transfers between devices: 113 us -> none  [shards(): summed = lax.psum(partial_terms, 'tp')]
    dot_general x4 -> x1, matrix products: 37.7 us -> 1.52 us  [shards(): jnp.dot(grads, queries.T, precision=lax.Precision.HIGHEST, preferred_elem...]
    ppermute x0 -> x20, waiting for transfers between devices: none -> 36 us  [swap(): lax.ppermute(value, 'tp', [(i, i ^ 1 << bit) for i in range(devices)])]
    pallas_call x0 -> x5, Pallas kernels: none -> 27.2 us  [the longest x4 26 us: project(): pl.pallas_call(functools.partial(project_kernel, low_bits), grid_spec=plt...]
    ppermute x0 -> x20, starting transfers between devices: none -> 24.3 us  [swap(): lax.ppermute(value, 'tp', [(i, i ^ 1 << bit) for i in range(devices)])]
    mul x1 -> x0, other arithmetic: 7.75 us -> none  [sequence_sums(): onehot[:, :, None] * proj_g[:, None, :]]
    unnamed x8 -> x10, local copies, waits for them, and re-layouts: 0.74 us -> 6.43 us
    add x0 -> x19, other arithmetic: none -> 3.73 us  [the longest x8 3.59 us: shards(): keep = keep[:half] + received[:half]]
  transfers between devices with their start and end apart: 1 -> 20, of which waited for: 1 -> 11; matrix products, arithmetic and copies ran while one was open for 0% -> 4% of each run, Pallas kernels for 0% -> 20%
where the time goes in v1:
time: 100 us; the launch traced here: 99.8 us
  waiting for transfers between devices  36 us (36%)
  Pallas kernels  27.2 us (27%)
  starting transfers between devices  24.3 us (24%)
  local copies, waits for them, and re-layouts  6.68 us (7%)
  other arithmetic  3.93 us (4%)
  matrix products  1.52 us (2%)
    ppermute x20, waiting for transfers between devices, swap(): lax.ppermute(value, 'tp', [(i, i ^ 1 << bit) for i in range(devices)])  36 us
    pallas_call x4, Pallas kernels, project(): pl.pallas_call(functools.partial(project_kernel, low_bits), grid_spec=plt...  26 us
    ppermute x20, starting transfers between devices, swap(): lax.ppermute(value, 'tp', [(i, i ^ 1 << bit) for i in range(devices)])  24.3 us
    unnamed x10, local copies, waits for them, and re-layouts  6.43 us
    add x8, other arithmetic, shards(): keep = keep[:half] + received[:half]  3.59 us
  transfers between devices with their start and end apart: 20, of which 11 were waited for; matrix products, arithmetic and copies ran while one was open for 4% of the time, Pallas kernels for 20%

profile of v1, /device:TPU:0, one launch (start us, length us, event | category | flops | bytes accessed | tf_op | source)
XLA Modules:
  0.0 99.8 jit_solution(915121783437099079)
XLA Ops:
  2.3 3.4 %copy-done.1 = bf16[8192,512]{1,0:T(8,128)(2,1)S(1)} copy-done((bf16[8192,512]{1,0:T(8,128)(2,1)S(1)}, bf16[8192,512]{1,0:T(8,128)(2,1)}, u32[]{:S(2)}) %copy-start.1) | copy-done | bytes 8388632
  5.7 6.5 %project.4 = (f32[1024,128]{1,0:T(8,128)}, f32[1024,128]{1,0:T(8,128)S(1)}) custom-call(s32[1]{0:T(128)} %bitcast.me_ref, bf16[8192,512]{1,0:T(8,128)(2,1)S(1)} %copy-done.1, bf16[8192,1792]{1,0:T(8,128)(2,1)} %g_ref.7, bf16[512,64]{1,0:T(8,128)(2,1)S(1)} %copy.23.pi_ref, bf16[1792,64]{1,0:T(8,128)(2,1)S(1)} %copy.24.po_ref), custom_call_target="tpu_custom_call" | custom-call | flops 603979776 | bytes 9437184 | tf_op jit(solution)/shard_map/project/pallas_call | solution.py:50
  13.4 6.5 %project.5 = (f32[1024,128]{1,0:T(8,128)}, f32[1024,128]{1,0:T(8,128)S(1)}) custom-call(s32[1]{0:T(128)} %bitcast.me_ref, bf16[8192,512]{1,0:T(8,128)(2,1)S(1)} %copy-done.1, bf16[8192,1792]{1,0:T(8,128)(2,1)} %g_ref.7, bf16[512,64]{1,0:T(8,128)(2,1)S(1)} %copy.23.pi_ref, bf16[1792,64]{1,0:T(8,128)(2,1)S(1)} %copy.24.po_ref), custom_call_target="tpu_custom_call" | custom-call | flops 603979776 | bytes 9437184 | tf_op jit(solution)/shard_map/project/pallas_call | solution.py:50
  20.0 6.5 %project.6 = (f32[1024,128]{1,0:T(8,128)}, f32[1024,128]{1,0:T(8,128)S(1)}) custom-call(s32[1]{0:T(128)} %bitcast.me_ref, bf16[8192,512]{1,0:T(8,128)(2,1)S(1)} %copy-done.1, bf16[8192,1792]{1,0:T(8,128)(2,1)} %g_ref.7, bf16[512,64]{1,0:T(8,128)(2,1)S(1)} %copy.23.pi_ref, bf16[1792,64]{1,0:T(8,128)(2,1)S(1)} %copy.24.po_ref), custom_call_target="tpu_custom_call" | custom-call | flops 603979776 | bytes 9437184 | tf_op jit(solution)/shard_map/project/pallas_call | solution.py:50
  26.9 6.5 %project.7 = (f32[1024,128]{1,0:T(8,128)}, f32[1024,128]{1,0:T(8,128)S(1)}) custom-call(s32[1]{0:T(128)} %bitcast.me_ref, bf16[8192,512]{1,0:T(8,128)(2,1)S(1)} %copy-done.1, bf16[8192,1792]{1,0:T(8,128)(2,1)} %g_ref.7, bf16[512,64]{1,0:T(8,128)(2,1)S(1)} %copy.23.pi_ref, bf16[1792,64]{1,0:T(8,128)(2,1)S(1)} %copy.24.po_ref), custom_call_target="tpu_custom_call" | custom-call | flops 603979776 | bytes 9437184 | tf_op jit(solution)/shard_map/project/pallas_call | solution.py:50
  34.9 3.0 %collective-permute-start.1 = (f32[512,128]{1,0:T(8,128)S(1)}, f32[512,128]{1,0:T(8,128)S(1)}, u32[]{:S(2)}, u32[]{:S(2)}) collective-permute-start(f32[512,128]{1,0:T(8,128)S(1)} %get-tuple-element.22), channel_id=1, source_target_pairs={{0,2},{1,3},{2,0},{3,1},{4,6},{5,7},{6,4},{7,5},{8,10},{9,11},{10,... | collective-permute-start | bytes 786440 | tf_op jit(solution)/shard_map/ppermute | solution.py:128
  40.2 2.1 %collective-permute-start.9 = (f32[512,128]{1,0:T(8,128)S(1)}, f32[512,128]{1,0:T(8,128)S(1)}, u32[]{:S(2)}, u32[]{:S(2)}) collective-permute-start(f32[512,128]{1,0:T(8,128)S(1)} %get-tuple-element.26), channel_id=1, source_target_pairs={{0,2},{1,3},{2,0},{3,1},{4,6},{5,7},{6,4},{7,5},{8,10},{9,11},{10,... | collective-permute-start | bytes 786440 | tf_op jit(solution)/shard_map/ppermute | solution.py:128
  42.5 2.6 %collective-permute-done.1 = f32[512,128]{1,0:T(8,128)S(1)} collective-permute-done((f32[512,128]{1,0:T(8,128)S(1)}, f32[512,128]{1,0:T(8,128)S(1)}, u32[]{:S(2)}, u32[]{:S(2)}) %collective-permute-start.1) | collective-permute-done | bytes 262176 | tf_op jit(solution)/shard_map/ppermute | solution.py:128
  45.1 2.2 %collective-permute-start.2 = (f32[256,128]{1,0:T(8,128)S(1)}, f32[256,128]{1,0:T(8,128)S(1)}, u32[]{:S(2)}, u32[]{:S(2)}) collective-permute-start(f32[256,128]{1,0:T(8,128)S(1)} %get-tuple-element.30), channel_id=1, source_target_pairs={{0,4},{1,5},{2,6},{3,7},{4,0},{5,1},{6,2},{7,3},{8,12},{9,13},{10,... | collective-permute-start | bytes 393224 | tf_op jit(solution)/shard_map/ppermute | solution.py:128
  47.3 3.4 %collective-permute-done.5 = f32[512,128]{1,0:T(8,128)S(1)} collective-permute-done((f32[512,128]{1,0:T(8,128)S(1)}, f32[512,128]{1,0:T(8,128)S(1)}, u32[]{:S(2)}, u32[]{:S(2)}) %collective-permute-start.5) | collective-permute-done | bytes 262176 | tf_op jit(solution)/shard_map/ppermute | solution.py:128
  50.7 2.2 %collective-permute-start.6 = (f32[256,128]{1,0:T(8,128)S(1)}, f32[256,128]{1,0:T(8,128)S(1)}, u32[]{:S(2)}, u32[]{:S(2)}) collective-permute-start(f32[256,128]{1,0:T(8,128)S(1)} %get-tuple-element.32), channel_id=1, source_target_pairs={{0,4},{1,5},{2,6},{3,7},{4,0},{5,1},{6,2},{7,3},{8,12},{9,13},{10,... | collective-permute-start | bytes 393224 | tf_op jit(solution)/shard_map/ppermute | solution.py:128
  52.9 3.4 %collective-permute-done.9 = f32[512,128]{1,0:T(8,128)S(1)} collective-permute-done((f32[512,128]{1,0:T(8,128)S(1)}, f32[512,128]{1,0:T(8,128)S(1)}, u32[]{:S(2)}, u32[]{:S(2)}) %collective-permute-start.9) | collective-permute-done | bytes 262176 | tf_op jit(solution)/shard_map/ppermute | solution.py:128
  56.3 2.2 %collective-permute-start.10 = (f32[256,128]{1,0:T(8,128)S(1)}, f32[256,128]{1,0:T(8,128)S(1)}, u32[]{:S(2)}, u32[]{:S(2)}) collective-permute-start(f32[256,128]{1,0:T(8,128)S(1)} %get-tuple-element.34), channel_id=1, source_target_pairs={{0,4},{1,5},{2,6},{3,7},{4,0},{5,1},{6,2},{7,3},{8,12},{9,13},{10,... | collective-permute-start | bytes 393224 | tf_op jit(solution)/shard_map/ppermute | solution.py:128
  58.5 2.8 %collective-permute-done.13 = f32[512,128]{1,0:T(8,128)S(1)} collective-permute-done((f32[512,128]{1,0:T(8,128)S(1)}, f32[512,128]{1,0:T(8,128)S(1)}, u32[]{:S(2)}, u32[]{:S(2)}) %collective-permute-start.13) | collective-permute-done | bytes 262176 | tf_op jit(solution)/shard_map/ppermute | solution.py:128
  61.3 1.9 %collective-permute-start.14 = (f32[256,128]{1,0:T(8,128)S(1)}, f32[256,128]{1,0:T(8,128)S(1)}, u32[]{:S(2)}, u32[]{:S(2)}) collective-permute-start(f32[256,128]{1,0:T(8,128)S(1)} %get-tuple-element.36), channel_id=1, source_target_pairs={{0,4},{1,5},{2,6},{3,7},{4,0},{5,1},{6,2},{7,3},{8,12},{9,13},{10,... | collective-permute-start | bytes 393224 | tf_op jit(solution)/shard_map/ppermute | solution.py:128
  63.2 2.7 %collective-permute-start.3 = (f32[128,128]{1,0:T(8,128)S(1)}, f32[128,128]{1,0:T(8,128)S(1)}, u32[]{:S(2)}, u32[]{:S(2)}) collective-permute-start(f32[128,128]{1,0:T(8,128)S(1)} %slice_add_fusion.22), channel_id=1, source_target_pairs={{0,8},{1,9},{2,10},{3,11},{4,12},{5,13},{6,14},{7,15},{8,0},{9,1},... | collective-permute-start | bytes 196616 | tf_op jit(solution)/shard_map/ppermute | solution.py:128
  66.3 2.7 %collective-permute-start.11 = (f32[128,128]{1,0:T(8,128)S(1)}, f32[128,128]{1,0:T(8,128)S(1)}, u32[]{:S(2)}, u32[]{:S(2)}) collective-permute-start(f32[128,128]{1,0:T(8,128)S(1)} %slice_add_fusion.18), channel_id=1, source_target_pairs={{0,8},{1,9},{2,10},{3,11},{4,12},{5,13},{6,14},{7,15},{8,0},{9,1},... | collective-permute-start | bytes 196616 | tf_op jit(solution)/shard_map/ppermute | solution.py:128
  69.0 1.6 %collective-permute-start.15 = (f32[128,128]{1,0:T(8,128)S(1)}, f32[128,128]{1,0:T(8,128)S(1)}, u32[]{:S(2)}, u32[]{:S(2)}) collective-permute-start(f32[128,128]{1,0:T(8,128)S(1)} %slice_add_fusion.16), channel_id=1, source_target_pairs={{0,8},{1,9},{2,10},{3,11},{4,12},{5,13},{6,14},{7,15},{8,0},{9,1},... | collective-permute-start | bytes 196616 | tf_op jit(solution)/shard_map/ppermute | solution.py:128
  70.6 4.7 %collective-permute-done.7 = f32[128,128]{1,0:T(8,128)S(1)} collective-permute-done((f32[128,128]{1,0:T(8,128)S(1)}, f32[128,128]{1,0:T(8,128)S(1)}, u32[]{:S(2)}, u32[]{:S(2)}) %collective-permute-start.7) | collective-permute-done | bytes 65568 | tf_op jit(solution)/shard_map/ppermute | solution.py:128
  80.5 1.6 %collective-permute-start.17 = (f32[8,4096]{1,0:T(8,128)S(1)}, f32[8,4096]{1,0:T(8,128)S(1)}, u32[]{:S(2)}, u32[]{:S(2)}) collective-permute-start(f32[8,4096]{1,0:T(8,128)S(1)} %add.128), channel_id=1, source_target_pairs={{0,2},{1,3},{2,0},{3,1},{4,6},{5,7},{6,4},{7,5},{8,10},{9,11},{10,... | collective-permute-start | bytes 393224 | tf_op jit(solution)/shard_map/ppermute | solution.py:128
  82.1 4.0 %collective-permute-done.17 = f32[8,4096]{1,0:T(8,128)S(1)} collective-permute-done((f32[8,4096]{1,0:T(8,128)S(1)}, f32[8,4096]{1,0:T(8,128)S(1)}, u32[]{:S(2)}, u32[]{:S(2)}) %collective-permute-start.17) | collective-permute-done | bytes 131104 | tf_op jit(solution)/shard_map/ppermute | solution.py:128
  86.2 5.0 %collective-permute-done.18 = f32[8,4096]{1,0:T(8,128)S(1)} collective-permute-done((f32[8,4096]{1,0:T(8,128)S(1)}, f32[8,4096]{1,0:T(8,128)S(1)}, u32[]{:S(2)}, u32[]{:S(2)}) %collective-permute-start.18) | collective-permute-done | bytes 131104 | tf_op jit(solution)/shard_map/ppermute | solution.py:128
  91.7 6.5 %collective-permute-done.19 = f32[8,4096]{1,0:T(8,128)S(1)} collective-permute-done((f32[8,4096]{1,0:T(8,128)S(1)}, f32[8,4096]{1,0:T(8,128)S(1)}, u32[]{:S(2)}, u32[]{:S(2)}) %collective-permute-start.19) | collective-permute-done | bytes 131104 | tf_op jit(solution)/shard_map/ppermute | solution.py:128
  98.3 1.5 %fusion = f32[8,64]{1,0:T(8,128)} fusion(f32[64,4096]{1,0:T(8,128)S(1)} %copy-done, f32[8,4096]{1,0:T(8,128)S(1)} %add.130, f32[8,4096]{1,0:T(8,128)S(1)} %collective-permute-done.19), kind=kOutput, calls=%fused_computation.19 | convolution fusion | flops 25198592 | bytes 1312768 | tf_op jit(solution)/shard_map/dot_general | solution.py:158
  (57 shorter events, 14.3 us)
Async XLA Ops:
  0.0 98.3 %copy-start = (f32[64,4096]{1,0:T(8,128)S(1)}, f32[64,4096]{1,0:T(8,128)}, u32[]{:S(2)}) copy-start(f32[64,4096]{1,0:T(8,128)} %param.11) | copy-start | bytes 3145732
  2.3 3.4 %copy-start.1 = (bf16[8192,512]{1,0:T(8,128)(2,1)S(1)}, bf16[8192,512]{1,0:T(8,128)(2,1)}, u32[]{:S(2)}) copy-start(bf16[8192,512]{1,0:T(8,128)(2,1)} %a_ref.7) | copy-start | bytes 25165828
  12.2 0.8 copy-start.2
  12.9 20.7 %collective-permute-start = (f32[1024,128]{1,0:T(8,128)}, f32[1024,128]{1,0:T(8,128)}, u32[]{:S(2)}, u32[]{:S(2)}) collective-permute-start(f32[1024,128]{1,0:T(8,128)} %get-tuple-element.14), channel_id=1, source_target_pairs={{0,1},{1,0},{2,3},{3,2},{4,5},{5,4},{6,7},{7,6},{8,9},{9,8},{10,11... | collective-permute-start | bytes 1572872 | tf_op jit(solution)/shard_map/ppermute | solution.py:128
  19.9 13.6 %copy-start.3 = (s32[8192]{0:T(1024)S(1)}, s32[8192]{0:T(1024)}, u32[]{:S(2)}) copy-start(s32[8192]{0:T(1024)} %param.10) | copy-start | bytes 98308
  19.9 18.1 %collective-permute-start.4 = (f32[1024,128]{1,0:T(8,128)}, f32[1024,128]{1,0:T(8,128)}, u32[]{:S(2)}, u32[]{:S(2)}) collective-permute-start(f32[1024,128]{1,0:T(8,128)} %get-tuple-element.16), channel_id=1, source_target_pairs={{0,1},{1,0},{2,3},{3,2},{4,5},{5,4},{6,7},{7,6},{8,9},{9,8},{10,11... | collective-permute-start | bytes 1572872 | tf_op jit(solution)/shard_map/ppermute | solution.py:128
  26.5 12.7 %collective-permute-start.8 = (f32[1024,128]{1,0:T(8,128)}, f32[1024,128]{1,0:T(8,128)}, u32[]{:S(2)}, u32[]{:S(2)}) collective-permute-start(f32[1024,128]{1,0:T(8,128)} %get-tuple-element.18), channel_id=1, source_target_pairs={{0,1},{1,0},{2,3},{3,2},{4,5},{5,4},{6,7},{7,6},{8,9},{9,8},{10,11... | collective-permute-start | bytes 1572872 | tf_op jit(solution)/shard_map/ppermute | solution.py:128
  33.4 8.9 %collective-permute-start.12 = (f32[1024,128]{1,0:T(8,128)}, f32[1024,128]{1,0:T(8,128)S(1)}, u32[]{:S(2)}, u32[]{:S(2)}) collective-permute-start(f32[1024,128]{1,0:T(8,128)} %get-tuple-element.20), channel_id=1, source_target_pairs={{0,1},{1,0},{2,3},{3,2},{4,5},{5,4},{6,7},{7,6},{8,9},{9,8},{10,11... | collective-permute-start | bytes 1572872 | tf_op jit(solution)/shard_map/ppermute | solution.py:128
  34.9 10.1 %collective-permute-start.1 = (f32[512,128]{1,0:T(8,128)S(1)}, f32[512,128]{1,0:T(8,128)S(1)}, u32[]{:S(2)}, u32[]{:S(2)}) collective-permute-start(f32[512,128]{1,0:T(8,128)S(1)} %get-tuple-element.22), channel_id=1, source_target_pairs={{0,2},{1,3},{2,0},{3,1},{4,6},{5,7},{6,4},{7,5},{8,10},{9,11},{10,... | collective-permute-start | bytes 786440 | tf_op jit(solution)/shard_map/ppermute | solution.py:128
  39.1 11.6 %collective-permute-start.5 = (f32[512,128]{1,0:T(8,128)S(1)}, f32[512,128]{1,0:T(8,128)S(1)}, u32[]{:S(2)}, u32[]{:S(2)}) collective-permute-start(f32[512,128]{1,0:T(8,128)S(1)} %get-tuple-element.24), channel_id=1, source_target_pairs={{0,2},{1,3},{2,0},{3,1},{4,6},{5,7},{6,4},{7,5},{8,10},{9,11},{10,... | collective-permute-start | bytes 786440 | tf_op jit(solution)/shard_map/ppermute | solution.py:128
  40.2 16.1 %collective-permute-start.9 = (f32[512,128]{1,0:T(8,128)S(1)}, f32[512,128]{1,0:T(8,128)S(1)}, u32[]{:S(2)}, u32[]{:S(2)}) collective-permute-start(f32[512,128]{1,0:T(8,128)S(1)} %get-tuple-element.26), channel_id=1, source_target_pairs={{0,2},{1,3},{2,0},{3,1},{4,6},{5,7},{6,4},{7,5},{8,10},{9,11},{10,... | collective-permute-start | bytes 786440 | tf_op jit(solution)/shard_map/ppermute | solution.py:128
  42.4 18.9 %collective-permute-start.13 = (f32[512,128]{1,0:T(8,128)S(1)}, f32[512,128]{1,0:T(8,128)S(1)}, u32[]{:S(2)}, u32[]{:S(2)}) collective-permute-start(f32[512,128]{1,0:T(8,128)S(1)} %get-tuple-element.28), channel_id=1, source_target_pairs={{0,2},{1,3},{2,0},{3,1},{4,6},{5,7},{6,4},{7,5},{8,10},{9,11},{10,... | collective-permute-start | bytes 786440 | tf_op jit(solution)/shard_map/ppermute | solution.py:128
  45.1 18.1 %collective-permute-start.2 = (f32[256,128]{1,0:T(8,128)S(1)}, f32[256,128]{1,0:T(8,128)S(1)}, u32[]{:S(2)}, u32[]{:S(2)}) collective-permute-start(f32[256,128]{1,0:T(8,128)S(1)} %get-tuple-element.30), channel_id=1, source_target_pairs={{0,4},{1,5},{2,6},{3,7},{4,0},{5,1},{6,2},{7,3},{8,12},{9,13},{10,... | collective-permute-start | bytes 393224 | tf_op jit(solution)/shard_map/ppermute | solution.py:128
  50.7 15.1 %collective-permute-start.6 = (f32[256,128]{1,0:T(8,128)S(1)}, f32[256,128]{1,0:T(8,128)S(1)}, u32[]{:S(2)}, u32[]{:S(2)}) collective-permute-start(f32[256,128]{1,0:T(8,128)S(1)} %get-tuple-element.32), channel_id=1, source_target_pairs={{0,4},{1,5},{2,6},{3,7},{4,0},{5,1},{6,2},{7,3},{8,12},{9,13},{10,... | collective-permute-start | bytes 393224 | tf_op jit(solution)/shard_map/ppermute | solution.py:128
  56.3 9.9 %collective-permute-start.10 = (f32[256,128]{1,0:T(8,128)S(1)}, f32[256,128]{1,0:T(8,128)S(1)}, u32[]{:S(2)}, u32[]{:S(2)}) collective-permute-start(f32[256,128]{1,0:T(8,128)S(1)} %get-tuple-element.34), channel_id=1, source_target_pairs={{0,4},{1,5},{2,6},{3,7},{4,0},{5,1},{6,2},{7,3},{8,12},{9,13},{10,... | collective-permute-start | bytes 393224 | tf_op jit(solution)/shard_map/ppermute | solution.py:128
  61.3 7.6 %collective-permute-start.14 = (f32[256,128]{1,0:T(8,128)S(1)}, f32[256,128]{1,0:T(8,128)S(1)}, u32[]{:S(2)}, u32[]{:S(2)}) collective-permute-start(f32[256,128]{1,0:T(8,128)S(1)} %get-tuple-element.36), channel_id=1, source_target_pairs={{0,4},{1,5},{2,6},{3,7},{4,0},{5,1},{6,2},{7,3},{8,12},{9,13},{10,... | collective-permute-start | bytes 393224 | tf_op jit(solution)/shard_map/ppermute | solution.py:128
  63.2 7.4 %collective-permute-start.3 = (f32[128,128]{1,0:T(8,128)S(1)}, f32[128,128]{1,0:T(8,128)S(1)}, u32[]{:S(2)}, u32[]{:S(2)}) collective-permute-start(f32[128,128]{1,0:T(8,128)S(1)} %slice_add_fusion.22), channel_id=1, source_target_pairs={{0,8},{1,9},{2,10},{3,11},{4,12},{5,13},{6,14},{7,15},{8,0},{9,1},... | collective-permute-start | bytes 196616 | tf_op jit(solution)/shard_map/ppermute | solution.py:128
  65.9 9.4 %collective-permute-start.7 = (f32[128,128]{1,0:T(8,128)S(1)}, f32[128,128]{1,0:T(8,128)S(1)}, u32[]{:S(2)}, u32[]{:S(2)}) collective-permute-start(f32[128,128]{1,0:T(8,128)S(1)} %slice_add_fusion.20), channel_id=1, source_target_pairs={{0,8},{1,9},{2,10},{3,11},{4,12},{5,13},{6,14},{7,15},{8,0},{9,1},... | collective-permute-start | bytes 196616 | tf_op jit(solution)/shard_map/ppermute | solution.py:128
  66.3 10.4 %collective-permute-start.11 = (f32[128,128]{1,0:T(8,128)S(1)}, f32[128,128]{1,0:T(8,128)S(1)}, u32[]{:S(2)}, u32[]{:S(2)}) collective-permute-start(f32[128,128]{1,0:T(8,128)S(1)} %slice_add_fusion.18), channel_id=1, source_target_pairs={{0,8},{1,9},{2,10},{3,11},{4,12},{5,13},{6,14},{7,15},{8,0},{9,1},... | collective-permute-start | bytes 196616 | tf_op jit(solution)/shard_map/ppermute | solution.py:128
  69.0 8.6 %collective-permute-start.15 = (f32[128,128]{1,0:T(8,128)S(1)}, f32[128,128]{1,0:T(8,128)S(1)}, u32[]{:S(2)}, u32[]{:S(2)}) collective-permute-start(f32[128,128]{1,0:T(8,128)S(1)} %slice_add_fusion.16), channel_id=1, source_target_pairs={{0,8},{1,9},{2,10},{3,11},{4,12},{5,13},{6,14},{7,15},{8,0},{9,1},... | collective-permute-start | bytes 196616 | tf_op jit(solution)/shard_map/ppermute | solution.py:128
  79.1 1.4 %collective-permute-start.16 = (f32[8,4096]{1,0:T(8,128)S(1)}, f32[8,4096]{1,0:T(8,128)S(1)}, u32[]{:S(2)}, u32[]{:S(2)}) collective-permute-start(f32[8,4096]{1,0:T(8,128)S(1)} %reshape.16), channel_id=1, source_target_pairs={{0,1},{1,0},{2,3},{3,2},{4,5},{5,4},{6,7},{7,6},{8,9},{9,8},{10,11... | collective-permute-start | bytes 393224 | tf_op jit(solution)/shard_map/ppermute | solution.py:128
  80.5 5.6 %collective-permute-start.17 = (f32[8,4096]{1,0:T(8,128)S(1)}, f32[8,4096]{1,0:T(8,128)S(1)}, u32[]{:S(2)}, u32[]{:S(2)}) collective-permute-start(f32[8,4096]{1,0:T(8,128)S(1)} %add.128), channel_id=1, source_target_pairs={{0,2},{1,3},{2,0},{3,1},{4,6},{5,7},{6,4},{7,5},{8,10},{9,11},{10,... | collective-permute-start | bytes 393224 | tf_op jit(solution)/shard_map/ppermute | solution.py:128
  86.1 5.0 %collective-permute-start.18 = (f32[8,4096]{1,0:T(8,128)S(1)}, f32[8,4096]{1,0:T(8,128)S(1)}, u32[]{:S(2)}, u32[]{:S(2)}) collective-permute-start(f32[8,4096]{1,0:T(8,128)S(1)} %add.129), channel_id=1, source_target_pairs={{0,4},{1,5},{2,6},{3,7},{4,0},{5,1},{6,2},{7,3},{8,12},{9,13},{10,... | collective-permute-start | bytes 393224 | tf_op jit(solution)/shard_map/ppermute | solution.py:128
  91.2 7.1 %collective-permute-start.19 = (f32[8,4096]{1,0:T(8,128)S(1)}, f32[8,4096]{1,0:T(8,128)S(1)}, u32[]{:S(2)}, u32[]{:S(2)}) collective-permute-start(f32[8,4096]{1,0:T(8,128)S(1)} %add.130), channel_id=1, source_target_pairs={{0,8},{1,9},{2,10},{3,11},{4,12},{5,13},{6,14},{7,15},{8,0},{9,1},... | collective-permute-start | bytes 393224 | tf_op jit(solution)/shard_map/ppermute | solution.py:128

commit v2 on v0

v2 whole, which is shorter than its diff:
```python
import functools

import jax
import jax.numpy as jnp
from jax import lax
from jax.experimental import pallas as pl
from jax.experimental.pallas import tpu as pltpu
from jax.sharding import PartitionSpec as P

SEQS = 8
UNITS = 16
CHUNKS = (2, 4, 4, 4, 2)
BOTH_SIDES = 1
BLOCK = 256
VMEM = 56 * 1024 * 1024
ROWS_BY_ROWS = (((1,), (1,)), ((), ()))


def project_kernel(first, rows, blocks, low_bits, me_ref, a_hbm, g_hbm, pi_ref, po_ref, send_ref, keep_ref, a_buf, g_buf, sems):
    size = rows // blocks
    count = 1 << low_bits
    part_rows = size // count
    high = me_ref[0] >> low_bits
    low = me_ref[0] & (count - 1)
    half = blocks // 2
    order = list(range(half, blocks)) + list(range(half))

    def copies(slot):
        start = pl.multiple_of(first + (order[slot] ^ high) * size, 16)
        held = pl.ds(slot * size, size)
        return (
            pltpu.make_async_copy(a_hbm.at[pl.ds(start, size), :], a_buf.at[held, :], sems.at[slot, 0]),
            pltpu.make_async_copy(g_hbm.at[pl.ds(start, size), :], g_buf.at[held, :], sems.at[slot, 1]),
        )

    for slot in range(blocks):
        for copy in copies(slot):
            copy.start()
    for slot in range(blocks):
        for copy in copies(slot):
            copy.wait()
        held = slice(slot * size, (slot + 1) * size)
        side_x = lax.dot_general(a_buf[held, :], pi_ref[...], ROWS_BY_ROWS, preferred_element_type=jnp.float32)
        side_g = lax.dot_general(g_buf[held, :], po_ref[...], ROWS_BY_ROWS, preferred_element_type=jnp.float32)
        both = jnp.concatenate([side_x, side_g], axis=1)
        out_ref = send_ref if slot < half else keep_ref
        base = (slot % half) * size
        for part in range(count):
            start = pl.multiple_of(base + (part ^ low) * part_rows, 8)
            out_ref[pl.ds(start, part_rows), :] = both[part * part_rows : (part + 1) * part_rows]


def project(first, rows, bits, me_rev, activations, out_grads, proj_in, proj_out):
    width = activations.shape[1]
    hidden = out_grads.shape[1]
    rank = proj_in.shape[0]
    block_bits = max(1, (-(-rows // BLOCK) - 1).bit_length())
    blocks = 1 << block_bits
    out = jax.ShapeDtypeStruct((rows // 2, 2 * rank), jnp.float32)
    vmem = pl.BlockSpec(memory_space=pltpu.VMEM)
    return pl.pallas_call(
        functools.partial(project_kernel, first, rows, blocks, bits - block_bits),
        in_specs=[
            pl.BlockSpec(memory_space=pltpu.SMEM),
            pl.BlockSpec(memory_space=pl.ANY),
            pl.BlockSpec(memory_space=pl.ANY),
            vmem,
            vmem,
        ],
        out_specs=[vmem, vmem],
        out_shape=[out, out],
        scratch_shapes=[
            pltpu.VMEM((rows, width), activations.dtype),
            pltpu.VMEM((rows, hidden), out_grads.dtype),
            pltpu.SemaphoreType.DMA((blocks, 2)),
        ],
        compiler_params=pltpu.CompilerParams(vmem_limit_bytes=VMEM),
        cost_estimate=pl.CostEstimate(
            flops=2 * rows * (width + hidden) * rank,
            bytes_accessed=2 * rows * (width + hidden),
            transcendentals=0,
        ),
        name="project",
    )(me_rev, activations, out_grads, proj_in, proj_out)


def product_kernel(pieces, bits, me_ref, edge_ref, scale_ref, *refs):
    term_refs = refs[: len(pieces)]
    send_ref, keep_ref, held_ref = refs[len(pieces) :]
    terms = jnp.concatenate([ref[...] for ref in term_refs], axis=0)
    total_rows = terms.shape[0]
    rank = terms.shape[1] // 2
    me = me_ref[0]
    lane = lax.broadcasted_iota(jnp.int32, (1, total_rows), 1)
    token = lane
    offset = 0
    for first, rows, count in pieces:
        for part in range(count):
            start = first + (me ^ part) * rows
            token = jnp.where(lane >= offset, lane + (start - offset), token)
            offset += rows
    proj_x = terms[:, :rank]
    x_hi = proj_x.astype(jnp.bfloat16)
    x_lo = (proj_x - x_hi.astype(jnp.float32)).astype(jnp.bfloat16)
    x_both = jnp.concatenate([x_hi, x_lo], axis=1)
    g_rows = terms.T[rank:, :]
    half = rank // 2
    side = me >> (bits - 1)
    group = SEQS // 2
    for place in range(SEQS):
        s = place ^ (side * group)
        inside = (token >= edge_ref[s]) & (token < edge_ref[s + 1])
        masked = jnp.where(inside, g_rows, 0.0)
        g_hi = masked.astype(jnp.bfloat16)
        g_lo = (masked - g_hi.astype(jnp.float32)).astype(jnp.bfloat16)
        quad = jnp.dot(jnp.concatenate([g_hi, g_lo], axis=0), x_both, preferred_element_type=jnp.float32)
        small = quad[rank:, rank:] + (quad[rank:, :rank] + quad[:rank, rank:])
        total = (quad[:rank, :rank] + small) * scale_ref[s]
        held_ref[place, :, :rank] = total
        even = held_ref[place, pl.ds(0, half, stride=2), :]
        odd = held_ref[place, pl.ds(1, half, stride=2), :]
        out_ref = keep_ref if place < group else send_ref
        row = (place % group) * half
        out_ref[row : row + half, :] = jnp.concatenate([even[:, :rank], odd[:, :rank]], axis=1)


def product(pieces, bits, me_rev, edges, scale, terms):
    rank = terms[0].shape[1] // 2
    out = jax.ShapeDtypeStruct((SEQS // 2 * rank // 2, 2 * rank), jnp.float32)
    vmem = pl.BlockSpec(memory_space=pltpu.VMEM)
    smem = pl.BlockSpec(memory_space=pltpu.SMEM)
    return pl.pallas_call(
        functools.partial(product_kernel, pieces, bits),
        in_specs=[smem, smem, smem] + [vmem] * len(terms),
        out_specs=[vmem, vmem],
        out_shape=[out, out],
        scratch_shapes=[pltpu.VMEM((SEQS, rank, 2 * rank), jnp.float32)],
        compiler_params=pltpu.CompilerParams(vmem_limit_bytes=VMEM),
        name="product",
    )(me_rev, edges, scale, *terms)


def score_kernel(side_ref, mine_ref, other_ref, q_ref, out_ref):
    queries, depth = q_ref.shape
    lanes = mine_ref.shape[1]
    columns = depth // lanes
    group = SEQS // 2
    step = 16
    rows = [[] for _ in range(SEQS)]
    for start in range(0, queries, step):
        sums = [jnp.zeros((step, lanes), jnp.float32) for _ in range(SEQS)]
        for column in range(columns):
            block = q_ref[start : start + step, column * lanes : (column + 1) * lanes]
            for s in range(SEQS):
                ref = mine_ref if s < group else other_ref
                row = (s % group) * columns + column
                sums[s] = sums[s] + block * ref[row : row + 1, :]
        for s in range(SEQS):
            rows[s].append(sums[s])
    lines = [jnp.sum(jnp.concatenate(parts, axis=0).T, axis=0, keepdims=True) for parts in rows]
    plain = jnp.concatenate(lines, axis=0)
    turned = jnp.concatenate(lines[group:] + lines[:group], axis=0)
    out_ref[...] = jnp.where(side_ref[0] == 0, plain, turned)


def score(side, mine, other, queries):
    vmem = pl.BlockSpec(memory_space=pltpu.VMEM)
    return pl.pallas_call(
        score_kernel,
        in_specs=[pl.BlockSpec(memory_space=pltpu.SMEM), vmem, vmem, vmem],
        out_specs=vmem,
        out_shape=jax.ShapeDtypeStruct((SEQS, queries.shape[0]), jnp.float32),
        compiler_params=pltpu.CompilerParams(vmem_limit_bytes=VMEM),
        name="score",
    )(side, mine, other, queries)


def shards(devices, activations, out_grads, proj_in, proj_out, seg_ids, queries):
    bits = devices.bit_length() - 1
    last = bits - 1
    tokens = activations.shape[0]
    unit = tokens // UNITS
    me = lax.axis_index("tp").astype(jnp.int32)
    me_rev = jnp.int32(0)
    for b in range(bits):
        me_rev = me_rev | (((me >> b) & 1) << (bits - 1 - b))
    me_rev = me_rev.reshape(1)
    weights_in, weights_out = proj_in.T, proj_out.T

    def swap(value, bit):
        return lax.ppermute(value, "tp", [(i, i ^ (1 << bit)) for i in range(devices)])

    edges = jnp.sum(
        (seg_ids[None, :] < jnp.arange(SEQS + 1, dtype=jnp.int32)[:, None]).astype(jnp.int32), axis=1
    )
    scale = 1.0 / (edges[1:] - edges[:-1]).astype(jnp.float32)

    tie = me_rev
    sums = []
    early, late = [], []
    for k, share in enumerate(CHUNKS):
        rows = share * unit
        first = sum(CHUNKS[:k]) * unit
        if k > 0:
            tie, _ = lax.optimization_barrier((me_rev, sums[max(0, k - 1 if k < 3 else k - 2)]))
        send, keep = project(first, rows, bits, tie, activations, out_grads, weights_in, weights_out)
        on_both = k >= len(CHUNKS) - BOTH_SIDES
        for b in range(bits):
            if b == last and on_both:
                half = keep.shape[0] // 2
                whole = jnp.concatenate([keep, send], axis=0)
                turned = swap(jnp.concatenate([send, keep], axis=0), b)
                keep = whole + turned
            else:
                received = swap(send, b)
                if b < last:
                    half = keep.shape[0] // 2
                    send = keep[half:] + received[half:]
                    keep = keep[:half] + received[:half]
                else:
                    keep = keep + received
            if b == 0:
                sums.append(send)
        (late if on_both else early).append((keep, (first, rows // devices, 2 if on_both else 1)))

    def group_product(group):
        return product(tuple(p for _, p in group), bits, me_rev, edges, scale, [t for t, _ in group])

    send, keep = group_product(early)
    grads = keep + swap(send, 0)
    grads = grads + swap(grads, last)
    send, keep = group_product(late)
    grads = grads + keep + swap(send, 0)
    for b in range(1, last):
        grads = grads + swap(grads, b)
    return score(me_rev >> last, grads, swap(grads, 0), queries)


def solution(mesh):
    placed = (P("grp", "tp"), P("grp", "tp"), P("tp", None), P("tp", None), P("grp"), P("tp", None))
    return jax.shard_map(
        functools.partial(shards, mesh.shape["tp"]),
        mesh=mesh,
        in_specs=placed,
        out_specs=P("grp", "tp"),
        check_vma=False,
    )
```

time: 177 us -> 118 us (0.67)
  waiting for transfers between devices: 113 us -> 32.8 us
  Pallas kernels: 0 us -> 48.9 us
  matrix products: 37.7 us -> 0 us
  starting transfers between devices: 0.01 us -> 24.7 us
  between operations: 13.4 us -> 0.25 us
  local copies, waits for them, and re-layouts: 2.45 us -> 0.65 us
    psum x1 -> x0, waiting for transfers between devices: 113 us -> none  [shards(): summed = lax.psum(partial_terms, 'tp')]
    pallas_call x0 -> x8, Pallas kernels: none -> 48.9 us  [the longest x5 41.6 us: project(): pl.pallas_call(functools.partial(project_kernel, first, rows, blocks, bit...]
    dot_general x4 -> x0, matrix products: 37.7 us -> none  [the longest x1 15.8 us: sequence_sums(): jnp.dot(weighted.T, proj_x, precision=lax.Precision.HIGHEST, preferred_el...]
    ppermute x0 -> x26, waiting for transfers between devices: none -> 32.8 us  [swap(): lax.ppermute(value, 'tp', [(i, i ^ 1 << bit) for i in range(devices)])]
    ppermute x0 -> x26, starting transfers between devices: none -> 24.7 us  [swap(): lax.ppermute(value, 'tp', [(i, i ^ 1 << bit) for i in range(devices)])]
    add x0 -> x24, other arithmetic: none -> 9.34 us  [the longest x10 4.42 us: shards(): keep = keep[:half] + received[:half]]
    mul x1 -> x0, other arithmetic: 7.75 us -> none  [sequence_sums(): onehot[:, :, None] * proj_g[:, None, :]]
    concatenate x1, other arithmetic: 2.23 us -> 0.01 us  [shards(): turned = swap(jnp.concatenate([send, keep], axis=0), b)]
  transfers between devices with their start and end apart: 1 -> 26, of which waited for: 1 -> 16; matrix products, arithmetic and copies ran while one was open for 0% -> 7% of each run, Pallas kernels for 0% -> 26%
where the time goes in v2:
time: 118 us; the launch traced here: 117 us
  Pallas kernels  48.9 us (41%)
  waiting for transfers between devices  32.8 us (28%)
  starting transfers between devices  24.7 us (21%)
  other arithmetic  10.1 us (9%)
    pallas_call x5, Pallas kernels, project(): pl.pallas_call(functools.partial(project_kernel, first, rows, blocks, bit...  41.6 us
    ppermute x26, waiting for transfers between devices, swap(): lax.ppermute(value, 'tp', [(i, i ^ 1 << bit) for i in range(devices)])  32.8 us
    ppermute x26, starting transfers between devices, swap(): lax.ppermute(value, 'tp', [(i, i ^ 1 << bit) for i in range(devices)])  24.7 us
    pallas_call x2, Pallas kernels, product(): pl.pallas_call(functools.partial(product_kernel, pieces, bits), in_specs=...  4.56 us
    add x10, other arithmetic, shards(): keep = keep[:half] + received[:half]  4.42 us
    pallas_call x1, Pallas kernels, score(): pl.pallas_call(score_kernel, in_specs=[pl.BlockSpec(memory_space=pltpu.SM...  2.78 us
    add x4, other arithmetic, shards(): keep = keep + received  2.52 us
  transfers between devices with their start and end apart: 26, of which 16 were waited for; matrix products, arithmetic and copies ran while one was open for 7% of the time, Pallas kernels for 26%

profile of v2, /device:TPU:0, one launch (start us, length us, event | category | flops | bytes accessed | tf_op | source)
XLA Modules:
  0.0 117.4 jit_solution(5710817017857493100)
XLA Ops:
  0.0 6.3 %project.5 = (f32[512,128]{1,0:T(8,128)}, f32[512,128]{1,0:T(8,128)}) custom-call(s32[1]{0:T(128)} %bitcast.me_ref, bf16[8192,512]{1,0:T(8,128)(2,1)} %a_hbm.9, bf16[8192,1792]{1,0:T(8,128)(2,1)} %g_hbm.9, bf16[64,512]{1,0:T(8,128)(2,1)} %bitcast.8, bf16[64,1792]{1,0:T(8,128)(2,1)} %bitcast.3), custom_call_target="tpu_custom_call" | custom-call | flops 301989888 | bytes 4718592 | tf_op jit(solution)/shard_map/project/pallas_call | solution.py:61
  9.2 9.7 %project.6 = (f32[1024,128]{1,0:T(8,128)}, f32[1024,128]{1,0:T(8,128)}) custom-call(s32[1]{0:T(128)} %bitcast.me_ref, bf16[8192,512]{1,0:T(8,128)(2,1)} %a_hbm.9, bf16[8192,1792]{1,0:T(8,128)(2,1)} %g_hbm.9, bf16[64,512]{1,0:T(8,128)(2,1)} %bitcast.9, bf16[64,1792]{1,0:T(8,128)(2,1)} %bitcast.4), custom_call_target="tpu_custom_call" | custom-call | flops 603979776 | bytes 9437184 | tf_op jit(solution)/shard_map/project/pallas_call | solution.py:61
  19.5 2.7 %collective-permute-start.1 = (f32[256,128]{1,0:T(8,128)S(1)}, f32[256,128]{1,0:T(8,128)S(1)}, u32[]{:S(2)}, u32[]{:S(2)}) collective-permute-start(f32[256,128]{1,0:T(8,128)S(1)} %get-tuple-element.52), channel_id=1, source_target_pairs={{0,2},{1,3},{2,0},{3,1},{4,6},{5,7},{6,4},{7,5},{8,10},{9,11},{10,... | collective-permute-start | bytes 393224 | tf_op jit(solution)/shard_map/ppermute | solution.py:191
  23.3 1.8 %collective-permute-start.5 = (f32[512,128]{1,0:T(8,128)S(1)}, f32[512,128]{1,0:T(8,128)S(1)}, u32[]{:S(2)}, u32[]{:S(2)}) collective-permute-start(f32[512,128]{1,0:T(8,128)S(1)} %get-tuple-element.44), channel_id=1, source_target_pairs={{0,2},{1,3},{2,0},{3,1},{4,6},{5,7},{6,4},{7,5},{8,10},{9,11},{10,... | collective-permute-start | bytes 786440 | tf_op jit(solution)/shard_map/ppermute | solution.py:191
  26.3 1.9 %collective-permute-start.2 = (f32[128,128]{1,0:T(8,128)S(1)}, f32[128,128]{1,0:T(8,128)S(1)}, u32[]{:S(2)}, u32[]{:S(2)}) collective-permute-start(f32[128,128]{1,0:T(8,128)S(1)} %get-tuple-element.56), channel_id=1, source_target_pairs={{0,4},{1,5},{2,6},{3,7},{4,0},{5,1},{6,2},{7,3},{8,12},{9,13},{10,... | collective-permute-start | bytes 196616 | tf_op jit(solution)/shard_map/ppermute | solution.py:191
  28.2 3.7 %collective-permute-done.5 = f32[512,128]{1,0:T(8,128)S(1)} collective-permute-done((f32[512,128]{1,0:T(8,128)S(1)}, f32[512,128]{1,0:T(8,128)S(1)}, u32[]{:S(2)}, u32[]{:S(2)}) %collective-permute-start.5) | collective-permute-done | bytes 262176 | tf_op jit(solution)/shard_map/ppermute | solution.py:191
  31.9 1.9 %collective-permute-start.6 = (f32[256,128]{1,0:T(8,128)S(1)}, f32[256,128]{1,0:T(8,128)S(1)}, u32[]{:S(2)}, u32[]{:S(2)}) collective-permute-start(f32[256,128]{1,0:T(8,128)S(1)} %get-tuple-element.50), channel_id=1, source_target_pairs={{0,4},{1,5},{2,6},{3,7},{4,0},{5,1},{6,2},{7,3},{8,12},{9,13},{10,... | collective-permute-start | bytes 393224 | tf_op jit(solution)/shard_map/ppermute | solution.py:191
  33.8 2.7 %collective-permute-start.3 = (f32[64,128]{1,0:T(8,128)S(1)}, f32[64,128]{1,0:T(8,128)S(1)}, u32[]{:S(2)}, u32[]{:S(2)}) collective-permute-start(f32[64,128]{1,0:T(8,128)S(1)} %slice_add_fusion.28), channel_id=1, source_target_pairs={{0,8},{1,9},{2,10},{3,11},{4,12},{5,13},{6,14},{7,15},{8,0},{9,1},... | collective-permute-start | bytes 98312 | tf_op jit(solution)/shard_map/ppermute | solution.py:191
  36.4 9.6 %project.8 = (f32[1024,128]{1,0:T(8,128)}, f32[1024,128]{1,0:T(8,128)}) custom-call(s32[1]{0:T(128)} %bitcast.me_ref, bf16[8192,512]{1,0:T(8,128)(2,1)} %a_hbm.9, bf16[8192,1792]{1,0:T(8,128)(2,1)} %g_hbm.9, bf16[64,512]{1,0:T(8,128)(2,1)} %bitcast.10, bf16[64,1792]{1,0:T(8,128)(2,1)} %bitcast.5), custom_call_target="tpu_custom_call" | custom-call | flops 603979776 | bytes 9437184 | tf_op jit(solution)/shard_map/project/pallas_call | solution.py:61
  46.2 9.7 %project.7 = (f32[1024,128]{1,0:T(8,128)}, f32[1024,128]{1,0:T(8,128)}) custom-call(s32[1]{0:T(128)} %bitcast.me_ref, bf16[8192,512]{1,0:T(8,128)(2,1)} %a_hbm.9, bf16[8192,1792]{1,0:T(8,128)(2,1)} %g_hbm.9, bf16[64,512]{1,0:T(8,128)(2,1)} %bitcast.11, bf16[64,1792]{1,0:T(8,128)(2,1)} %bitcast.6), custom_call_target="tpu_custom_call" | custom-call | flops 603979776 | bytes 9437184 | tf_op jit(solution)/shard_map/project/pallas_call | solution.py:61
  57.5 5.3 %collective-permute-done.7 = f32[128,128]{1,0:T(8,128)S(1)} collective-permute-done((f32[128,128]{1,0:T(8,128)S(1)}, f32[128,128]{1,0:T(8,128)S(1)}, u32[]{:S(2)}, u32[]{:S(2)}) %collective-permute-start.7) | collective-permute-done | bytes 65568 | tf_op jit(solution)/shard_map/ppermute | solution.py:191
  66.7 6.3 %project.9 = (f32[512,128]{1,0:T(8,128)}, f32[512,128]{1,0:T(8,128)}) custom-call(s32[1]{0:T(128)} %bitcast.me_ref, bf16[8192,512]{1,0:T(8,128)(2,1)} %a_hbm.9, bf16[8192,1792]{1,0:T(8,128)(2,1)} %g_hbm.9, bf16[64,512]{1,0:T(8,128)(2,1)} %bitcast.12, bf16[64,1792]{1,0:T(8,128)(2,1)} %bitcast.7), custom_call_target="tpu_custom_call" | custom-call | flops 301989888 | bytes 4718592 | tf_op jit(solution)/shard_map/project/pallas_call | solution.py:61
  73.4 3.9 %collective-permute-done.9 = f32[512,128]{1,0:T(8,128)S(1)} collective-permute-done((f32[512,128]{1,0:T(8,128)S(1)}, f32[512,128]{1,0:T(8,128)S(1)}, u32[]{:S(2)}, u32[]{:S(2)}) %collective-permute-start.9) | collective-permute-done | bytes 262176 | tf_op jit(solution)/shard_map/ppermute | solution.py:191
  80.1 2.3 %collective-permute-done.10 = f32[256,128]{1,0:T(8,128)S(1)} collective-permute-done((f32[256,128]{1,0:T(8,128)S(1)}, f32[256,128]{1,0:T(8,128)S(1)}, u32[]{:S(2)}, u32[]{:S(2)}) %collective-permute-start.10) | collective-permute-done | bytes 131104 | tf_op jit(solution)/shard_map/ppermute | solution.py:191
  83.4 2.1 %collective-permute-start.20 = (f32[128,128]{1,0:T(8,128)S(1)}, f32[128,128]{1,0:T(8,128)S(1)}, u32[]{:S(2)}, u32[]{:S(2)}) collective-permute-start(f32[128,128]{1,0:T(8,128)S(1)} %get-tuple-element.58), channel_id=1, source_target_pairs={{0,4},{1,5},{2,6},{3,7},{4,0},{5,1},{6,2},{7,3},{8,12},{9,13},{10,... | collective-permute-start | bytes 196616 | tf_op jit(solution)/shard_map/ppermute | solution.py:191
  85.5 2.3 %collective-permute-done.15 = f32[128,128]{1,0:T(8,128)S(1)} collective-permute-done((f32[128,128]{1,0:T(8,128)S(1)}, f32[128,128]{1,0:T(8,128)S(1)}, u32[]{:S(2)}, u32[]{:S(2)}) %collective-permute-start.15) | collective-permute-done | bytes 65568 | tf_op jit(solution)/shard_map/ppermute | solution.py:191
  89.2 2.4 %product.2 = (f32[128,128]{1,0:T(8,128)}, f32[128,128]{1,0:T(8,128)}) custom-call(s32[1]{0:T(128)} %bitcast.me_ref, s32[9]{0:T(128)} %copy-done.4, f32[8]{0:T(128)} %convert_divide_fusion.scale_ref, f32[64,128]{1,0:T(8,128)} %fusion.3.refs_0_, f32[128,128]{1,0:T(8,128)} %fusion.2.refs_1_, f32[128,128]{1,0:T(8,128)} %fusion.1.refs_2_, f32[128,128]{1,0:T(8,128)} %fusion.refs_3_), custom_call_target="tpu_custom_call" | custom-call | tf_op jit(solution)/shard_map/product/pallas_call | solution.py:132
  93.9 1.6 %collective-permute-start.17 = (f32[128,128]{1,0:T(8,128)S(1)}, f32[128,128]{1,0:T(8,128)S(1)}, u32[]{:S(2)}, u32[]{:S(2)}) collective-permute-start(f32[128,128]{1,0:T(8,128)S(1)} %add.151), channel_id=1, source_target_pairs={{0,8},{1,9},{2,10},{3,11},{4,12},{5,13},{6,14},{7,15},{8,0},{9,1},... | collective-permute-start | bytes 196616 | tf_op jit(solution)/shard_map/ppermute | solution.py:191
  95.5 2.1 %collective-permute-done.21 = f32[128,128]{1,0:T(8,128)S(1)} collective-permute-done((f32[128,128]{1,0:T(8,128)S(1)}, f32[128,128]{1,0:T(8,128)S(1)}, u32[]{:S(2)}, u32[]{:S(2)}) %collective-permute-start.21) | collective-permute-done | bytes 65568 | tf_op jit(solution)/shard_map/ppermute | solution.py:191
  98.3 2.1 %product.3 = (f32[128,128]{1,0:T(8,128)}, f32[128,128]{1,0:T(8,128)}) custom-call(s32[1]{0:T(128)} %bitcast.me_ref, s32[9]{0:T(128)} %copy-done.4, f32[8]{0:T(128)} %convert_divide_fusion.scale_ref, f32[128,128]{1,0:T(8,128)} %maximum_add_fusion.refs_0_), custom_call_target="tpu_custom_call" | custom-call | tf_op jit(solution)/shard_map/product/pallas_call | solution.py:132
  102.7 3.1 %collective-permute-start.23 = (f32[128,128]{1,0:T(8,128)S(1)}, f32[128,128]{1,0:T(8,128)S(1)}, u32[]{:S(2)}, u32[]{:S(2)}) collective-permute-start(f32[128,128]{1,0:T(8,128)S(1)} %add_add_fusion), channel_id=1, source_target_pairs={{0,2},{1,3},{2,0},{3,1},{4,6},{5,7},{6,4},{7,5},{8,10},{9,11},{10,... | collective-permute-start | bytes 196616 | tf_op jit(solution)/shard_map/ppermute | solution.py:191
  105.8 2.4 %collective-permute-done.23 = f32[128,128]{1,0:T(8,128)S(1)} collective-permute-done((f32[128,128]{1,0:T(8,128)S(1)}, f32[128,128]{1,0:T(8,128)S(1)}, u32[]{:S(2)}, u32[]{:S(2)}) %collective-permute-start.23) | collective-permute-done | bytes 65568 | tf_op jit(solution)/shard_map/ppermute | solution.py:191
  108.3 4.3 %collective-permute-done.24 = f32[128,128]{1,0:T(8,128)S(1)} collective-permute-done((f32[128,128]{1,0:T(8,128)S(1)}, f32[128,128]{1,0:T(8,128)S(1)}, u32[]{:S(2)}, u32[]{:S(2)}) %collective-permute-start.24) | collective-permute-done | bytes 65568 | tf_op jit(solution)/shard_map/ppermute | solution.py:191
  114.6 2.8 %score.1 = f32[8,64]{1,0:T(8,128)} custom-call(s32[1]{0:T(128)S(6)} %shift_right_arithmetic.19.side_ref, f32[128,128]{1,0:T(8,128)} %copy-done.1, f32[128,128]{1,0:T(8,128)} %copy-done.2, f32[64,4096]{1,0:T(8,128)} %q_ref.1), custom_call_target="tpu_custom_call" | custom-call | tf_op jit(solution)/shard_map/score/pallas_call | solution.py:168
  (73 shorter events, 24.3 us)
Async XLA Ops:
  6.3 1.9 %collective-permute-start = (f32[512,128]{1,0:T(8,128)}, f32[512,128]{1,0:T(8,128)S(1)}, u32[]{:S(2)}, u32[]{:S(2)}) collective-permute-start(f32[512,128]{1,0:T(8,128)} %get-tuple-element.23), channel_id=1, source_target_pairs={{0,1},{1,0},{2,3},{3,2},{4,5},{5,4},{6,7},{7,6},{8,9},{9,8},{10,11... | collective-permute-start | bytes 786440 | tf_op jit(solution)/shard_map/ppermute | solution.py:191
  18.9 3.4 %collective-permute-start.4 = (f32[1024,128]{1,0:T(8,128)}, f32[1024,128]{1,0:T(8,128)S(1)}, u32[]{:S(2)}, u32[]{:S(2)}) collective-permute-start(f32[1024,128]{1,0:T(8,128)} %get-tuple-element.26), channel_id=1, source_target_pairs={{0,1},{1,0},{2,3},{3,2},{4,5},{5,4},{6,7},{7,6},{8,9},{9,8},{10,11... | collective-permute-start | bytes 1572872 | tf_op jit(solution)/shard_map/ppermute | solution.py:191
  19.5 6.8 %collective-permute-start.1 = (f32[256,128]{1,0:T(8,128)S(1)}, f32[256,128]{1,0:T(8,128)S(1)}, u32[]{:S(2)}, u32[]{:S(2)}) collective-permute-start(f32[256,128]{1,0:T(8,128)S(1)} %get-tuple-element.52), channel_id=1, source_target_pairs={{0,2},{1,3},{2,0},{3,1},{4,6},{5,7},{6,4},{7,5},{8,10},{9,11},{10,... | collective-permute-start | bytes 393224 | tf_op jit(solution)/shard_map/ppermute | solution.py:191
  23.3 8.5 %collective-permute-start.5 = (f32[512,128]{1,0:T(8,128)S(1)}, f32[512,128]{1,0:T(8,128)S(1)}, u32[]{:S(2)}, u32[]{:S(2)}) collective-permute-start(f32[512,128]{1,0:T(8,128)S(1)} %get-tuple-element.44), channel_id=1, source_target_pairs={{0,2},{1,3},{2,0},{3,1},{4,6},{5,7},{6,4},{7,5},{8,10},{9,11},{10,... | collective-permute-start | bytes 786440 | tf_op jit(solution)/shard_map/ppermute | solution.py:191
  26.3 7.4 %collective-permute-start.2 = (f32[128,128]{1,0:T(8,128)S(1)}, f32[128,128]{1,0:T(8,128)S(1)}, u32[]{:S(2)}, u32[]{:S(2)}) collective-permute-start(f32[128,128]{1,0:T(8,128)S(1)} %get-tuple-element.56), channel_id=1, source_target_pairs={{0,4},{1,5},{2,6},{3,7},{4,0},{5,1},{6,2},{7,3},{8,12},{9,13},{10,... | collective-permute-start | bytes 196616 | tf_op jit(solution)/shard_map/ppermute | solution.py:191
  31.9 24.5 %collective-permute-start.6 = (f32[256,128]{1,0:T(8,128)S(1)}, f32[256,128]{1,0:T(8,128)S(1)}, u32[]{:S(2)}, u32[]{:S(2)}) collective-permute-start(f32[256,128]{1,0:T(8,128)S(1)} %get-tuple-element.50), channel_id=1, source_target_pairs={{0,4},{1,5},{2,6},{3,7},{4,0},{5,1},{6,2},{7,3},{8,12},{9,13},{10,... | collective-permute-start | bytes 393224 | tf_op jit(solution)/shard_map/ppermute | solution.py:191
  33.8 23.1 %collective-permute-start.3 = (f32[64,128]{1,0:T(8,128)S(1)}, f32[64,128]{1,0:T(8,128)S(1)}, u32[]{:S(2)}, u32[]{:S(2)}) collective-permute-start(f32[64,128]{1,0:T(8,128)S(1)} %slice_add_fusion.28), channel_id=1, source_target_pairs={{0,8},{1,9},{2,10},{3,11},{4,12},{5,13},{6,14},{7,15},{8,0},{9,1},... | collective-permute-start | bytes 98312 | tf_op jit(solution)/shard_map/ppermute | solution.py:191
  46.1 17.3 %collective-permute-start.12 = (f32[1024,128]{1,0:T(8,128)}, f32[1024,128]{1,0:T(8,128)S(1)}, u32[]{:S(2)}, u32[]{:S(2)}) collective-permute-start(f32[1024,128]{1,0:T(8,128)} %get-tuple-element.31), channel_id=1, source_target_pairs={{0,1},{1,0},{2,3},{3,2},{4,5},{5,4},{6,7},{7,6},{8,9},{9,8},{10,11... | collective-permute-start | bytes 1572872 | tf_op jit(solution)/shard_map/ppermute | solution.py:191
  55.9 9.1 %collective-permute-start.8 = (f32[1024,128]{1,0:T(8,128)}, f32[1024,128]{1,0:T(8,128)S(1)}, u32[]{:S(2)}, u32[]{:S(2)}) collective-permute-start(f32[1024,128]{1,0:T(8,128)} %get-tuple-element.29), channel_id=1, source_target_pairs={{0,1},{1,0},{2,3},{3,2},{4,5},{5,4},{6,7},{7,6},{8,9},{9,8},{10,11... | collective-permute-start | bytes 1572872 | tf_op jit(solution)/shard_map/ppermute | solution.py:191
  56.4 6.3 %collective-permute-start.7 = (f32[128,128]{1,0:T(8,128)S(1)}, f32[128,128]{1,0:T(8,128)S(1)}, u32[]{:S(2)}, u32[]{:S(2)}) collective-permute-start(f32[128,128]{1,0:T(8,128)S(1)} %slice_add_fusion.22), channel_id=1, source_target_pairs={{0,8},{1,9},{2,10},{3,11},{4,12},{5,13},{6,14},{7,15},{8,0},{9,1},... | collective-permute-start | bytes 196616 | tf_op jit(solution)/shard_map/ppermute | solution.py:191
  63.5 9.8 %collective-permute-start.13 = (f32[512,128]{1,0:T(8,128)S(1)}, f32[512,128]{1,0:T(8,128)S(1)}, u32[]{:S(2)}, u32[]{:S(2)}) collective-permute-start(f32[512,128]{1,0:T(8,128)S(1)} %get-tuple-element.40), channel_id=1, source_target_pairs={{0,2},{1,3},{2,0},{3,1},{4,6},{5,7},{6,4},{7,5},{8,10},{9,11},{10,... | collective-permute-start | bytes 786440 | tf_op jit(solution)/shard_map/ppermute | solution.py:191
  66.2 11.1 %collective-permute-start.9 = (f32[512,128]{1,0:T(8,128)S(1)}, f32[512,128]{1,0:T(8,128)S(1)}, u32[]{:S(2)}, u32[]{:S(2)}) collective-permute-start(f32[512,128]{1,0:T(8,128)S(1)} %get-tuple-element.42), channel_id=1, source_target_pairs={{0,2},{1,3},{2,0},{3,1},{4,6},{5,7},{6,4},{7,5},{8,10},{9,11},{10,... | collective-permute-start | bytes 786440 | tf_op jit(solution)/shard_map/ppermute | solution.py:191
  73.0 4.4 %collective-permute-start.18 = (f32[512,128]{1,0:T(8,128)}, f32[512,128]{1,0:T(8,128)S(1)}, u32[]{:S(2)}, u32[]{:S(2)}) collective-permute-start(f32[512,128]{1,0:T(8,128)} %get-tuple-element.36), channel_id=1, source_target_pairs={{0,1},{1,0},{2,3},{3,2},{4,5},{5,4},{6,7},{7,6},{8,9},{9,8},{10,11... | collective-permute-start | bytes 786440 | tf_op jit(solution)/shard_map/ppermute | solution.py:191
  73.3 6.7 %collective-permute-start.14 = (f32[256,128]{1,0:T(8,128)S(1)}, f32[256,128]{1,0:T(8,128)S(1)}, u32[]{:S(2)}, u32[]{:S(2)}) collective-permute-start(f32[256,128]{1,0:T(8,128)S(1)} %get-tuple-element.46), channel_id=1, source_target_pairs={{0,4},{1,5},{2,6},{3,7},{4,0},{5,1},{6,2},{7,3},{8,12},{9,13},{10,... | collective-permute-start | bytes 393224 | tf_op jit(solution)/shard_map/ppermute | solution.py:191
  77.3 5.0 %collective-permute-start.10 = (f32[256,128]{1,0:T(8,128)S(1)}, f32[256,128]{1,0:T(8,128)S(1)}, u32[]{:S(2)}, u32[]{:S(2)}) collective-permute-start(f32[256,128]{1,0:T(8,128)S(1)} %get-tuple-element.48), channel_id=1, source_target_pairs={{0,4},{1,5},{2,6},{3,7},{4,0},{5,1},{6,2},{7,3},{8,12},{9,13},{10,... | collective-permute-start | bytes 393224 | tf_op jit(solution)/shard_map/ppermute | solution.py:191
  78.4 5.0 %collective-permute-start.19 = (f32[256,128]{1,0:T(8,128)S(1)}, f32[256,128]{1,0:T(8,128)S(1)}, u32[]{:S(2)}, u32[]{:S(2)}) collective-permute-start(f32[256,128]{1,0:T(8,128)S(1)} %get-tuple-element.54), channel_id=1, source_target_pairs={{0,2},{1,3},{2,0},{3,1},{4,6},{5,7},{6,4},{7,5},{8,10},{9,11},{10,... | collective-permute-start | bytes 393224 | tf_op jit(solution)/shard_map/ppermute | solution.py:191
  80.0 7.8 %collective-permute-start.15 = (f32[128,128]{1,0:T(8,128)S(1)}, f32[128,128]{1,0:T(8,128)S(1)}, u32[]{:S(2)}, u32[]{:S(2)}) collective-permute-start(f32[128,128]{1,0:T(8,128)S(1)} %slice_add_fusion.18), channel_id=1, source_target_pairs={{0,8},{1,9},{2,10},{3,11},{4,12},{5,13},{6,14},{7,15},{8,0},{9,1},... | collective-permute-start | bytes 196616 | tf_op jit(solution)/shard_map/ppermute | solution.py:191
  82.3 6.2 %collective-permute-start.11 = (f32[128,128]{1,0:T(8,128)S(1)}, f32[128,128]{1,0:T(8,128)S(1)}, u32[]{:S(2)}, u32[]{:S(2)}) collective-permute-start(f32[128,128]{1,0:T(8,128)S(1)} %slice_add_fusion.20), channel_id=1, source_target_pairs={{0,8},{1,9},{2,10},{3,11},{4,12},{5,13},{6,14},{7,15},{8,0},{9,1},... | collective-permute-start | bytes 196616 | tf_op jit(solution)/shard_map/ppermute | solution.py:191
  83.4 8.1 %collective-permute-start.20 = (f32[128,128]{1,0:T(8,128)S(1)}, f32[128,128]{1,0:T(8,128)S(1)}, u32[]{:S(2)}, u32[]{:S(2)}) collective-permute-start(f32[128,128]{1,0:T(8,128)S(1)} %get-tuple-element.58), channel_id=1, source_target_pairs={{0,4},{1,5},{2,6},{3,7},{4,0},{5,1},{6,2},{7,3},{8,12},{9,13},{10,... | collective-permute-start | bytes 196616 | tf_op jit(solution)/shard_map/ppermute | solution.py:191
  91.6 1.5 %collective-permute-start.16 = (f32[128,128]{1,0:T(8,128)}, f32[128,128]{1,0:T(8,128)S(1)}, u32[]{:S(2)}, u32[]{:S(2)}) collective-permute-start(f32[128,128]{1,0:T(8,128)} %get-tuple-element.33), channel_id=1, source_target_pairs={{0,1},{1,0},{2,3},{3,2},{4,5},{5,4},{6,7},{7,6},{8,9},{9,8},{10,11... | collective-permute-start | bytes 196616 | tf_op jit(solution)/shard_map/ppermute | solution.py:191
  91.6 6.0 %collective-permute-start.21 = (f32[128,128]{1,0:T(8,128)S(1)}, f32[128,128]{1,0:T(8,128)S(1)}, u32[]{:S(2)}, u32[]{:S(2)}) collective-permute-start(f32[128,128]{1,0:T(8,128)S(1)} %pad_maximum_fusion), channel_id=1, source_target_pairs={{0,8},{1,9},{2,10},{3,11},{4,12},{5,13},{6,14},{7,15},{8,0},{9,1},... | collective-permute-start | bytes 196616 | tf_op jit(solution)/shard_map/ppermute | solution.py:191
  93.9 6.6 %collective-permute-start.17 = (f32[128,128]{1,0:T(8,128)S(1)}, f32[128,128]{1,0:T(8,128)S(1)}, u32[]{:S(2)}, u32[]{:S(2)}) collective-permute-start(f32[128,128]{1,0:T(8,128)S(1)} %add.151), channel_id=1, source_target_pairs={{0,8},{1,9},{2,10},{3,11},{4,12},{5,13},{6,14},{7,15},{8,0},{9,1},... | collective-permute-start | bytes 196616 | tf_op jit(solution)/shard_map/ppermute | solution.py:191
  102.7 5.5 %collective-permute-start.23 = (f32[128,128]{1,0:T(8,128)S(1)}, f32[128,128]{1,0:T(8,128)S(1)}, u32[]{:S(2)}, u32[]{:S(2)}) collective-permute-start(f32[128,128]{1,0:T(8,128)S(1)} %add_add_fusion), channel_id=1, source_target_pairs={{0,2},{1,3},{2,0},{3,1},{4,6},{5,7},{6,4},{7,5},{8,10},{9,11},{10,... | collective-permute-start | bytes 196616 | tf_op jit(solution)/shard_map/ppermute | solution.py:191
  108.3 4.3 %collective-permute-start.24 = (f32[128,128]{1,0:T(8,128)S(1)}, f32[128,128]{1,0:T(8,128)S(1)}, u32[]{:S(2)}, u32[]{:S(2)}) collective-permute-start(f32[128,128]{1,0:T(8,128)S(1)} %add.162), channel_id=1, source_target_pairs={{0,4},{1,5},{2,6},{3,7},{4,0},{5,1},{6,2},{7,3},{8,12},{9,13},{10,... | collective-permute-start | bytes 196616 | tf_op jit(solution)/shard_map/ppermute | solution.py:191
  (7 other events, 77.8 us)

commit v3 on v0

v3 whole, which is shorter than its diff:
```python
import functools

import jax
import jax.numpy as jnp
from jax import lax
from jax.experimental import pallas as pl
from jax.experimental.pallas import tpu as pltpu
from jax.sharding import PartitionSpec as P

SEQS = 8
UNITS = 16
CHUNKS = (4, 4, 4, 3, 1)
BOTH_SIDES = 2
BLOCK = 512
VMEM = 48 * 1024 * 1024
ROWS_BY_ROWS = (((1,), (1,)), ((), ()))


def project_kernel(bits, block_bits, shares, a_hbm, g_hbm, pi_hbm, po_hbm, *refs):
    outs, (pi_ref, po_ref, a_buf, g_buf, sems) = refs[:-5], refs[-5:]
    ring, size = a_buf.shape[0], a_buf.shape[1]
    blocks = 1 << block_bits
    count = 1 << (bits - block_bits)
    own = size // count
    half = blocks // 2
    me_rev = reversed_index(bits)
    high = me_rev >> (bits - block_bits)
    low = me_rev & (count - 1)

    def copies(step):
        slot = lax.rem(step, ring)
        start = pl.multiple_of((step ^ high) * size, size)
        return (
            pltpu.make_async_copy(a_hbm.at[pl.ds(start, size), :], a_buf.at[slot], sems.at[slot, 0]),
            pltpu.make_async_copy(g_hbm.at[pl.ds(start, size), :], g_buf.at[slot], sems.at[slot, 1]),
        )

    weights = (
        pltpu.make_async_copy(pi_hbm, pi_ref, sems.at[ring, 0]),
        pltpu.make_async_copy(po_hbm, po_ref, sems.at[ring, 1]),
    )
    for copy in weights:
        copy.start()
    for step in range(min(ring - 1, blocks)):
        for copy in copies(jnp.int32(step)):
            copy.start()
    for copy in weights:
        copy.wait()

    def body(step, carry):
        @pl.when(step + ring - 1 < blocks)
        def _():
            for copy in copies(step + ring - 1):
                copy.start()

        for copy in copies(step):
            copy.wait()
        slot = lax.rem(step, ring)
        side_x = lax.dot_general(a_buf[slot], pi_ref[...], ROWS_BY_ROWS, preferred_element_type=jnp.float32)
        side_g = lax.dot_general(g_buf[slot], po_ref[...], ROWS_BY_ROWS, preferred_element_type=jnp.float32)
        both = jnp.concatenate([side_x, side_g], axis=1)
        base = (step & (half - 1)) * count

        def store(out_refs):
            for part in range(count):
                place = base + (part ^ low)
                row = part * own
                for share, out_ref in zip(shares, out_refs, strict=True):
                    start = pl.multiple_of(place * share, 8)
                    out_ref[pl.ds(start, share), :] = both[row : row + share]
                    row += share

        @pl.when(step < half)
        def _():
            store(outs[1::2])

        @pl.when(step >= half)
        def _():
            store(outs[0::2])

        return carry

    lax.fori_loop(0, blocks, body, 0)


def reversed_index(bits):
    me = lax.axis_index("tp").astype(jnp.int32)
    flipped = jnp.int32(0)
    for b in range(bits):
        flipped = flipped | (((me >> b) & 1) << (bits - 1 - b))
    return flipped


def project(bits, shares, activations, out_grads, proj_in, proj_out):
    tokens, width = activations.shape
    hidden = out_grads.shape[1]
    rank = proj_in.shape[0]
    block_bits = min(bits, max(2, (tokens // BLOCK - 1).bit_length()))
    size = tokens >> block_bits
    ring = 4
    outs = [
        jax.ShapeDtypeStruct(((1 << bits) // 2 * share, 2 * rank), jnp.float32)
        for share in shares
        for _ in range(2)
    ]
    vmem = pl.BlockSpec(memory_space=pltpu.VMEM)
    return pl.pallas_call(
        functools.partial(project_kernel, bits, block_bits, shares),
        in_specs=[pl.BlockSpec(memory_space=pl.ANY)] * 4,
        out_specs=[vmem] * len(outs),
        out_shape=outs,
        scratch_shapes=[
            pltpu.VMEM(proj_in.shape, proj_in.dtype),
            pltpu.VMEM(proj_out.shape, proj_out.dtype),
            pltpu.VMEM((ring, size, width), activations.dtype),
            pltpu.VMEM((ring, size, hidden), out_grads.dtype),
            pltpu.SemaphoreType.DMA((ring + 1, 2)),
        ],
        compiler_params=pltpu.CompilerParams(vmem_limit_bytes=VMEM),
        name="project",
    )(activations, out_grads, proj_in, proj_out)


def product_kernel(pieces, bits, own, edge_ref, scale_ref, *refs):
    term_refs = refs[: len(pieces)]
    send_ref, keep_ref, held_ref = refs[len(pieces) :]
    terms = jnp.concatenate([ref[...] for ref in term_refs], axis=0)
    total_rows = terms.shape[0]
    rank = terms.shape[1] // 2
    me = reversed_index(bits)
    lane = lax.broadcasted_iota(jnp.int32, (1, total_rows), 1)
    token = lane
    offset = 0
    for first, rows, count in pieces:
        for part in range(count):
            start = (me ^ part) * own + first
            token = jnp.where(lane >= offset, lane + (start - offset), token)
            offset += rows
    proj_x = terms[:, :rank]
    x_hi = proj_x.astype(jnp.bfloat16)
    x_lo = (proj_x - x_hi.astype(jnp.float32)).astype(jnp.bfloat16)
    x_both = jnp.concatenate([x_hi, x_lo], axis=1)
    g_rows = terms.T[rank:, :]
    half = rank // 2
    side = me >> (bits - 1)
    group = SEQS // 2
    places = [place ^ (side * group) for place in range(SEQS)]
    high_parts, low_parts = [], []
    for s in places:
        inside = (token >= edge_ref[s]) & (token < edge_ref[s + 1])
        masked = jnp.where(inside, g_rows, 0.0)
        g_hi = masked.astype(jnp.bfloat16)
        high_parts.append(g_hi)
        low_parts.append((masked - g_hi.astype(jnp.float32)).astype(jnp.bfloat16))
    g_both = jnp.concatenate(high_parts + low_parts, axis=0)
    quad = jnp.dot(g_both, x_both, preferred_element_type=jnp.float32)
    upper, lower = quad[: SEQS * rank], quad[SEQS * rank :]
    total = upper[:, :rank] + (upper[:, rank:] + lower[:, :rank] + lower[:, rank:])
    for place, s in enumerate(places):
        rows = slice(place * rank, (place + 1) * rank)
        held_ref[rows, :rank] = total[rows] * scale_ref[s]
    even = held_ref[pl.ds(0, SEQS * half, stride=2), :]
    odd = held_ref[pl.ds(1, SEQS * half, stride=2), :]
    packed = jnp.concatenate([even[:, :rank], odd[:, :rank]], axis=1)
    keep_ref[...] = packed[: group * half]
    send_ref[...] = packed[group * half :]


def product(pieces, bits, own, edges, scale, terms):
    rank = terms[0].shape[1] // 2
    out = jax.ShapeDtypeStruct((SEQS // 2 * rank // 2, 2 * rank), jnp.float32)
    vmem = pl.BlockSpec(memory_space=pltpu.VMEM)
    smem = pl.BlockSpec(memory_space=pltpu.SMEM)
    return pl.pallas_call(
        functools.partial(product_kernel, pieces, bits, own),
        in_specs=[smem, smem] + [vmem] * len(terms),
        out_specs=[vmem, vmem],
        out_shape=[out, out],
        scratch_shapes=[pltpu.VMEM((SEQS * rank, 2 * rank), jnp.float32)],
        compiler_params=pltpu.CompilerParams(vmem_limit_bytes=VMEM // 4),
        name="product",
    )(edges, scale, *terms)


def shards(devices, activations, out_grads, proj_in, proj_out, seg_ids, queries):
    bits = devices.bit_length() - 1
    last = bits - 1
    rank = proj_in.shape[1]
    tokens = activations.shape[0]
    own = tokens // devices
    me = lax.axis_index("tp")

    def swap(value, bit):
        return lax.ppermute(value, "tp", [(i, i ^ (1 << bit)) for i in range(devices)])

    edges = jnp.sum(
        (seg_ids[None, :] < jnp.arange(SEQS + 1, dtype=jnp.int32)[:, None]).astype(jnp.int32), axis=1
    )
    scale = 1.0 / (edges[1:] - edges[:-1]).astype(jnp.float32)

    shares = tuple(own * share // UNITS for share in CHUNKS)
    chunks = len(shares)
    halves = project(bits, shares, activations, out_grads, proj_in.T, proj_out.T)
    sends, keeps = list(halves[0::2]), list(halves[1::2])
    on_both = [k >= chunks - BOTH_SIDES for k in range(chunks)]
    moves = sorted(
        ((k, b) for k in range(chunks) for b in range(bits)),
        key=lambda move: (0 if move[1] == 0 else move[0] + move[1], move[1], move[0]),
    )
    latest = None
    for k, b in moves:
        send, keep = sends[k], keeps[k]
        both = b == last and on_both[k]
        received = swap(jnp.concatenate([send, keep], axis=0) if both else send, b)
        if latest is not None:
            received, _ = lax.optimization_barrier((received, latest))
        if both:
            keeps[k] = latest = jnp.concatenate([keep, send], axis=0) + received
        elif b == last:
            keeps[k] = latest = keep + received
        else:
            half = keep.shape[0] // 2
            sends[k] = latest = keep[half:] + received[half:]
            keeps[k] = keep[:half] + received[:half]
    pieces = [(sum(shares[:k]), shares[k], 2 if on_both[k] else 1) for k in range(chunks)]
    early = [(keeps[k], pieces[k]) for k in range(chunks) if not on_both[k]]
    late = [(keeps[k], pieces[k]) for k in range(chunks) if on_both[k]]

    def group_product(group):
        return product(tuple(p for _, p in group), bits, own, edges, scale, [t for t, _ in group])

    send, keep = group_product(early)
    grads = keep + swap(send, 0)
    grads = grads + swap(grads, last)
    send, keep = group_product(late)
    grads = grads + keep + swap(send, 0)
    for b in range(1, last):
        grads = grads + swap(grads, b)
    pair = jnp.concatenate([grads, swap(grads, 0)], axis=0).reshape(SEQS, rank * rank)
    scores = jnp.dot(
        pair, queries.T, precision=lax.Precision.HIGHEST, preferred_element_type=jnp.float32
    )
    turned = jnp.concatenate([scores[SEQS // 2 :], scores[: SEQS // 2]], axis=0)
    return jnp.where((me & 1) == 0, scores, turned)


def solution(mesh):
    placed = (P("grp", "tp"), P("grp", "tp"), P("tp", None), P("tp", None), P("grp"), P("tp", None))
    return jax.shard_map(
        functools.partial(shards, mesh.shape["tp"]),
        mesh=mesh,
        in_specs=placed,
        out_specs=P("grp", "tp"),
        check_vma=False,
    )
```

time: 177 us -> 75.7 us (0.43)
  waiting for transfers between devices: 113 us -> 19.2 us
  matrix products: 37.7 us -> 0.91 us
  starting transfers between devices: 0.01 us -> 33.7 us
  Pallas kernels: 0 us -> 18.2 us
  between operations: 13.4 us -> 0.22 us
  other arithmetic: 10.2 us -> 1.39 us
    psum x1 -> x0, waiting for transfers between devices: 113 us -> none  [shards(): summed = lax.psum(partial_terms, 'tp')]
    dot_general x4 -> x1, matrix products: 37.7 us -> 0.91 us  [shards(): jnp.dot(pair, queries.T, precision=lax.Precision.HIGHEST, preferred_eleme...]
    ppermute x0 -> x26, starting transfers between devices: none -> 33.7 us  [swap(): lax.ppermute(value, 'tp', [(i, i ^ 1 << bit) for i in range(devices)])]
    ppermute x0 -> x26, waiting for transfers between devices: none -> 19.2 us  [swap(): lax.ppermute(value, 'tp', [(i, i ^ 1 << bit) for i in range(devices)])]
    pallas_call x0 -> x3, Pallas kernels: none -> 18.2 us  [the longest x1 15.7 us: project(): pl.pallas_call(functools.partial(project_kernel, bits, block_bits, shares...]
    mul x1 -> x0, other arithmetic: 7.75 us -> none  [sequence_sums(): onehot[:, :, None] * proj_g[:, None, :]]
    concatenate x1 -> x3, other arithmetic: 2.23 us -> 0.02 us  [the longest x2 0.01 us: shards(): received = swap(jnp.concatenate([send, keep], axis=0) if both else send, b)]
  transfers between devices with their start and end apart: 1 -> 26, of which waited for: 1 -> 10; matrix products, arithmetic and copies ran while one was open for 0% -> 1% of each run, Pallas kernels for 0% -> 3%
where the time goes in v3:
time: 75.7 us; the launch traced here: 75.5 us
  starting transfers between devices  33.7 us (45%)
  waiting for transfers between devices  19.2 us (25%)
  Pallas kernels  18.2 us (24%)
  local copies, waits for them, and re-layouts  1.91 us (3%)
  other arithmetic  1.39 us (2%)
  matrix products  0.91 us (1%)
    ppermute x26, starting transfers between devices, swap(): lax.ppermute(value, 'tp', [(i, i ^ 1 << bit) for i in range(devices)])  33.7 us
    ppermute x26, waiting for transfers between devices, swap(): lax.ppermute(value, 'tp', [(i, i ^ 1 << bit) for i in range(devices)])  19.2 us
    pallas_call x1, Pallas kernels, project(): pl.pallas_call(functools.partial(project_kernel, bits, block_bits, shares...  15.7 us
    pallas_call x2, Pallas kernels, product(): pl.pallas_call(functools.partial(product_kernel, pieces, bits, own), in_s...  2.47 us
    unnamed x8, local copies, waits for them, and re-layouts  1.87 us
  transfers between devices with their start and end apart: 26, of which 10 were waited for; matrix products, arithmetic and copies ran while one was open for 1% of the time, Pallas kernels for 3%

profile of v3, /device:TPU:0, one launch (start us, length us, event | category | flops | bytes accessed | tf_op | source)
XLA Modules:
  0.0 75.5 jit_solution(3926964390513478968)
XLA Ops:
  0.0 1.0 %copy-done.1 = bf16[1792,64]{0,1:T(8,128)(2,1)S(1)} copy-done((bf16[1792,64]{0,1:T(8,128)(2,1)S(1)}, bf16[1792,64]{0,1:T(8,128)(2,1)}, u32[]{:S(2)}) %copy-start.1) | copy-done | bytes 229400
  1.9 15.7 %project.1 = (f32[1024,128]{1,0:T(8,128)S(1)}, f32[1024,128]{1,0:T(8,128)S(1)}, f32[1024,128]{1,0:T(8,128)S(1)}, f32[1024,128]{1,0:T(8,128)S(1)}, f32[1024,128]{...) custom-call(bf16[8192,512]{1,0:T(8,128)(2,1)} %a_hbm.1, ...), custom_call_target="tpu_custom_call" | custom-call | tf_op jit(solution)/shard_map/project/pallas_call | solution.py:107
  19.7 3.0 %collective-permute-start.1 = (f32[512,128]{1,0:T(8,128)S(1)}, f32[512,128]{1,0:T(8,128)S(1)}, u32[]{:S(2)}, u32[]{:S(2)}) collective-permute-start(f32[512,128]{1,0:T(8,128)S(1)} %get-tuple-element.76), channel_id=1, source_target_pairs={{0,2},{1,3},{2,0},{3,1},{4,6},{5,7},{6,4},{7,5},{8,10},{9,11},{10,... | collective-permute-start | bytes 786440 | tf_op jit(solution)/shard_map/ppermute | solution.py:194
  23.5 1.5 %collective-permute-start.10 = (f32[512,128]{1,0:T(8,128)S(1)}, f32[512,128]{1,0:T(8,128)S(1)}, u32[]{:S(2)}, u32[]{:S(2)}) collective-permute-start(f32[512,128]{1,0:T(8,128)S(1)} %get-tuple-element.72), channel_id=1, source_target_pairs={{0,2},{1,3},{2,0},{3,1},{4,6},{5,7},{6,4},{7,5},{8,10},{9,11},{10,... | collective-permute-start | bytes 786440 | tf_op jit(solution)/shard_map/ppermute | solution.py:194
  25.7 1.5 %collective-permute-start.16 = (f32[128,128]{1,0:T(8,128)S(1)}, f32[128,128]{1,0:T(8,128)S(1)}, u32[]{:S(2)}, u32[]{:S(2)}) collective-permute-start(f32[128,128]{1,0:T(8,128)S(1)} %get-tuple-element.88), channel_id=1, source_target_pairs={{0,2},{1,3},{2,0},{3,1},{4,6},{5,7},{6,4},{7,5},{8,10},{9,11},{10,... | collective-permute-start | bytes 196616 | tf_op jit(solution)/shard_map/ppermute | solution.py:194
  27.2 2.6 %collective-permute-done.1 = f32[512,128]{1,0:T(8,128)S(1)} collective-permute-done((f32[512,128]{1,0:T(8,128)S(1)}, f32[512,128]{1,0:T(8,128)S(1)}, u32[]{:S(2)}, u32[]{:S(2)}) %collective-permute-start.1) | collective-permute-done | bytes 262176 | tf_op jit(solution)/shard_map/ppermute | solution.py:194
  29.8 2.2 %collective-permute-start.6 = (f32[256,128]{1,0:T(8,128)S(1)}, f32[256,128]{1,0:T(8,128)S(1)}, u32[]{:S(2)}, u32[]{:S(2)}) collective-permute-start(f32[256,128]{1,0:T(8,128)S(1)} %get-tuple-element.83), channel_id=1, source_target_pairs={{0,4},{1,5},{2,6},{3,7},{4,0},{5,1},{6,2},{7,3},{8,12},{9,13},{10,... | collective-permute-start | bytes 393224 | tf_op jit(solution)/shard_map/ppermute | solution.py:194
  32.0 3.4 %collective-permute-done.7 = f32[512,128]{1,0:T(8,128)S(1)} collective-permute-done((f32[512,128]{1,0:T(8,128)S(1)}, f32[512,128]{1,0:T(8,128)S(1)}, u32[]{:S(2)}, u32[]{:S(2)}) %collective-permute-start.7) | collective-permute-done | bytes 262176 | tf_op jit(solution)/shard_map/ppermute | solution.py:194
  35.4 2.2 %collective-permute-start.9 = (f32[256,128]{1,0:T(8,128)S(1)}, f32[256,128]{1,0:T(8,128)S(1)}, u32[]{:S(2)}, u32[]{:S(2)}) collective-permute-start(f32[256,128]{1,0:T(8,128)S(1)} %get-tuple-element.82), channel_id=1, source_target_pairs={{0,4},{1,5},{2,6},{3,7},{4,0},{5,1},{6,2},{7,3},{8,12},{9,13},{10,... | collective-permute-start | bytes 393224 | tf_op jit(solution)/shard_map/ppermute | solution.py:194
  37.6 2.7 %collective-permute-start.8 = (f32[128,128]{1,0:T(8,128)S(1)}, f32[128,128]{1,0:T(8,128)S(1)}, u32[]{:S(2)}, u32[]{:S(2)}) collective-permute-start(f32[128,128]{1,0:T(8,128)S(1)} %slice_add_fusion.20), channel_id=1, source_target_pairs={{0,8},{1,9},{2,10},{3,11},{4,12},{5,13},{6,14},{7,15},{8,0},{9,1},... | collective-permute-start | bytes 196616 | tf_op jit(solution)/shard_map/ppermute | solution.py:194
  41.0 2.2 %collective-permute-start.12 = (f32[256,128]{1,0:T(8,128)S(1)}, f32[256,128]{1,0:T(8,128)S(1)}, u32[]{:S(2)}, u32[]{:S(2)}) collective-permute-start(f32[256,128]{1,0:T(8,128)S(1)} %get-tuple-element.80), channel_id=1, source_target_pairs={{0,4},{1,5},{2,6},{3,7},{4,0},{5,1},{6,2},{7,3},{8,12},{9,13},{10,... | collective-permute-start | bytes 393224 | tf_op jit(solution)/shard_map/ppermute | solution.py:194
  43.2 2.7 %collective-permute-start.11 = (f32[128,128]{1,0:T(8,128)S(1)}, f32[128,128]{1,0:T(8,128)S(1)}, u32[]{:S(2)}, u32[]{:S(2)}) collective-permute-start(f32[128,128]{1,0:T(8,128)S(1)} %slice_add_fusion.19), channel_id=1, source_target_pairs={{0,8},{1,9},{2,10},{3,11},{4,12},{5,13},{6,14},{7,15},{8,0},{9,1},... | collective-permute-start | bytes 196616 | tf_op jit(solution)/shard_map/ppermute | solution.py:194
  45.9 1.4 %collective-permute-start.15 = (f32[192,128]{1,0:T(8,128)S(1)}, f32[192,128]{1,0:T(8,128)S(1)}, u32[]{:S(2)}, u32[]{:S(2)}) collective-permute-start(f32[192,128]{1,0:T(8,128)S(1)} %get-tuple-element.85), channel_id=1, source_target_pairs={{0,4},{1,5},{2,6},{3,7},{4,0},{5,1},{6,2},{7,3},{8,12},{9,13},{10,... | collective-permute-start | bytes 294920 | tf_op jit(solution)/shard_map/ppermute | solution.py:194
  47.3 2.7 %collective-permute-start.14 = (f32[128,128]{1,0:T(8,128)S(1)}, f32[128,128]{1,0:T(8,128)S(1)}, u32[]{:S(2)}, u32[]{:S(2)}) collective-permute-start(f32[128,128]{1,0:T(8,128)S(1)} %slice_add_fusion.17), channel_id=1, source_target_pairs={{0,8},{1,9},{2,10},{3,11},{4,12},{5,13},{6,14},{7,15},{8,0},{9,1},... | collective-permute-start | bytes 196616 | tf_op jit(solution)/shard_map/ppermute | solution.py:194
  51.5 1.6 %collective-permute-start.19 = (f32[192,128]{1,0:T(8,128)S(1)}, f32[192,128]{1,0:T(8,128)S(1)}, u32[]{:S(2)}, u32[]{:S(2)}) collective-permute-start(f32[192,128]{1,0:T(8,128)S(1)} %pad_maximum_fusion.1), channel_id=1, source_target_pairs={{0,8},{1,9},{2,10},{3,11},{4,12},{5,13},{6,14},{7,15},{8,0},{9,1},... | collective-permute-start | bytes 294920 | tf_op jit(solution)/shard_map/ppermute | solution.py:194
  53.2 1.3 %product.2 = (f32[128,128]{1,0:T(8,128)S(1)}, f32[128,128]{1,0:T(8,128)S(1)}) custom-call(s32[9]{0:T(128)S(1)} %convert_reduce_fusion.edge_ref, f32[8]{0:T(128)S(1)} %convert_divide_fusion.scale_ref, f32[128,128]{1,0:T(8,128)S(1)} %fusion.2.refs_0_, f32[128,128]{1,0:T(8,128)S(1)} %fusion.1.refs_1_, f32[128,128]{1,0:T(8,128)S(1)} %fusion.refs_2_), custom_call_target="tpu_custom_call" | custom-call | tf_op jit(solution)/shard_map/product/pallas_call | solution.py:174
  54.6 2.7 %collective-permute-start.21 = (f32[64,128]{1,0:T(8,128)S(1)}, f32[64,128]{1,0:T(8,128)S(1)}, u32[]{:S(2)}, u32[]{:S(2)}) collective-permute-start(f32[64,128]{1,0:T(8,128)S(1)} %pad_maximum_fusion.2), channel_id=1, source_target_pairs={{0,8},{1,9},{2,10},{3,11},{4,12},{5,13},{6,14},{7,15},{8,0},{9,1},... | collective-permute-start | bytes 98312 | tf_op jit(solution)/shard_map/ppermute | solution.py:194
  57.2 1.2 %collective-permute-start.18 = (f32[128,128]{1,0:T(8,128)S(1)}, f32[128,128]{1,0:T(8,128)S(1)}, u32[]{:S(2)}, u32[]{:S(2)}) collective-permute-start(f32[128,128]{1,0:T(8,128)S(1)} %add.152), channel_id=1, source_target_pairs={{0,8},{1,9},{2,10},{3,11},{4,12},{5,13},{6,14},{7,15},{8,0},{9,1},... | collective-permute-start | bytes 196616 | tf_op jit(solution)/shard_map/ppermute | solution.py:194
  59.5 1.2 %product.3 = (f32[128,128]{1,0:T(8,128)S(1)}, f32[128,128]{1,0:T(8,128)S(1)}) custom-call(s32[9]{0:T(128)S(1)} %convert_reduce_fusion.edge_ref, f32[8]{0:T(128)S(1)} %convert_divide_fusion.scale_ref, f32[192,128]{1,0:T(8,128)S(1)} %maximum_add_fusion.refs_0_, f32[64,128]{1,0:T(8,128)S(1)} %maximum_add_fusion.1.refs_1_), custom_call_target="tpu_custom_call" | custom-call | tf_op jit(solution)/shard_map/product/pallas_call | solution.py:174
  60.7 3.2 %collective-permute-done.18 = f32[128,128]{1,0:T(8,128)S(1)} collective-permute-done((f32[128,128]{1,0:T(8,128)S(1)}, f32[128,128]{1,0:T(8,128)S(1)}, u32[]{:S(2)}, u32[]{:S(2)}) %collective-permute-start.18) | collective-permute-done | bytes 65568 | tf_op jit(solution)/shard_map/ppermute | solution.py:194
  63.9 1.6 %collective-permute-start.23 = (f32[128,128]{1,0:T(8,128)S(1)}, f32[128,128]{1,0:T(8,128)S(1)}, u32[]{:S(2)}, u32[]{:S(2)}) collective-permute-start(f32[128,128]{1,0:T(8,128)S(1)} %add_add_fusion), channel_id=1, source_target_pairs={{0,2},{1,3},{2,0},{3,1},{4,6},{5,7},{6,4},{7,5},{8,10},{9,11},{10,... | collective-permute-start | bytes 196616 | tf_op jit(solution)/shard_map/ppermute | solution.py:194
  65.5 2.7 %collective-permute-done.23 = f32[128,128]{1,0:T(8,128)S(1)} collective-permute-done((f32[128,128]{1,0:T(8,128)S(1)}, f32[128,128]{1,0:T(8,128)S(1)}, u32[]{:S(2)}, u32[]{:S(2)}) %collective-permute-start.23) | collective-permute-done | bytes 65568 | tf_op jit(solution)/shard_map/ppermute | solution.py:194
  69.1 3.5 %collective-permute-done.24 = f32[128,128]{1,0:T(8,128)S(1)} collective-permute-done((f32[128,128]{1,0:T(8,128)S(1)}, f32[128,128]{1,0:T(8,128)S(1)}, u32[]{:S(2)}, u32[]{:S(2)}) %collective-permute-start.24) | collective-permute-done | bytes 65568 | tf_op jit(solution)/shard_map/ppermute | solution.py:194
  72.7 1.2 %collective-permute-done.25 = f32[128,128]{1,0:T(8,128)S(1)} collective-permute-done((f32[128,128]{1,0:T(8,128)S(1)}, f32[128,128]{1,0:T(8,128)S(1)}, u32[]{:S(2)}, u32[]{:S(2)}) %collective-permute-start.25) | collective-permute-done | bytes 65568 | tf_op jit(solution)/shard_map/ppermute | solution.py:194
  (72 shorter events, 10.6 us)
Async XLA Ops:
  18.1 4.6 %collective-permute-start.5 = (f32[1024,128]{1,0:T(8,128)S(1)}, f32[1024,128]{1,0:T(8,128)S(1)}, u32[]{:S(2)}, u32[]{:S(2)}) collective-permute-start(f32[1024,128]{1,0:T(8,128)S(1)} %get-tuple-element.47), channel_id=1, source_target_pairs={{0,1},{1,0},{2,3},{3,2},{4,5},{5,4},{6,7},{7,6},{8,9},{9,8},{10,11... | collective-permute-start | bytes 1572872 | tf_op jit(solution)/shard_map/ppermute | solution.py:194
  18.2 5.2 %collective-permute-start.4 = (f32[1024,128]{1,0:T(8,128)S(1)}, f32[1024,128]{1,0:T(8,128)S(1)}, u32[]{:S(2)}, u32[]{:S(2)}) collective-permute-start(f32[1024,128]{1,0:T(8,128)S(1)} %get-tuple-element.45), channel_id=1, source_target_pairs={{0,1},{1,0},{2,3},{3,2},{4,5},{5,4},{6,7},{7,6},{8,9},{9,8},{10,11... | collective-permute-start | bytes 1572872 | tf_op jit(solution)/shard_map/ppermute | solution.py:194
  18.6 6.3 %collective-permute-start.3 = (f32[768,128]{1,0:T(8,128)S(1)}, f32[768,128]{1,0:T(8,128)S(1)}, u32[]{:S(2)}, u32[]{:S(2)}) collective-permute-start(f32[768,128]{1,0:T(8,128)S(1)} %get-tuple-element.43), channel_id=1, source_target_pairs={{0,1},{1,0},{2,3},{3,2},{4,5},{5,4},{6,7},{7,6},{8,9},{9,8},{10,11... | collective-permute-start | bytes 1179656 | tf_op jit(solution)/shard_map/ppermute | solution.py:194
  18.7 7.0 %collective-permute-start.2 = (f32[256,128]{1,0:T(8,128)S(1)}, f32[256,128]{1,0:T(8,128)S(1)}, u32[]{:S(2)}, u32[]{:S(2)}) collective-permute-start(f32[256,128]{1,0:T(8,128)S(1)} %get-tuple-element.41), channel_id=1, source_target_pairs={{0,1},{1,0},{2,3},{3,2},{4,5},{5,4},{6,7},{7,6},{8,9},{9,8},{10,11... | collective-permute-start | bytes 393224 | tf_op jit(solution)/shard_map/ppermute | solution.py:194
  19.7 10.0 %collective-permute-start.1 = (f32[512,128]{1,0:T(8,128)S(1)}, f32[512,128]{1,0:T(8,128)S(1)}, u32[]{:S(2)}, u32[]{:S(2)}) collective-permute-start(f32[512,128]{1,0:T(8,128)S(1)} %get-tuple-element.76), channel_id=1, source_target_pairs={{0,2},{1,3},{2,0},{3,1},{4,6},{5,7},{6,4},{7,5},{8,10},{9,11},{10,... | collective-permute-start | bytes 786440 | tf_op jit(solution)/shard_map/ppermute | solution.py:194
  22.7 12.6 %collective-permute-start.7 = (f32[512,128]{1,0:T(8,128)S(1)}, f32[512,128]{1,0:T(8,128)S(1)}, u32[]{:S(2)}, u32[]{:S(2)}) collective-permute-start(f32[512,128]{1,0:T(8,128)S(1)} %get-tuple-element.74), channel_id=1, source_target_pairs={{0,2},{1,3},{2,0},{3,1},{4,6},{5,7},{6,4},{7,5},{8,10},{9,11},{10,... | collective-permute-start | bytes 786440 | tf_op jit(solution)/shard_map/ppermute | solution.py:194
  23.5 17.5 %collective-permute-start.10 = (f32[512,128]{1,0:T(8,128)S(1)}, f32[512,128]{1,0:T(8,128)S(1)}, u32[]{:S(2)}, u32[]{:S(2)}) collective-permute-start(f32[512,128]{1,0:T(8,128)S(1)} %get-tuple-element.72), channel_id=1, source_target_pairs={{0,2},{1,3},{2,0},{3,1},{4,6},{5,7},{6,4},{7,5},{8,10},{9,11},{10,... | collective-permute-start | bytes 786440 | tf_op jit(solution)/shard_map/ppermute | solution.py:194
  25.0 20.9 %collective-permute-start.13 = (f32[384,128]{1,0:T(8,128)S(1)}, f32[384,128]{1,0:T(8,128)S(1)}, u32[]{:S(2)}, u32[]{:S(2)}) collective-permute-start(f32[384,128]{1,0:T(8,128)S(1)} %get-tuple-element.77), channel_id=1, source_target_pairs={{0,2},{1,3},{2,0},{3,1},{4,6},{5,7},{6,4},{7,5},{8,10},{9,11},{10,... | collective-permute-start | bytes 589832 | tf_op jit(solution)/shard_map/ppermute | solution.py:194
  25.7 24.3 %collective-permute-start.16 = (f32[128,128]{1,0:T(8,128)S(1)}, f32[128,128]{1,0:T(8,128)S(1)}, u32[]{:S(2)}, u32[]{:S(2)}) collective-permute-start(f32[128,128]{1,0:T(8,128)S(1)} %get-tuple-element.88), channel_id=1, source_target_pairs={{0,2},{1,3},{2,0},{3,1},{4,6},{5,7},{6,4},{7,5},{8,10},{9,11},{10,... | collective-permute-start | bytes 196616 | tf_op jit(solution)/shard_map/ppermute | solution.py:194
  29.8 7.8 %collective-permute-start.6 = (f32[256,128]{1,0:T(8,128)S(1)}, f32[256,128]{1,0:T(8,128)S(1)}, u32[]{:S(2)}, u32[]{:S(2)}) collective-permute-start(f32[256,128]{1,0:T(8,128)S(1)} %get-tuple-element.83), channel_id=1, source_target_pairs={{0,4},{1,5},{2,6},{3,7},{4,0},{5,1},{6,2},{7,3},{8,12},{9,13},{10,... | collective-permute-start | bytes 393224 | tf_op jit(solution)/shard_map/ppermute | solution.py:194
  35.4 7.8 %collective-permute-start.9 = (f32[256,128]{1,0:T(8,128)S(1)}, f32[256,128]{1,0:T(8,128)S(1)}, u32[]{:S(2)}, u32[]{:S(2)}) collective-permute-start(f32[256,128]{1,0:T(8,128)S(1)} %get-tuple-element.82), channel_id=1, source_target_pairs={{0,4},{1,5},{2,6},{3,7},{4,0},{5,1},{6,2},{7,3},{8,12},{9,13},{10,... | collective-permute-start | bytes 393224 | tf_op jit(solution)/shard_map/ppermute | solution.py:194
  37.6 8.3 %collective-permute-start.8 = (f32[128,128]{1,0:T(8,128)S(1)}, f32[128,128]{1,0:T(8,128)S(1)}, u32[]{:S(2)}, u32[]{:S(2)}) collective-permute-start(f32[128,128]{1,0:T(8,128)S(1)} %slice_add_fusion.20), channel_id=1, source_target_pairs={{0,8},{1,9},{2,10},{3,11},{4,12},{5,13},{6,14},{7,15},{8,0},{9,1},... | collective-permute-start | bytes 196616 | tf_op jit(solution)/shard_map/ppermute | solution.py:194
  41.0 6.3 %collective-permute-start.12 = (f32[256,128]{1,0:T(8,128)S(1)}, f32[256,128]{1,0:T(8,128)S(1)}, u32[]{:S(2)}, u32[]{:S(2)}) collective-permute-start(f32[256,128]{1,0:T(8,128)S(1)} %get-tuple-element.80), channel_id=1, source_target_pairs={{0,4},{1,5},{2,6},{3,7},{4,0},{5,1},{6,2},{7,3},{8,12},{9,13},{10,... | collective-permute-start | bytes 393224 | tf_op jit(solution)/shard_map/ppermute | solution.py:194
  43.2 6.8 %collective-permute-start.11 = (f32[128,128]{1,0:T(8,128)S(1)}, f32[128,128]{1,0:T(8,128)S(1)}, u32[]{:S(2)}, u32[]{:S(2)}) collective-permute-start(f32[128,128]{1,0:T(8,128)S(1)} %slice_add_fusion.19), channel_id=1, source_target_pairs={{0,8},{1,9},{2,10},{3,11},{4,12},{5,13},{6,14},{7,15},{8,0},{9,1},... | collective-permute-start | bytes 196616 | tf_op jit(solution)/shard_map/ppermute | solution.py:194
  45.9 5.6 %collective-permute-start.15 = (f32[192,128]{1,0:T(8,128)S(1)}, f32[192,128]{1,0:T(8,128)S(1)}, u32[]{:S(2)}, u32[]{:S(2)}) collective-permute-start(f32[192,128]{1,0:T(8,128)S(1)} %get-tuple-element.85), channel_id=1, source_target_pairs={{0,4},{1,5},{2,6},{3,7},{4,0},{5,1},{6,2},{7,3},{8,12},{9,13},{10,... | collective-permute-start | bytes 294920 | tf_op jit(solution)/shard_map/ppermute | solution.py:194
  47.3 5.8 %collective-permute-start.14 = (f32[128,128]{1,0:T(8,128)S(1)}, f32[128,128]{1,0:T(8,128)S(1)}, u32[]{:S(2)}, u32[]{:S(2)}) collective-permute-start(f32[128,128]{1,0:T(8,128)S(1)} %slice_add_fusion.17), channel_id=1, source_target_pairs={{0,8},{1,9},{2,10},{3,11},{4,12},{5,13},{6,14},{7,15},{8,0},{9,1},... | collective-permute-start | bytes 196616 | tf_op jit(solution)/shard_map/ppermute | solution.py:194
  50.0 4.5 %collective-permute-start.20 = (f32[64,128]{1,0:T(8,128)S(1)}, f32[64,128]{1,0:T(8,128)S(1)}, u32[]{:S(2)}, u32[]{:S(2)}) collective-permute-start(f32[64,128]{1,0:T(8,128)S(1)} %get-tuple-element.92), channel_id=1, source_target_pairs={{0,4},{1,5},{2,6},{3,7},{4,0},{5,1},{6,2},{7,3},{8,12},{9,13},{10,... | collective-permute-start | bytes 98312 | tf_op jit(solution)/shard_map/ppermute | solution.py:194
  51.5 6.9 %collective-permute-start.19 = (f32[192,128]{1,0:T(8,128)S(1)}, f32[192,128]{1,0:T(8,128)S(1)}, u32[]{:S(2)}, u32[]{:S(2)}) collective-permute-start(f32[192,128]{1,0:T(8,128)S(1)} %pad_maximum_fusion.1), channel_id=1, source_target_pairs={{0,8},{1,9},{2,10},{3,11},{4,12},{5,13},{6,14},{7,15},{8,0},{9,1},... | collective-permute-start | bytes 294920 | tf_op jit(solution)/shard_map/ppermute | solution.py:194
  54.5 2.8 %collective-permute-start.17 = (f32[128,128]{1,0:T(8,128)S(1)}, f32[128,128]{1,0:T(8,128)S(1)}, u32[]{:S(2)}, u32[]{:S(2)}) collective-permute-start(f32[128,128]{1,0:T(8,128)S(1)} %get-tuple-element.65), channel_id=1, source_target_pairs={{0,1},{1,0},{2,3},{3,2},{4,5},{5,4},{6,7},{7,6},{8,9},{9,8},{10,11... | collective-permute-start | bytes 196616 | tf_op jit(solution)/shard_map/ppermute | solution.py:194
  54.6 4.9 %collective-permute-start.21 = (f32[64,128]{1,0:T(8,128)S(1)}, f32[64,128]{1,0:T(8,128)S(1)}, u32[]{:S(2)}, u32[]{:S(2)}) collective-permute-start(f32[64,128]{1,0:T(8,128)S(1)} %pad_maximum_fusion.2), channel_id=1, source_target_pairs={{0,8},{1,9},{2,10},{3,11},{4,12},{5,13},{6,14},{7,15},{8,0},{9,1},... | collective-permute-start | bytes 98312 | tf_op jit(solution)/shard_map/ppermute | solution.py:194
  57.2 6.6 %collective-permute-start.18 = (f32[128,128]{1,0:T(8,128)S(1)}, f32[128,128]{1,0:T(8,128)S(1)}, u32[]{:S(2)}, u32[]{:S(2)}) collective-permute-start(f32[128,128]{1,0:T(8,128)S(1)} %add.152), channel_id=1, source_target_pairs={{0,8},{1,9},{2,10},{3,11},{4,12},{5,13},{6,14},{7,15},{8,0},{9,1},... | collective-permute-start | bytes 196616 | tf_op jit(solution)/shard_map/ppermute | solution.py:194
  60.6 3.3 %collective-permute-start.22 = (f32[128,128]{1,0:T(8,128)S(1)}, f32[128,128]{1,0:T(8,128)S(1)}, u32[]{:S(2)}, u32[]{:S(2)}) collective-permute-start(f32[128,128]{1,0:T(8,128)S(1)} %get-tuple-element.70), channel_id=1, source_target_pairs={{0,1},{1,0},{2,3},{3,2},{4,5},{5,4},{6,7},{7,6},{8,9},{9,8},{10,11... | collective-permute-start | bytes 196616 | tf_op jit(solution)/shard_map/ppermute | solution.py:194
  63.9 4.3 %collective-permute-start.23 = (f32[128,128]{1,0:T(8,128)S(1)}, f32[128,128]{1,0:T(8,128)S(1)}, u32[]{:S(2)}, u32[]{:S(2)}) collective-permute-start(f32[128,128]{1,0:T(8,128)S(1)} %add_add_fusion), channel_id=1, source_target_pairs={{0,2},{1,3},{2,0},{3,1},{4,6},{5,7},{6,4},{7,5},{8,10},{9,11},{10,... | collective-permute-start | bytes 196616 | tf_op jit(solution)/shard_map/ppermute | solution.py:194
  68.3 4.3 %collective-permute-start.24 = (f32[128,128]{1,0:T(8,128)S(1)}, f32[128,128]{1,0:T(8,128)S(1)}, u32[]{:S(2)}, u32[]{:S(2)}) collective-permute-start(f32[128,128]{1,0:T(8,128)S(1)} %add.162), channel_id=1, source_target_pairs={{0,4},{1,5},{2,6},{3,7},{4,0},{5,1},{6,2},{7,3},{8,12},{9,13},{10,... | collective-permute-start | bytes 196616 | tf_op jit(solution)/shard_map/ppermute | solution.py:194
  (6 other events, 96.5 us)

commit v4 on v3

--- a/solution.py
+++ b/solution.py
@@ -9,27 +9,29 @@
 
 SEQS = 8
 UNITS = 16
-CHUNKS = (4, 4, 4, 3, 1)
-BOTH_SIDES = 2
-BLOCK = 512
+CHUNKS = (4, 4, 4, 4)
+BOTH_SIDES = 0
+RING = 4
+COST = 1
+EARLY = 0
+PAIR = 2
+JOIN = 1
+CROSSED = (1, 3)
+CUT = 4
 VMEM = 48 * 1024 * 1024
 ROWS_BY_ROWS = (((1,), (1,)), ((), ()))
 
 
-def project_kernel(bits, block_bits, shares, a_hbm, g_hbm, pi_hbm, po_hbm, *refs):
+def project_kernel(bits, own, first, shares, a_hbm, g_hbm, pi_hbm, po_hbm, *refs):
     outs, (pi_ref, po_ref, a_buf, g_buf, sems) = refs[:-5], refs[-5:]
     ring, size = a_buf.shape[0], a_buf.shape[1]
-    blocks = 1 << block_bits
-    count = 1 << (bits - block_bits)
-    own = size // count
+    blocks = 1 << bits
     half = blocks // 2
     me_rev = reversed_index(bits)
-    high = me_rev >> (bits - block_bits)
-    low = me_rev & (count - 1)
 
     def copies(step):
         slot = lax.rem(step, ring)
-        start = pl.multiple_of((step ^ high) * size, size)
+        start = pl.multiple_of((step ^ me_rev) * own + first, 16)
         return (
             pltpu.make_async_copy(a_hbm.at[pl.ds(start, size), :], a_buf.at[slot], sems.at[slot, 0]),
             pltpu.make_async_copy(g_hbm.at[pl.ds(start, size), :], g_buf.at[slot], sems.at[slot, 1]),
@@ -41,7 +43,7 @@
     )
     for copy in weights:
         copy.start()
-    for step in range(min(ring - 1, blocks)):
+    for step in range(ring - 1):
         for copy in copies(jnp.int32(step)):
             copy.start()
     for copy in weights:
@@ -59,16 +61,14 @@
         side_x = lax.dot_general(a_buf[slot], pi_ref[...], ROWS_BY_ROWS, preferred_element_type=jnp.float32)
         side_g = lax.dot_general(g_buf[slot], po_ref[...], ROWS_BY_ROWS, preferred_element_type=jnp.float32)
         both = jnp.concatenate([side_x, side_g], axis=1)
-        base = (step & (half - 1)) * count
+        place = step & (half - 1)
 
         def store(out_refs):
-            for part in range(count):
-                place = base + (part ^ low)
-                row = part * own
-                for share, out_ref in zip(shares, out_refs, strict=True):
-                    start = pl.multiple_of(place * share, 8)
-                    out_ref[pl.ds(start, share), :] = both[row : row + share]
-                    row += share
+            row = 0
+            for share, out_ref in zip(shares, out_refs, strict=True):
+                start = pl.multiple_of(place * share, 8)
+                out_ref[pl.ds(start, share), :] = both[row : row + share]
+                row += share
 
         @pl.when(step < half)
         def _():
@@ -91,13 +91,12 @@
     return flipped
 
 
-def project(bits, shares, activations, out_grads, proj_in, proj_out):
+def project(bits, first, shares, activations, out_grads, proj_in, proj_out):
     tokens, width = activations.shape
     hidden = out_grads.shape[1]
     rank = proj_in.shape[0]
-    block_bits = min(bits, max(2, (tokens // BLOCK - 1).bit_length()))
-    size = tokens >> block_bits
-    ring = 4
+    size = sum(shares)
+    ring = min(RING, 1 << bits)
     outs = [
         jax.ShapeDtypeStruct(((1 << bits) // 2 * share, 2 * rank), jnp.float32)
         for share in shares
@@ -105,7 +104,7 @@
     ]
     vmem = pl.BlockSpec(memory_space=pltpu.VMEM)
     return pl.pallas_call(
-        functools.partial(project_kernel, bits, block_bits, shares),
+        functools.partial(project_kernel, bits, tokens >> bits, first, shares),
         in_specs=[pl.BlockSpec(memory_space=pl.ANY)] * 4,
         out_specs=[vmem] * len(outs),
         out_shape=outs,
@@ -117,6 +116,7 @@
             pltpu.SemaphoreType.DMA((ring + 1, 2)),
         ],
         compiler_params=pltpu.CompilerParams(vmem_limit_bytes=VMEM),
+        cost_estimate=pl.CostEstimate(flops=COST, bytes_accessed=COST, transcendentals=0),
         name="project",
     )(activations, out_grads, proj_in, proj_out)
 
@@ -200,16 +200,47 @@
 
     shares = tuple(own * share // UNITS for share in CHUNKS)
     chunks = len(shares)
-    halves = project(bits, shares, activations, out_grads, proj_in.T, proj_out.T)
-    sends, keeps = list(halves[0::2]), list(halves[1::2])
     on_both = [k >= chunks - BOTH_SIDES for k in range(chunks)]
+    weights = (proj_in.T, proj_out.T)
+    halves = list(project(bits, 0, shares[:CUT], activations, out_grads, *weights))
+    sends, keeps = halves[0::2], halves[1::2]
+
+    def route(k):
+        return [0, 2, 1, *range(3, bits)] if k in CROSSED else list(range(bits))
+
+    def turn(k, stage):
+        if stage == 0:
+            return 0.0 if k < CUT else 0.5
+        return 0.4 if stage == 1 and k < EARLY else float(k // PAIR + stage)
+
+    def split(value, left, b):
+        shape = (1 << left.index(b), 2, -1, value.shape[1])
+        parts = value.reshape(shape)
+        return parts[:, 1].reshape(-1, value.shape[1]), parts[:, 0].reshape(-1, value.shape[1])
+
     moves = sorted(
-        ((k, b) for k in range(chunks) for b in range(bits)),
-        key=lambda move: (0 if move[1] == 0 else move[0] + move[1], move[1], move[0]),
-    )
+        ((k, stage) for k in range(chunks) for stage in range(bits)),
+        key=lambda move: (turn(*move), move[1], move[0]),
+    )
+    remaining = [list(range(1, bits)) for _ in range(chunks)]
     latest = None
-    for k, b in moves:
+    for k, stage in moves:
+        b = route(k)[stage]
+        if len(sends) < chunks and stage == 1:
+            weights, _ = lax.optimization_barrier((weights, sends))
+            halves = list(project(bits, sum(shares[:CUT]), shares[CUT:], activations, out_grads, *weights))
+            sends, keeps = sends + halves[0::2], keeps + halves[1::2]
         send, keep = sends[k], keeps[k]
+        if b == last and not BOTH_SIDES:
+            joined = [j for j in range(chunks) if j // JOIN == k // JOIN]
+            if k == joined[-1]:
+                send = jnp.concatenate([sends[j] for j in joined], axis=0)
+                received, _ = lax.optimization_barrier((swap(send, b), latest))
+                row = 0
+                for j in joined:
+                    keeps[j] = latest = keeps[j] + received[row : row + sends[j].shape[0]]
+                    row += sends[j].shape[0]
+            continue
         both = b == last and on_both[k]
         received = swap(jnp.concatenate([send, keep], axis=0) if both else send, b)
         if latest is not None:
@@ -219,9 +250,11 @@
         elif b == last:
             keeps[k] = latest = keep + received
         else:
-            half = keep.shape[0] // 2
-            sends[k] = latest = keep[half:] + received[half:]
-            keeps[k] = keep[:half] + received[:half]
+            following = route(k)[stage + 1]
+            old, new = split(keep, remaining[k], following), split(received, remaining[k], following)
+            remaining[k].remove(following)
+            sends[k] = latest = old[0] + new[0]
+            keeps[k] = old[1] + new[1]
     pieces = [(sum(shares[:k]), shares[k], 2 if on_both[k] else 1) for k in range(chunks)]
     early = [(keeps[k], pieces[k]) for k in range(chunks) if not on_both[k]]
     late = [(keeps[k], pieces[k]) for k in range(chunks) if on_both[k]]
@@ -229,19 +262,21 @@
     def group_product(group):
         return product(tuple(p for _, p in group), bits, own, edges, scale, [t for t, _ in group])
 
-    send, keep = group_product(early)
+    send, keep = group_product(early or late)
     grads = keep + swap(send, 0)
-    grads = grads + swap(grads, last)
-    send, keep = group_product(late)
-    grads = grads + keep + swap(send, 0)
-    for b in range(1, last):
+    hops = range(1, last if late else bits)
+    if early and late:
+        grads = grads + swap(grads, last)
+        send, keep = group_product(late)
+        grads = grads + keep + swap(send, 0)
+    for b in hops:
         grads = grads + swap(grads, b)
-    pair = jnp.concatenate([grads, swap(grads, 0)], axis=0).reshape(SEQS, rank * rank)
-    scores = jnp.dot(
-        pair, queries.T, precision=lax.Precision.HIGHEST, preferred_element_type=jnp.float32
-    )
-    turned = jnp.concatenate([scores[SEQS // 2 :], scores[: SEQS // 2]], axis=0)
-    return jnp.where((me & 1) == 0, scores, turned)
+    other = swap(grads, 0)
+    even = (me & 1) == 0
+    pair = jnp.concatenate([jnp.where(even, grads, other), jnp.where(even, other, grads)], axis=0)
+    return jnp.dot(
+        pair.reshape(SEQS, rank * rank), queries.T, precision=lax.Precision.HIGHEST, preferred_element_type=jnp.float32
+    )
 
 
 def solution(mesh):

time: 75.7 us -> 74.1 us (0.979)
  starting transfers between devices: 33.7 us -> 23.3 us
  waiting for transfers between devices: 19.2 us -> 29.2 us
  Pallas kernels: 18.2 us -> 17.1 us
    ppermute x26 -> x21, starting transfers between devices: 33.7 us -> 23.3 us  [swap(): lax.ppermute(value, 'tp', [(i, i ^ 1 << bit) for i in range(devices)])]
    ppermute x26 -> x21, waiting for transfers between devices: 19.2 us -> 29.2 us  [swap(): lax.ppermute(value, 'tp', [(i, i ^ 1 << bit) for i in range(devices)])]
    pallas_call x2 -> x1, Pallas kernels: 2.47 us -> 1.37 us  [product(): pl.pallas_call(functools.partial(product_kernel, pieces, bits, own), in_s...]
  transfers between devices with their start and end apart: 26 -> 21, of which waited for: 10 -> 13; matrix products, arithmetic and copies ran while one was open for 1% -> 1% of each run, Pallas kernels for 3% -> 0%
where the time goes in v4:
time: 74.1 us; the launch traced here: 74 us
  waiting for transfers between devices  29.2 us (39%)
  starting transfers between devices  23.3 us (31%)
  Pallas kernels  17.1 us (23%)
  local copies, waits for them, and re-layouts  1.9 us (3%)
  matrix products  1.52 us (2%)
  other arithmetic  0.75 us (1%)
    ppermute x21, waiting for transfers between devices, swap(): lax.ppermute(value, 'tp', [(i, i ^ 1 << bit) for i in range(devices)])  29.2 us
    ppermute x21, starting transfers between devices, swap(): lax.ppermute(value, 'tp', [(i, i ^ 1 << bit) for i in range(devices)])  23.3 us
    pallas_call x1, Pallas kernels, project(): pl.pallas_call(functools.partial(project_kernel, bits, tokens >> bits, fi...  15.7 us
    unnamed x8, local copies, waits for them, and re-layouts  1.87 us
    dot_general x1, matrix products, shards(): jnp.dot(pair.reshape(SEQS, rank * rank), queries.T, precision=lax.Precisi...  1.52 us
  transfers between devices with their start and end apart: 21, of which 13 were waited for; matrix products, arithmetic and copies ran while one was open for 1% of the time, Pallas kernels for 0%

profile of v4, /device:TPU:0, one launch (start us, length us, event | category | flops | bytes accessed | tf_op | source)
XLA Modules:
  0.0 74.0 jit_solution(9812309797070676980)
XLA Ops:
  0.0 1.0 %copy-done.1 = bf16[1792,64]{0,1:T(8,128)(2,1)S(1)} copy-done((bf16[1792,64]{0,1:T(8,128)(2,1)S(1)}, bf16[1792,64]{0,1:T(8,128)(2,1)}, u32[]{:S(2)}) %copy-start.1) | copy-done | bytes 229400
  1.9 15.7 %project.1 = (f32[1024,128]{1,0:T(8,128)S(1)}, f32[1024,128]{1,0:T(8,128)S(1)}, f32[1024,128]{1,0:T(8,128)S(1)}, f32[1024,128]{1,0:T(8,128)S(1)}, f32[1024,128]{...) custom-call(bf16[8192,512]{1,0:T(8,128)(2,1)} %a_hbm.1, ...), custom_call_target="tpu_custom_call" | custom-call | flops 1 | bytes 1 | tf_op jit(solution)/shard_map/project/pallas_call | solution.py:106
  19.7 3.0 %collective-permute-start.1 = (f32[512,128]{1,0:T(8,128)S(1)}, f32[512,128]{1,0:T(8,128)S(1)}, u32[]{:S(2)}, u32[]{:S(2)}) collective-permute-start(f32[512,128]{1,0:T(8,128)S(1)} %get-tuple-element.58), channel_id=1, source_target_pairs={{0,2},{1,3},{2,0},{3,1},{4,6},{5,7},{6,4},{7,5},{8,10},{9,11},{10,... | collective-permute-start | bytes 786440 | tf_op jit(solution)/shard_map/ppermute | solution.py:194
  22.7 1.6 %collective-permute-start.8 = (f32[512,128]{1,0:T(8,128)S(1)}, f32[512,128]{1,0:T(8,128)S(1)}, u32[]{:S(2)}, u32[]{:S(2)}) collective-permute-start(f32[512,128]{1,0:T(8,128)S(1)} %bitcast.117), channel_id=1, source_target_pairs={{0,4},{1,5},{2,6},{3,7},{4,0},{5,1},{6,2},{7,3},{8,12},{9,13},{10,... | collective-permute-start | bytes 786440 | tf_op jit(solution)/shard_map/ppermute | solution.py:194
  25.9 3.8 %collective-permute-done.1 = f32[512,128]{1,0:T(8,128)S(1)} collective-permute-done((f32[512,128]{1,0:T(8,128)S(1)}, f32[512,128]{1,0:T(8,128)S(1)}, u32[]{:S(2)}, u32[]{:S(2)}) %collective-permute-start.1) | collective-permute-done | bytes 262176 | tf_op jit(solution)/shard_map/ppermute | solution.py:194
  29.8 2.2 %collective-permute-start.5 = (f32[256,128]{1,0:T(8,128)S(1)}, f32[256,128]{1,0:T(8,128)S(1)}, u32[]{:S(2)}, u32[]{:S(2)}) collective-permute-start(f32[256,128]{1,0:T(8,128)S(1)} %get-tuple-element.66), channel_id=1, source_target_pairs={{0,4},{1,5},{2,6},{3,7},{4,0},{5,1},{6,2},{7,3},{8,12},{9,13},{10,... | collective-permute-start | bytes 393224 | tf_op jit(solution)/shard_map/ppermute | solution.py:194
  32.0 1.6 %collective-permute-start.12 = (f32[256,128]{1,0:T(8,128)S(1)}, f32[256,128]{1,0:T(8,128)S(1)}, u32[]{:S(2)}, u32[]{:S(2)}) collective-permute-start(f32[256,128]{1,0:T(8,128)S(1)} %get-tuple-element.64), channel_id=1, source_target_pairs={{0,2},{1,3},{2,0},{3,1},{4,6},{5,7},{6,4},{7,5},{8,10},{9,11},{10,... | collective-permute-start | bytes 393224 | tf_op jit(solution)/shard_map/ppermute | solution.py:194
  33.6 1.8 %collective-permute-done.7 = f32[512,128]{1,0:T(8,128)S(1)} collective-permute-done((f32[512,128]{1,0:T(8,128)S(1)}, f32[512,128]{1,0:T(8,128)S(1)}, u32[]{:S(2)}, u32[]{:S(2)}) %collective-permute-start.7) | collective-permute-done | bytes 262176 | tf_op jit(solution)/shard_map/ppermute | solution.py:194
  35.4 2.2 %collective-permute-start.11 = (f32[256,128]{1,0:T(8,128)S(1)}, f32[256,128]{1,0:T(8,128)S(1)}, u32[]{:S(2)}, u32[]{:S(2)}) collective-permute-start(f32[256,128]{1,0:T(8,128)S(1)} %get-tuple-element.62), channel_id=1, source_target_pairs={{0,4},{1,5},{2,6},{3,7},{4,0},{5,1},{6,2},{7,3},{8,12},{9,13},{10,... | collective-permute-start | bytes 393224 | tf_op jit(solution)/shard_map/ppermute | solution.py:194
  37.6 1.6 %collective-permute-start.10 = (f32[256,128]{1,0:T(8,128)S(1)}, f32[256,128]{1,0:T(8,128)S(1)}, u32[]{:S(2)}, u32[]{:S(2)}) collective-permute-start(f32[256,128]{1,0:T(8,128)S(1)} %get-tuple-element.60), channel_id=1, source_target_pairs={{0,2},{1,3},{2,0},{3,1},{4,6},{5,7},{6,4},{7,5},{8,10},{9,11},{10,... | collective-permute-start | bytes 393224 | tf_op jit(solution)/shard_map/ppermute | solution.py:194
  39.2 1.2 %collective-permute-done.5 = f32[256,128]{1,0:T(8,128)S(1)} collective-permute-done((f32[256,128]{1,0:T(8,128)S(1)}, f32[256,128]{1,0:T(8,128)S(1)}, u32[]{:S(2)}, u32[]{:S(2)}) %collective-permute-start.5) | collective-permute-done | bytes 131104 | tf_op jit(solution)/shard_map/ppermute | solution.py:194
  40.4 2.6 %collective-permute-start.9 = (f32[128,128]{1,0:T(8,128)S(1)}, f32[128,128]{1,0:T(8,128)S(1)}, u32[]{:S(2)}, u32[]{:S(2)}) collective-permute-start(f32[128,128]{1,0:T(8,128)S(1)} %fusion.19), channel_id=1, source_target_pairs={{0,8},{1,9},{2,10},{3,11},{4,12},{5,13},{6,14},{7,15},{8,0},{9,1},... | collective-permute-start | bytes 196616 | tf_op jit(solution)/shard_map/ppermute | solution.py:194
  43.5 2.6 %collective-permute-start.14 = (f32[128,128]{1,0:T(8,128)S(1)}, f32[128,128]{1,0:T(8,128)S(1)}, u32[]{:S(2)}, u32[]{:S(2)}) collective-permute-start(f32[128,128]{1,0:T(8,128)S(1)} %fusion.17), channel_id=1, source_target_pairs={{0,8},{1,9},{2,10},{3,11},{4,12},{5,13},{6,14},{7,15},{8,0},{9,1},... | collective-permute-start | bytes 196616 | tf_op jit(solution)/shard_map/ppermute | solution.py:194
  46.6 3.9 %collective-permute-done.9 = f32[128,128]{1,0:T(8,128)S(1)} collective-permute-done((f32[128,128]{1,0:T(8,128)S(1)}, f32[128,128]{1,0:T(8,128)S(1)}, u32[]{:S(2)}, u32[]{:S(2)}) %collective-permute-start.9) | collective-permute-done | bytes 65568 | tf_op jit(solution)/shard_map/ppermute | solution.py:194
  50.5 2.1 %collective-permute-done.13 = f32[128,128]{1,0:T(8,128)S(1)} collective-permute-done((f32[128,128]{1,0:T(8,128)S(1)}, f32[128,128]{1,0:T(8,128)S(1)}, u32[]{:S(2)}, u32[]{:S(2)}) %collective-permute-start.13) | collective-permute-done | bytes 65568 | tf_op jit(solution)/shard_map/ppermute | solution.py:194
  54.1 1.4 %product.1 = (f32[128,128]{1,0:T(8,128)S(1)}, f32[128,128]{1,0:T(8,128)S(1)}) custom-call(s32[9]{0:T(128)S(1)} %convert_reduce_fusion.edge_ref, f32[8]{0:T(128)S(1)} %convert_divide_fusion.scale_ref, f32[128,128]{1,0:T(8,128)S(1)} %fusion.21.refs_0_, f32[128,128]{1,0:T(8,128)S(1)} %fusion.15.refs_1_, f32[128,128]{1,0:T(8,128)S(1)} %fusion.13.refs_2_, ...), custom_call_target="tpu_custom_call" | custom-call | tf_op jit(solution)/shard_map/product/pallas_call | solution.py:174
  55.6 1.2 %collective-permute-done.16 = f32[128,128]{1,0:T(8,128)S(1)} collective-permute-done((f32[128,128]{1,0:T(8,128)S(1)}, f32[128,128]{1,0:T(8,128)S(1)}, u32[]{:S(2)}, u32[]{:S(2)}) %collective-permute-start.16) | collective-permute-done | bytes 65568 | tf_op jit(solution)/shard_map/ppermute | solution.py:194
  56.8 1.2 %collective-permute-start.17 = (f32[128,128]{1,0:T(8,128)S(1)}, f32[128,128]{1,0:T(8,128)S(1)}, u32[]{:S(2)}, u32[]{:S(2)}) collective-permute-start(f32[128,128]{1,0:T(8,128)S(1)} %add.276), channel_id=1, source_target_pairs={{0,2},{1,3},{2,0},{3,1},{4,6},{5,7},{6,4},{7,5},{8,10},{9,11},{10,... | collective-permute-start | bytes 196616 | tf_op jit(solution)/shard_map/ppermute | solution.py:194
  58.0 3.1 %collective-permute-done.17 = f32[128,128]{1,0:T(8,128)S(1)} collective-permute-done((f32[128,128]{1,0:T(8,128)S(1)}, f32[128,128]{1,0:T(8,128)S(1)}, u32[]{:S(2)}, u32[]{:S(2)}) %collective-permute-start.17) | collective-permute-done | bytes 65568 | tf_op jit(solution)/shard_map/ppermute | solution.py:194
  61.2 4.3 %collective-permute-done.18 = f32[128,128]{1,0:T(8,128)S(1)} collective-permute-done((f32[128,128]{1,0:T(8,128)S(1)}, f32[128,128]{1,0:T(8,128)S(1)}, u32[]{:S(2)}, u32[]{:S(2)}) %collective-permute-start.18) | collective-permute-done | bytes 65568 | tf_op jit(solution)/shard_map/ppermute | solution.py:194
  65.5 1.1 %collective-permute-start.19 = (f32[128,128]{1,0:T(8,128)S(1)}, f32[128,128]{1,0:T(8,128)S(1)}, u32[]{:S(2)}, u32[]{:S(2)}) collective-permute-start(f32[128,128]{1,0:T(8,128)S(1)} %add.278), channel_id=1, source_target_pairs={{0,8},{1,9},{2,10},{3,11},{4,12},{5,13},{6,14},{7,15},{8,0},{9,1},... | collective-permute-start | bytes 196616 | tf_op jit(solution)/shard_map/ppermute | solution.py:194
  66.6 4.4 %collective-permute-done.19 = f32[128,128]{1,0:T(8,128)S(1)} collective-permute-done((f32[128,128]{1,0:T(8,128)S(1)}, f32[128,128]{1,0:T(8,128)S(1)}, u32[]{:S(2)}, u32[]{:S(2)}) %collective-permute-start.19) | collective-permute-done | bytes 65568 | tf_op jit(solution)/shard_map/ppermute | solution.py:194
  71.1 1.2 %collective-permute-done.20 = f32[128,128]{1,0:T(8,128)S(1)} collective-permute-done((f32[128,128]{1,0:T(8,128)S(1)}, f32[128,128]{1,0:T(8,128)S(1)}, u32[]{:S(2)}, u32[]{:S(2)}) %collective-permute-start.20) | collective-permute-done | bytes 65568 | tf_op jit(solution)/shard_map/ppermute | solution.py:194
  72.4 1.5 %fusion.22 = f32[8,64]{1,0:T(8,128)} fusion(f32[8,4096]{1,0:T(8,128)S(1)} %reshape.236, f32[64,4096]{1,0:T(8,128)S(1)} %copy-done), kind=kOutput, calls=%fused_computation.54 | convolution fusion | flops 25165824 | bytes 1181696 | tf_op jit(solution)/shard_map/dot_general | solution.py:277
  (56 shorter events, 7.4 us)
Async XLA Ops:
  0.0 72.4 %copy-start = (f32[64,4096]{1,0:T(8,128)S(1)}, f32[64,4096]{1,0:T(8,128)}, u32[]{:S(2)}) copy-start(f32[64,4096]{1,0:T(8,128)} %param.11) | copy-start | bytes 3145732
  0.0 1.0 %copy-start.1 = (bf16[1792,64]{0,1:T(8,128)(2,1)S(1)}, bf16[1792,64]{0,1:T(8,128)(2,1)}, u32[]{:S(2)}) copy-start(bf16[1792,64]{0,1:T(8,128)(2,1)} %param.9) | copy-start | bytes 688132
  1.9 16.8 %copy-start.3 = (s32[8192]{0:T(1024)S(1)}, s32[8192]{0:T(1024)}, u32[]{:S(2)}) copy-start(s32[8192]{0:T(1024)} %param.10) | copy-start | bytes 98308
  17.6 2.1 %collective-permute-start = (f32[1024,128]{1,0:T(8,128)S(1)}, f32[1024,128]{1,0:T(8,128)S(1)}, u32[]{:S(2)}, u32[]{:S(2)}) collective-permute-start(f32[1024,128]{1,0:T(8,128)S(1)} %get-tuple-element.31), channel_id=1, source_target_pairs={{0,1},{1,0},{2,3},{3,2},{4,5},{5,4},{6,7},{7,6},{8,9},{9,8},{10,11... | collective-permute-start | bytes 1572872 | tf_op jit(solution)/shard_map/ppermute | solution.py:194
  18.1 4.6 %collective-permute-start.4 = (f32[1024,128]{1,0:T(8,128)S(1)}, f32[1024,128]{1,0:T(8,128)S(1)}, u32[]{:S(2)}, u32[]{:S(2)}) collective-permute-start(f32[1024,128]{1,0:T(8,128)S(1)} %get-tuple-element.37), channel_id=1, source_target_pairs={{0,1},{1,0},{2,3},{3,2},{4,5},{5,4},{6,7},{7,6},{8,9},{9,8},{10,11... | collective-permute-start | bytes 1572872 | tf_op jit(solution)/shard_map/ppermute | solution.py:194
  18.2 6.1 %collective-permute-start.3 = (f32[1024,128]{1,0:T(8,128)S(1)}, f32[1024,128]{1,0:T(8,128)S(1)}, u32[]{:S(2)}, u32[]{:S(2)}) collective-permute-start(f32[1024,128]{1,0:T(8,128)S(1)} %get-tuple-element.35), channel_id=1, source_target_pairs={{0,1},{1,0},{2,3},{3,2},{4,5},{5,4},{6,7},{7,6},{8,9},{9,8},{10,11... | collective-permute-start | bytes 1572872 | tf_op jit(solution)/shard_map/ppermute | solution.py:194
  18.6 6.5 %collective-permute-start.2 = (f32[1024,128]{1,0:T(8,128)S(1)}, f32[1024,128]{1,0:T(8,128)S(1)}, u32[]{:S(2)}, u32[]{:S(2)}) collective-permute-start(f32[1024,128]{1,0:T(8,128)S(1)} %get-tuple-element.33), channel_id=1, source_target_pairs={{0,1},{1,0},{2,3},{3,2},{4,5},{5,4},{6,7},{7,6},{8,9},{9,8},{10,11... | collective-permute-start | bytes 1572872 | tf_op jit(solution)/shard_map/ppermute | solution.py:194
  19.7 10.0 %collective-permute-start.1 = (f32[512,128]{1,0:T(8,128)S(1)}, f32[512,128]{1,0:T(8,128)S(1)}, u32[]{:S(2)}, u32[]{:S(2)}) collective-permute-start(f32[512,128]{1,0:T(8,128)S(1)} %get-tuple-element.58), channel_id=1, source_target_pairs={{0,2},{1,3},{2,0},{3,1},{4,6},{5,7},{6,4},{7,5},{8,10},{9,11},{10,... | collective-permute-start | bytes 786440 | tf_op jit(solution)/shard_map/ppermute | solution.py:194
  22.7 9.3 %collective-permute-start.8 = (f32[512,128]{1,0:T(8,128)S(1)}, f32[512,128]{1,0:T(8,128)S(1)}, u32[]{:S(2)}, u32[]{:S(2)}) collective-permute-start(f32[512,128]{1,0:T(8,128)S(1)} %bitcast.117), channel_id=1, source_target_pairs={{0,4},{1,5},{2,6},{3,7},{4,0},{5,1},{6,2},{7,3},{8,12},{9,13},{10,... | collective-permute-start | bytes 786440 | tf_op jit(solution)/shard_map/ppermute | solution.py:194
  24.4 11.0 %collective-permute-start.7 = (f32[512,128]{1,0:T(8,128)S(1)}, f32[512,128]{1,0:T(8,128)S(1)}, u32[]{:S(2)}, u32[]{:S(2)}) collective-permute-start(f32[512,128]{1,0:T(8,128)S(1)} %get-tuple-element.56), channel_id=1, source_target_pairs={{0,2},{1,3},{2,0},{3,1},{4,6},{5,7},{6,4},{7,5},{8,10},{9,11},{10,... | collective-permute-start | bytes 786440 | tf_op jit(solution)/shard_map/ppermute | solution.py:194
  25.2 12.4 %collective-permute-start.6 = (f32[512,128]{1,0:T(8,128)S(1)}, f32[512,128]{1,0:T(8,128)S(1)}, u32[]{:S(2)}, u32[]{:S(2)}) collective-permute-start(f32[512,128]{1,0:T(8,128)S(1)} %bitcast.115), channel_id=1, source_target_pairs={{0,4},{1,5},{2,6},{3,7},{4,0},{5,1},{6,2},{7,3},{8,12},{9,13},{10,... | collective-permute-start | bytes 786440 | tf_op jit(solution)/shard_map/ppermute | solution.py:194
  29.8 10.6 %collective-permute-start.5 = (f32[256,128]{1,0:T(8,128)S(1)}, f32[256,128]{1,0:T(8,128)S(1)}, u32[]{:S(2)}, u32[]{:S(2)}) collective-permute-start(f32[256,128]{1,0:T(8,128)S(1)} %get-tuple-element.66), channel_id=1, source_target_pairs={{0,4},{1,5},{2,6},{3,7},{4,0},{5,1},{6,2},{7,3},{8,12},{9,13},{10,... | collective-permute-start | bytes 393224 | tf_op jit(solution)/shard_map/ppermute | solution.py:194
  32.0 11.1 %collective-permute-start.12 = (f32[256,128]{1,0:T(8,128)S(1)}, f32[256,128]{1,0:T(8,128)S(1)}, u32[]{:S(2)}, u32[]{:S(2)}) collective-permute-start(f32[256,128]{1,0:T(8,128)S(1)} %get-tuple-element.64), channel_id=1, source_target_pairs={{0,2},{1,3},{2,0},{3,1},{4,6},{5,7},{6,4},{7,5},{8,10},{9,11},{10,... | collective-permute-start | bytes 393224 | tf_op jit(solution)/shard_map/ppermute | solution.py:194
  35.4 8.1 %collective-permute-start.11 = (f32[256,128]{1,0:T(8,128)S(1)}, f32[256,128]{1,0:T(8,128)S(1)}, u32[]{:S(2)}, u32[]{:S(2)}) collective-permute-start(f32[256,128]{1,0:T(8,128)S(1)} %get-tuple-element.62), channel_id=1, source_target_pairs={{0,4},{1,5},{2,6},{3,7},{4,0},{5,1},{6,2},{7,3},{8,12},{9,13},{10,... | collective-permute-start | bytes 393224 | tf_op jit(solution)/shard_map/ppermute | solution.py:194
  37.6 8.5 %collective-permute-start.10 = (f32[256,128]{1,0:T(8,128)S(1)}, f32[256,128]{1,0:T(8,128)S(1)}, u32[]{:S(2)}, u32[]{:S(2)}) collective-permute-start(f32[256,128]{1,0:T(8,128)S(1)} %get-tuple-element.60), channel_id=1, source_target_pairs={{0,2},{1,3},{2,0},{3,1},{4,6},{5,7},{6,4},{7,5},{8,10},{9,11},{10,... | collective-permute-start | bytes 393224 | tf_op jit(solution)/shard_map/ppermute | solution.py:194
  40.4 10.1 %collective-permute-start.9 = (f32[128,128]{1,0:T(8,128)S(1)}, f32[128,128]{1,0:T(8,128)S(1)}, u32[]{:S(2)}, u32[]{:S(2)}) collective-permute-start(f32[128,128]{1,0:T(8,128)S(1)} %fusion.19), channel_id=1, source_target_pairs={{0,8},{1,9},{2,10},{3,11},{4,12},{5,13},{6,14},{7,15},{8,0},{9,1},... | collective-permute-start | bytes 196616 | tf_op jit(solution)/shard_map/ppermute | solution.py:194
  43.1 9.5 %collective-permute-start.13 = (f32[128,128]{1,0:T(8,128)S(1)}, f32[128,128]{1,0:T(8,128)S(1)}, u32[]{:S(2)}, u32[]{:S(2)}) collective-permute-start(f32[128,128]{1,0:T(8,128)S(1)} %fusion.18), channel_id=1, source_target_pairs={{0,8},{1,9},{2,10},{3,11},{4,12},{5,13},{6,14},{7,15},{8,0},{9,1},... | collective-permute-start | bytes 196616 | tf_op jit(solution)/shard_map/ppermute | solution.py:194
  43.5 9.9 %collective-permute-start.14 = (f32[128,128]{1,0:T(8,128)S(1)}, f32[128,128]{1,0:T(8,128)S(1)}, u32[]{:S(2)}, u32[]{:S(2)}) collective-permute-start(f32[128,128]{1,0:T(8,128)S(1)} %fusion.17), channel_id=1, source_target_pairs={{0,8},{1,9},{2,10},{3,11},{4,12},{5,13},{6,14},{7,15},{8,0},{9,1},... | collective-permute-start | bytes 196616 | tf_op jit(solution)/shard_map/ppermute | solution.py:194
  46.2 7.9 %collective-permute-start.15 = (f32[128,128]{1,0:T(8,128)S(1)}, f32[128,128]{1,0:T(8,128)S(1)}, u32[]{:S(2)}, u32[]{:S(2)}) collective-permute-start(f32[128,128]{1,0:T(8,128)S(1)} %fusion.16), channel_id=1, source_target_pairs={{0,8},{1,9},{2,10},{3,11},{4,12},{5,13},{6,14},{7,15},{8,0},{9,1},... | collective-permute-start | bytes 196616 | tf_op jit(solution)/shard_map/ppermute | solution.py:194
  55.5 1.3 %collective-permute-start.16 = (f32[128,128]{1,0:T(8,128)S(1)}, f32[128,128]{1,0:T(8,128)S(1)}, u32[]{:S(2)}, u32[]{:S(2)}) collective-permute-start(f32[128,128]{1,0:T(8,128)S(1)} %get-tuple-element.54), channel_id=1, source_target_pairs={{0,1},{1,0},{2,3},{3,2},{4,5},{5,4},{6,7},{7,6},{8,9},{9,8},{10,11... | collective-permute-start | bytes 196616 | tf_op jit(solution)/shard_map/ppermute | solution.py:194
  56.8 4.3 %collective-permute-start.17 = (f32[128,128]{1,0:T(8,128)S(1)}, f32[128,128]{1,0:T(8,128)S(1)}, u32[]{:S(2)}, u32[]{:S(2)}) collective-permute-start(f32[128,128]{1,0:T(8,128)S(1)} %add.276), channel_id=1, source_target_pairs={{0,2},{1,3},{2,0},{3,1},{4,6},{5,7},{6,4},{7,5},{8,10},{9,11},{10,... | collective-permute-start | bytes 196616 | tf_op jit(solution)/shard_map/ppermute | solution.py:194
  61.2 4.3 %collective-permute-start.18 = (f32[128,128]{1,0:T(8,128)S(1)}, f32[128,128]{1,0:T(8,128)S(1)}, u32[]{:S(2)}, u32[]{:S(2)}) collective-permute-start(f32[128,128]{1,0:T(8,128)S(1)} %add.277), channel_id=1, source_target_pairs={{0,4},{1,5},{2,6},{3,7},{4,0},{5,1},{6,2},{7,3},{8,12},{9,13},{10,... | collective-permute-start | bytes 196616 | tf_op jit(solution)/shard_map/ppermute | solution.py:194
  65.5 5.5 %collective-permute-start.19 = (f32[128,128]{1,0:T(8,128)S(1)}, f32[128,128]{1,0:T(8,128)S(1)}, u32[]{:S(2)}, u32[]{:S(2)}) collective-permute-start(f32[128,128]{1,0:T(8,128)S(1)} %add.278), channel_id=1, source_target_pairs={{0,8},{1,9},{2,10},{3,11},{4,12},{5,13},{6,14},{7,15},{8,0},{9,1},... | collective-permute-start | bytes 196616 | tf_op jit(solution)/shard_map/ppermute | solution.py:194
  71.0 1.3 %collective-permute-start.20 = (f32[128,128]{1,0:T(8,128)S(1)}, f32[128,128]{1,0:T(8,128)S(1)}, u32[]{:S(2)}, u32[]{:S(2)}) collective-permute-start(f32[128,128]{1,0:T(8,128)S(1)} %add.279), channel_id=1, source_target_pairs={{0,1},{1,0},{2,3},{3,2},{4,5},{5,4},{6,7},{7,6},{8,9},{9,8},{10,11... | collective-permute-start | bytes 196616 | tf_op jit(solution)/shard_map/ppermute | solution.py:194
  (1 other events, 0.8 us)

commit v5 on v4

--- a/solution.py
+++ b/solution.py
@@ -22,8 +22,9 @@
 ROWS_BY_ROWS = (((1,), (1,)), ((), ()))
 
 
-def project_kernel(bits, own, first, shares, a_hbm, g_hbm, pi_hbm, po_hbm, *refs):
-    outs, (pi_ref, po_ref, a_buf, g_buf, sems) = refs[:-5], refs[-5:]
+def project_kernel(bits, own, first, shares, a_hbm, g_hbm, w_hbm, *refs):
+    outs, (w_ref, a_buf, g_buf, sems) = refs[:-4], refs[-4:]
+    width = a_buf.shape[2]
     ring, size = a_buf.shape[0], a_buf.shape[1]
     blocks = 1 << bits
     half = blocks // 2
@@ -37,17 +38,12 @@
             pltpu.make_async_copy(g_hbm.at[pl.ds(start, size), :], g_buf.at[slot], sems.at[slot, 1]),
         )
 
-    weights = (
-        pltpu.make_async_copy(pi_hbm, pi_ref, sems.at[ring, 0]),
-        pltpu.make_async_copy(po_hbm, po_ref, sems.at[ring, 1]),
-    )
-    for copy in weights:
-        copy.start()
+    weights = pltpu.make_async_copy(w_hbm, w_ref, sems.at[ring, 0])
+    weights.start()
     for step in range(ring - 1):
         for copy in copies(jnp.int32(step)):
             copy.start()
-    for copy in weights:
-        copy.wait()
+    weights.wait()
 
     def body(step, carry):
         @pl.when(step + ring - 1 < blocks)
@@ -58,8 +54,8 @@
         for copy in copies(step):
             copy.wait()
         slot = lax.rem(step, ring)
-        side_x = lax.dot_general(a_buf[slot], pi_ref[...], ROWS_BY_ROWS, preferred_element_type=jnp.float32)
-        side_g = lax.dot_general(g_buf[slot], po_ref[...], ROWS_BY_ROWS, preferred_element_type=jnp.float32)
+        side_x = lax.dot_general(a_buf[slot], w_ref[:, :width], ROWS_BY_ROWS, preferred_element_type=jnp.float32)
+        side_g = lax.dot_general(g_buf[slot], w_ref[:, width:], ROWS_BY_ROWS, preferred_element_type=jnp.float32)
         both = jnp.concatenate([side_x, side_g], axis=1)
         place = step & (half - 1)
 
@@ -91,10 +87,10 @@
     return flipped
 
 
-def project(bits, first, shares, activations, out_grads, proj_in, proj_out):
+def project(bits, first, shares, activations, out_grads, weights):
     tokens, width = activations.shape
     hidden = out_grads.shape[1]
-    rank = proj_in.shape[0]
+    rank = weights.shape[0]
     size = sum(shares)
     ring = min(RING, 1 << bits)
     outs = [
@@ -105,12 +101,11 @@
     vmem = pl.BlockSpec(memory_space=pltpu.VMEM)
     return pl.pallas_call(
         functools.partial(project_kernel, bits, tokens >> bits, first, shares),
-        in_specs=[pl.BlockSpec(memory_space=pl.ANY)] * 4,
+        in_specs=[pl.BlockSpec(memory_space=pl.ANY)] * 3,
         out_specs=[vmem] * len(outs),
         out_shape=outs,
         scratch_shapes=[
-            pltpu.VMEM(proj_in.shape, proj_in.dtype),
-            pltpu.VMEM(proj_out.shape, proj_out.dtype),
+            pltpu.VMEM(weights.shape, weights.dtype),
             pltpu.VMEM((ring, size, width), activations.dtype),
             pltpu.VMEM((ring, size, hidden), out_grads.dtype),
             pltpu.SemaphoreType.DMA((ring + 1, 2)),
@@ -118,7 +113,7 @@
         compiler_params=pltpu.CompilerParams(vmem_limit_bytes=VMEM),
         cost_estimate=pl.CostEstimate(flops=COST, bytes_accessed=COST, transcendentals=0),
         name="project",
-    )(activations, out_grads, proj_in, proj_out)
+    )(activations, out_grads, weights)
 
 
 def product_kernel(pieces, bits, own, edge_ref, scale_ref, *refs):
@@ -201,8 +196,8 @@
     shares = tuple(own * share // UNITS for share in CHUNKS)
     chunks = len(shares)
     on_both = [k >= chunks - BOTH_SIDES for k in range(chunks)]
-    weights = (proj_in.T, proj_out.T)
-    halves = list(project(bits, 0, shares[:CUT], activations, out_grads, *weights))
+    weights = jnp.concatenate([proj_in.T, proj_out.T], axis=1)
+    halves = list(project(bits, 0, shares[:CUT], activations, out_grads, weights))
     sends, keeps = halves[0::2], halves[1::2]
 
     def route(k):
@@ -228,7 +223,7 @@
         b = route(k)[stage]
         if len(sends) < chunks and stage == 1:
             weights, _ = lax.optimization_barrier((weights, sends))
-            halves = list(project(bits, sum(shares[:CUT]), shares[CUT:], activations, out_grads, *weights))
+            halves = list(project(bits, sum(shares[:CUT]), shares[CUT:], activations, out_grads, weights))
             sends, keeps = sends + halves[0::2], keeps + halves[1::2]
         send, keep = sends[k], keeps[k]
         if b == last and not BOTH_SIDES:

time: 74.1 us -> 73 us (0.985)
  local copies, waits for them, and re-layouts: 1.9 us -> 0.04 us
  other arithmetic: 0.75 us -> 1.82 us
    unnamed x8 -> x4, local copies, waits for them, and re-layouts: 1.87 us -> 0.01 us
    concatenate x0 -> x1, other arithmetic: none -> 1.07 us  [shards(): weights = jnp.concatenate([proj_in.T, proj_out.T], axis=1)]
where the time goes in v5:
time: 73 us; the launch traced here: 72.9 us
  waiting for transfers between devices  29.2 us (40%)
  starting transfers between devices  23.3 us (32%)
  Pallas kernels  16.8 us (23%)
  other arithmetic  1.82 us (2%)
  matrix products  1.52 us (2%)
    ppermute x21, waiting for transfers between devices, swap(): lax.ppermute(value, 'tp', [(i, i ^ 1 << bit) for i in range(devices)])  29.2 us
    ppermute x21, starting transfers between devices, swap(): lax.ppermute(value, 'tp', [(i, i ^ 1 << bit) for i in range(devices)])  23.3 us
    pallas_call x1, Pallas kernels, project(): pl.pallas_call(functools.partial(project_kernel, bits, tokens >> bits, fi...  15.4 us
    dot_general x1, matrix products, shards(): jnp.dot(pair.reshape(SEQS, rank * rank), queries.T, precision=lax.Precisi...  1.52 us
  transfers between devices with their start and end apart: 21, of which 13 were waited for; matrix products, arithmetic and copies ran while one was open for 1% of the time, Pallas kernels for 0%

profile of v5, /device:TPU:0, one launch (start us, length us, event | category | flops | bytes accessed | tf_op | source)
XLA Modules:
  0.0 72.9 jit_solution(5960552876445751630)
XLA Ops:
  0.0 1.1 %pad_maximum_fusion.w_hbm = bf16[64,2304]{1,0:T(8,128)(2,1)S(1)} fusion(bf16[64,1792]{1,0:T(8,128)(2,1)} %bitcast.116, bf16[64,512]{1,0:T(8,128)(2,1)} %bitcast.125), kind=kLoop, calls=%fused_computation.2 | loop fusion | flops 589824 | bytes 589824 | tf_op jit(solution)/shard_map/concatenate | solution.py:199
  1.1 15.4 %project.1 = (f32[1024,128]{1,0:T(8,128)S(1)}, f32[1024,128]{1,0:T(8,128)S(1)}, f32[1024,128]{1,0:T(8,128)S(1)}, f32[1024,128]{1,0:T(8,128)S(1)}, f32[1024,128]{...) custom-call(bf16[8192,512]{1,0:T(8,128)(2,1)} %a_hbm.1, ...), custom_call_target="tpu_custom_call" | custom-call | flops 1 | bytes 1 | tf_op jit(solution)/shard_map/project/pallas_call | solution.py:102
  18.6 2.9 %collective-permute-start.1 = (f32[512,128]{1,0:T(8,128)S(1)}, f32[512,128]{1,0:T(8,128)S(1)}, u32[]{:S(2)}, u32[]{:S(2)}) collective-permute-start(f32[512,128]{1,0:T(8,128)S(1)} %get-tuple-element.58), channel_id=1, source_target_pairs={{0,2},{1,3},{2,0},{3,1},{4,6},{5,7},{6,4},{7,5},{8,10},{9,11},{10,... | collective-permute-start | bytes 786440 | tf_op jit(solution)/shard_map/ppermute | solution.py:189
  21.6 1.6 %collective-permute-start.8 = (f32[512,128]{1,0:T(8,128)S(1)}, f32[512,128]{1,0:T(8,128)S(1)}, u32[]{:S(2)}, u32[]{:S(2)}) collective-permute-start(f32[512,128]{1,0:T(8,128)S(1)} %bitcast.115), channel_id=1, source_target_pairs={{0,4},{1,5},{2,6},{3,7},{4,0},{5,1},{6,2},{7,3},{8,12},{9,13},{10,... | collective-permute-start | bytes 786440 | tf_op jit(solution)/shard_map/ppermute | solution.py:189
  24.9 3.8 %collective-permute-done.1 = f32[512,128]{1,0:T(8,128)S(1)} collective-permute-done((f32[512,128]{1,0:T(8,128)S(1)}, f32[512,128]{1,0:T(8,128)S(1)}, u32[]{:S(2)}, u32[]{:S(2)}) %collective-permute-start.1) | collective-permute-done | bytes 262176 | tf_op jit(solution)/shard_map/ppermute | solution.py:189
  28.7 2.2 %collective-permute-start.5 = (f32[256,128]{1,0:T(8,128)S(1)}, f32[256,128]{1,0:T(8,128)S(1)}, u32[]{:S(2)}, u32[]{:S(2)}) collective-permute-start(f32[256,128]{1,0:T(8,128)S(1)} %get-tuple-element.66), channel_id=1, source_target_pairs={{0,4},{1,5},{2,6},{3,7},{4,0},{5,1},{6,2},{7,3},{8,12},{9,13},{10,... | collective-permute-start | bytes 393224 | tf_op jit(solution)/shard_map/ppermute | solution.py:189
  30.9 1.6 %collective-permute-start.12 = (f32[256,128]{1,0:T(8,128)S(1)}, f32[256,128]{1,0:T(8,128)S(1)}, u32[]{:S(2)}, u32[]{:S(2)}) collective-permute-start(f32[256,128]{1,0:T(8,128)S(1)} %get-tuple-element.64), channel_id=1, source_target_pairs={{0,2},{1,3},{2,0},{3,1},{4,6},{5,7},{6,4},{7,5},{8,10},{9,11},{10,... | collective-permute-start | bytes 393224 | tf_op jit(solution)/shard_map/ppermute | solution.py:189
  32.5 1.8 %collective-permute-done.7 = f32[512,128]{1,0:T(8,128)S(1)} collective-permute-done((f32[512,128]{1,0:T(8,128)S(1)}, f32[512,128]{1,0:T(8,128)S(1)}, u32[]{:S(2)}, u32[]{:S(2)}) %collective-permute-start.7) | collective-permute-done | bytes 262176 | tf_op jit(solution)/shard_map/ppermute | solution.py:189
  34.3 2.2 %collective-permute-start.11 = (f32[256,128]{1,0:T(8,128)S(1)}, f32[256,128]{1,0:T(8,128)S(1)}, u32[]{:S(2)}, u32[]{:S(2)}) collective-permute-start(f32[256,128]{1,0:T(8,128)S(1)} %get-tuple-element.62), channel_id=1, source_target_pairs={{0,4},{1,5},{2,6},{3,7},{4,0},{5,1},{6,2},{7,3},{8,12},{9,13},{10,... | collective-permute-start | bytes 393224 | tf_op jit(solution)/shard_map/ppermute | solution.py:189
  36.6 1.6 %collective-permute-start.10 = (f32[256,128]{1,0:T(8,128)S(1)}, f32[256,128]{1,0:T(8,128)S(1)}, u32[]{:S(2)}, u32[]{:S(2)}) collective-permute-start(f32[256,128]{1,0:T(8,128)S(1)} %get-tuple-element.60), channel_id=1, source_target_pairs={{0,2},{1,3},{2,0},{3,1},{4,6},{5,7},{6,4},{7,5},{8,10},{9,11},{10,... | collective-permute-start | bytes 393224 | tf_op jit(solution)/shard_map/ppermute | solution.py:189
  38.1 1.2 %collective-permute-done.5 = f32[256,128]{1,0:T(8,128)S(1)} collective-permute-done((f32[256,128]{1,0:T(8,128)S(1)}, f32[256,128]{1,0:T(8,128)S(1)}, u32[]{:S(2)}, u32[]{:S(2)}) %collective-permute-start.5) | collective-permute-done | bytes 131104 | tf_op jit(solution)/shard_map/ppermute | solution.py:189
  39.3 2.7 %collective-permute-start.9 = (f32[128,128]{1,0:T(8,128)S(1)}, f32[128,128]{1,0:T(8,128)S(1)}, u32[]{:S(2)}, u32[]{:S(2)}) collective-permute-start(f32[128,128]{1,0:T(8,128)S(1)} %fusion.19), channel_id=1, source_target_pairs={{0,8},{1,9},{2,10},{3,11},{4,12},{5,13},{6,14},{7,15},{8,0},{9,1},... | collective-permute-start | bytes 196616 | tf_op jit(solution)/shard_map/ppermute | solution.py:189
  42.4 2.7 %collective-permute-start.14 = (f32[128,128]{1,0:T(8,128)S(1)}, f32[128,128]{1,0:T(8,128)S(1)}, u32[]{:S(2)}, u32[]{:S(2)}) collective-permute-start(f32[128,128]{1,0:T(8,128)S(1)} %fusion.17), channel_id=1, source_target_pairs={{0,8},{1,9},{2,10},{3,11},{4,12},{5,13},{6,14},{7,15},{8,0},{9,1},... | collective-permute-start | bytes 196616 | tf_op jit(solution)/shard_map/ppermute | solution.py:189
  45.5 3.9 %collective-permute-done.9 = f32[128,128]{1,0:T(8,128)S(1)} collective-permute-done((f32[128,128]{1,0:T(8,128)S(1)}, f32[128,128]{1,0:T(8,128)S(1)}, u32[]{:S(2)}, u32[]{:S(2)}) %collective-permute-start.9) | collective-permute-done | bytes 65568 | tf_op jit(solution)/shard_map/ppermute | solution.py:189
  49.4 2.1 %collective-permute-done.13 = f32[128,128]{1,0:T(8,128)S(1)} collective-permute-done((f32[128,128]{1,0:T(8,128)S(1)}, f32[128,128]{1,0:T(8,128)S(1)}, u32[]{:S(2)}, u32[]{:S(2)}) %collective-permute-start.13) | collective-permute-done | bytes 65568 | tf_op jit(solution)/shard_map/ppermute | solution.py:189
  53.1 1.4 %product.1 = (f32[128,128]{1,0:T(8,128)S(1)}, f32[128,128]{1,0:T(8,128)S(1)}) custom-call(s32[9]{0:T(128)S(1)} %convert_reduce_fusion.edge_ref, f32[8]{0:T(128)S(1)} %convert_divide_fusion.scale_ref, f32[128,128]{1,0:T(8,128)S(1)} %fusion.21.refs_0_, f32[128,128]{1,0:T(8,128)S(1)} %fusion.15.refs_1_, f32[128,128]{1,0:T(8,128)S(1)} %fusion.13.refs_2_, ...), custom_call_target="tpu_custom_call" | custom-call | tf_op jit(solution)/shard_map/product/pallas_call | solution.py:169
  54.5 1.2 %collective-permute-done.16 = f32[128,128]{1,0:T(8,128)S(1)} collective-permute-done((f32[128,128]{1,0:T(8,128)S(1)}, f32[128,128]{1,0:T(8,128)S(1)}, u32[]{:S(2)}, u32[]{:S(2)}) %collective-permute-start.16) | collective-permute-done | bytes 65568 | tf_op jit(solution)/shard_map/ppermute | solution.py:189
  55.8 1.2 %collective-permute-start.17 = (f32[128,128]{1,0:T(8,128)S(1)}, f32[128,128]{1,0:T(8,128)S(1)}, u32[]{:S(2)}, u32[]{:S(2)}) collective-permute-start(f32[128,128]{1,0:T(8,128)S(1)} %add.276), channel_id=1, source_target_pairs={{0,2},{1,3},{2,0},{3,1},{4,6},{5,7},{6,4},{7,5},{8,10},{9,11},{10,... | collective-permute-start | bytes 196616 | tf_op jit(solution)/shard_map/ppermute | solution.py:189
  57.0 3.1 %collective-permute-done.17 = f32[128,128]{1,0:T(8,128)S(1)} collective-permute-done((f32[128,128]{1,0:T(8,128)S(1)}, f32[128,128]{1,0:T(8,128)S(1)}, u32[]{:S(2)}, u32[]{:S(2)}) %collective-permute-start.17) | collective-permute-done | bytes 65568 | tf_op jit(solution)/shard_map/ppermute | solution.py:189
  60.2 4.3 %collective-permute-done.18 = f32[128,128]{1,0:T(8,128)S(1)} collective-permute-done((f32[128,128]{1,0:T(8,128)S(1)}, f32[128,128]{1,0:T(8,128)S(1)}, u32[]{:S(2)}, u32[]{:S(2)}) %collective-permute-start.18) | collective-permute-done | bytes 65568 | tf_op jit(solution)/shard_map/ppermute | solution.py:189
  64.4 1.1 %collective-permute-start.19 = (f32[128,128]{1,0:T(8,128)S(1)}, f32[128,128]{1,0:T(8,128)S(1)}, u32[]{:S(2)}, u32[]{:S(2)}) collective-permute-start(f32[128,128]{1,0:T(8,128)S(1)} %add.278), channel_id=1, source_target_pairs={{0,8},{1,9},{2,10},{3,11},{4,12},{5,13},{6,14},{7,15},{8,0},{9,1},... | collective-permute-start | bytes 196616 | tf_op jit(solution)/shard_map/ppermute | solution.py:189
  65.6 4.4 %collective-permute-done.19 = f32[128,128]{1,0:T(8,128)S(1)} collective-permute-done((f32[128,128]{1,0:T(8,128)S(1)}, f32[128,128]{1,0:T(8,128)S(1)}, u32[]{:S(2)}, u32[]{:S(2)}) %collective-permute-start.19) | collective-permute-done | bytes 65568 | tf_op jit(solution)/shard_map/ppermute | solution.py:189
  70.1 1.2 %collective-permute-done.20 = f32[128,128]{1,0:T(8,128)S(1)} collective-permute-done((f32[128,128]{1,0:T(8,128)S(1)}, f32[128,128]{1,0:T(8,128)S(1)}, u32[]{:S(2)}, u32[]{:S(2)}) %collective-permute-start.20) | collective-permute-done | bytes 65568 | tf_op jit(solution)/shard_map/ppermute | solution.py:189
  71.4 1.5 %fusion.22 = f32[8,64]{1,0:T(8,128)} fusion(f32[8,4096]{1,0:T(8,128)S(1)} %reshape.236, f32[64,4096]{1,0:T(8,128)S(1)} %copy-done), kind=kOutput, calls=%fused_computation.55 | convolution fusion | flops 25165824 | bytes 1181696 | tf_op jit(solution)/shard_map/dot_general | solution.py:272
  (53 shorter events, 6.5 us)
Async XLA Ops:
  0.0 71.4 %copy-start = (f32[64,4096]{1,0:T(8,128)S(1)}, f32[64,4096]{1,0:T(8,128)}, u32[]{:S(2)}) copy-start(f32[64,4096]{1,0:T(8,128)} %param.11) | copy-start | bytes 3145732
  0.0 17.6 %copy-start.1 = (s32[8192]{0:T(1024)S(1)}, s32[8192]{0:T(1024)}, u32[]{:S(2)}) copy-start(s32[8192]{0:T(1024)} %param.10) | copy-start | bytes 98308
  16.5 2.1 %collective-permute-start = (f32[1024,128]{1,0:T(8,128)S(1)}, f32[1024,128]{1,0:T(8,128)S(1)}, u32[]{:S(2)}, u32[]{:S(2)}) collective-permute-start(f32[1024,128]{1,0:T(8,128)S(1)} %get-tuple-element.31), channel_id=1, source_target_pairs={{0,1},{1,0},{2,3},{3,2},{4,5},{5,4},{6,7},{7,6},{8,9},{9,8},{10,11... | collective-permute-start | bytes 1572872 | tf_op jit(solution)/shard_map/ppermute | solution.py:189
  17.1 4.5 %collective-permute-start.4 = (f32[1024,128]{1,0:T(8,128)S(1)}, f32[1024,128]{1,0:T(8,128)S(1)}, u32[]{:S(2)}, u32[]{:S(2)}) collective-permute-start(f32[1024,128]{1,0:T(8,128)S(1)} %get-tuple-element.37), channel_id=1, source_target_pairs={{0,1},{1,0},{2,3},{3,2},{4,5},{5,4},{6,7},{7,6},{8,9},{9,8},{10,11... | collective-permute-start | bytes 1572872 | tf_op jit(solution)/shard_map/ppermute | solution.py:189
  17.1 6.1 %collective-permute-start.3 = (f32[1024,128]{1,0:T(8,128)S(1)}, f32[1024,128]{1,0:T(8,128)S(1)}, u32[]{:S(2)}, u32[]{:S(2)}) collective-permute-start(f32[1024,128]{1,0:T(8,128)S(1)} %get-tuple-element.35), channel_id=1, source_target_pairs={{0,1},{1,0},{2,3},{3,2},{4,5},{5,4},{6,7},{7,6},{8,9},{9,8},{10,11... | collective-permute-start | bytes 1572872 | tf_op jit(solution)/shard_map/ppermute | solution.py:189
  17.6 6.5 %collective-permute-start.2 = (f32[1024,128]{1,0:T(8,128)S(1)}, f32[1024,128]{1,0:T(8,128)S(1)}, u32[]{:S(2)}, u32[]{:S(2)}) collective-permute-start(f32[1024,128]{1,0:T(8,128)S(1)} %get-tuple-element.33), channel_id=1, source_target_pairs={{0,1},{1,0},{2,3},{3,2},{4,5},{5,4},{6,7},{7,6},{8,9},{9,8},{10,11... | collective-permute-start | bytes 1572872 | tf_op jit(solution)/shard_map/ppermute | solution.py:189
  18.6 10.0 %collective-permute-start.1 = (f32[512,128]{1,0:T(8,128)S(1)}, f32[512,128]{1,0:T(8,128)S(1)}, u32[]{:S(2)}, u32[]{:S(2)}) collective-permute-start(f32[512,128]{1,0:T(8,128)S(1)} %get-tuple-element.58), channel_id=1, source_target_pairs={{0,2},{1,3},{2,0},{3,1},{4,6},{5,7},{6,4},{7,5},{8,10},{9,11},{10,... | collective-permute-start | bytes 786440 | tf_op jit(solution)/shard_map/ppermute | solution.py:189
  21.6 9.3 %collective-permute-start.8 = (f32[512,128]{1,0:T(8,128)S(1)}, f32[512,128]{1,0:T(8,128)S(1)}, u32[]{:S(2)}, u32[]{:S(2)}) collective-permute-start(f32[512,128]{1,0:T(8,128)S(1)} %bitcast.115), channel_id=1, source_target_pairs={{0,4},{1,5},{2,6},{3,7},{4,0},{5,1},{6,2},{7,3},{8,12},{9,13},{10,... | collective-permute-start | bytes 786440 | tf_op jit(solution)/shard_map/ppermute | solution.py:189
  23.3 11.0 %collective-permute-start.7 = (f32[512,128]{1,0:T(8,128)S(1)}, f32[512,128]{1,0:T(8,128)S(1)}, u32[]{:S(2)}, u32[]{:S(2)}) collective-permute-start(f32[512,128]{1,0:T(8,128)S(1)} %get-tuple-element.56), channel_id=1, source_target_pairs={{0,2},{1,3},{2,0},{3,1},{4,6},{5,7},{6,4},{7,5},{8,10},{9,11},{10,... | collective-permute-start | bytes 786440 | tf_op jit(solution)/shard_map/ppermute | solution.py:189
  24.1 12.4 %collective-permute-start.6 = (f32[512,128]{1,0:T(8,128)S(1)}, f32[512,128]{1,0:T(8,128)S(1)}, u32[]{:S(2)}, u32[]{:S(2)}) collective-permute-start(f32[512,128]{1,0:T(8,128)S(1)} %bitcast.113), channel_id=1, source_target_pairs={{0,4},{1,5},{2,6},{3,7},{4,0},{5,1},{6,2},{7,3},{8,12},{9,13},{10,... | collective-permute-start | bytes 786440 | tf_op jit(solution)/shard_map/ppermute | solution.py:189
  28.7 10.6 %collective-permute-start.5 = (f32[256,128]{1,0:T(8,128)S(1)}, f32[256,128]{1,0:T(8,128)S(1)}, u32[]{:S(2)}, u32[]{:S(2)}) collective-permute-start(f32[256,128]{1,0:T(8,128)S(1)} %get-tuple-element.66), channel_id=1, source_target_pairs={{0,4},{1,5},{2,6},{3,7},{4,0},{5,1},{6,2},{7,3},{8,12},{9,13},{10,... | collective-permute-start | bytes 393224 | tf_op jit(solution)/shard_map/ppermute | solution.py:189
  30.9 11.1 %collective-permute-start.12 = (f32[256,128]{1,0:T(8,128)S(1)}, f32[256,128]{1,0:T(8,128)S(1)}, u32[]{:S(2)}, u32[]{:S(2)}) collective-permute-start(f32[256,128]{1,0:T(8,128)S(1)} %get-tuple-element.64), channel_id=1, source_target_pairs={{0,2},{1,3},{2,0},{3,1},{4,6},{5,7},{6,4},{7,5},{8,10},{9,11},{10,... | collective-permute-start | bytes 393224 | tf_op jit(solution)/shard_map/ppermute | solution.py:189
  34.3 8.1 %collective-permute-start.11 = (f32[256,128]{1,0:T(8,128)S(1)}, f32[256,128]{1,0:T(8,128)S(1)}, u32[]{:S(2)}, u32[]{:S(2)}) collective-permute-start(f32[256,128]{1,0:T(8,128)S(1)} %get-tuple-element.62), channel_id=1, source_target_pairs={{0,4},{1,5},{2,6},{3,7},{4,0},{5,1},{6,2},{7,3},{8,12},{9,13},{10,... | collective-permute-start | bytes 393224 | tf_op jit(solution)/shard_map/ppermute | solution.py:189
  36.6 8.5 %collective-permute-start.10 = (f32[256,128]{1,0:T(8,128)S(1)}, f32[256,128]{1,0:T(8,128)S(1)}, u32[]{:S(2)}, u32[]{:S(2)}) collective-permute-start(f32[256,128]{1,0:T(8,128)S(1)} %get-tuple-element.60), channel_id=1, source_target_pairs={{0,2},{1,3},{2,0},{3,1},{4,6},{5,7},{6,4},{7,5},{8,10},{9,11},{10,... | collective-permute-start | bytes 393224 | tf_op jit(solution)/shard_map/ppermute | solution.py:189
  39.3 10.1 %collective-permute-start.9 = (f32[128,128]{1,0:T(8,128)S(1)}, f32[128,128]{1,0:T(8,128)S(1)}, u32[]{:S(2)}, u32[]{:S(2)}) collective-permute-start(f32[128,128]{1,0:T(8,128)S(1)} %fusion.19), channel_id=1, source_target_pairs={{0,8},{1,9},{2,10},{3,11},{4,12},{5,13},{6,14},{7,15},{8,0},{9,1},... | collective-permute-start | bytes 196616 | tf_op jit(solution)/shard_map/ppermute | solution.py:189
  42.0 9.5 %collective-permute-start.13 = (f32[128,128]{1,0:T(8,128)S(1)}, f32[128,128]{1,0:T(8,128)S(1)}, u32[]{:S(2)}, u32[]{:S(2)}) collective-permute-start(f32[128,128]{1,0:T(8,128)S(1)} %fusion.18), channel_id=1, source_target_pairs={{0,8},{1,9},{2,10},{3,11},{4,12},{5,13},{6,14},{7,15},{8,0},{9,1},... | collective-permute-start | bytes 196616 | tf_op jit(solution)/shard_map/ppermute | solution.py:189
  42.4 9.9 %collective-permute-start.14 = (f32[128,128]{1,0:T(8,128)S(1)}, f32[128,128]{1,0:T(8,128)S(1)}, u32[]{:S(2)}, u32[]{:S(2)}) collective-permute-start(f32[128,128]{1,0:T(8,128)S(1)} %fusion.17), channel_id=1, source_target_pairs={{0,8},{1,9},{2,10},{3,11},{4,12},{5,13},{6,14},{7,15},{8,0},{9,1},... | collective-permute-start | bytes 196616 | tf_op jit(solution)/shard_map/ppermute | solution.py:189
  45.1 7.9 %collective-permute-start.15 = (f32[128,128]{1,0:T(8,128)S(1)}, f32[128,128]{1,0:T(8,128)S(1)}, u32[]{:S(2)}, u32[]{:S(2)}) collective-permute-start(f32[128,128]{1,0:T(8,128)S(1)} %fusion.16), channel_id=1, source_target_pairs={{0,8},{1,9},{2,10},{3,11},{4,12},{5,13},{6,14},{7,15},{8,0},{9,1},... | collective-permute-start | bytes 196616 | tf_op jit(solution)/shard_map/ppermute | solution.py:189
  54.4 1.3 %collective-permute-start.16 = (f32[128,128]{1,0:T(8,128)S(1)}, f32[128,128]{1,0:T(8,128)S(1)}, u32[]{:S(2)}, u32[]{:S(2)}) collective-permute-start(f32[128,128]{1,0:T(8,128)S(1)} %get-tuple-element.54), channel_id=1, source_target_pairs={{0,1},{1,0},{2,3},{3,2},{4,5},{5,4},{6,7},{7,6},{8,9},{9,8},{10,11... | collective-permute-start | bytes 196616 | tf_op jit(solution)/shard_map/ppermute | solution.py:189
  55.8 4.3 %collective-permute-start.17 = (f32[128,128]{1,0:T(8,128)S(1)}, f32[128,128]{1,0:T(8,128)S(1)}, u32[]{:S(2)}, u32[]{:S(2)}) collective-permute-start(f32[128,128]{1,0:T(8,128)S(1)} %add.276), channel_id=1, source_target_pairs={{0,2},{1,3},{2,0},{3,1},{4,6},{5,7},{6,4},{7,5},{8,10},{9,11},{10,... | collective-permute-start | bytes 196616 | tf_op jit(solution)/shard_map/ppermute | solution.py:189
  60.1 4.3 %collective-permute-start.18 = (f32[128,128]{1,0:T(8,128)S(1)}, f32[128,128]{1,0:T(8,128)S(1)}, u32[]{:S(2)}, u32[]{:S(2)}) collective-permute-start(f32[128,128]{1,0:T(8,128)S(1)} %add.277), channel_id=1, source_target_pairs={{0,4},{1,5},{2,6},{3,7},{4,0},{5,1},{6,2},{7,3},{8,12},{9,13},{10,... | collective-permute-start | bytes 196616 | tf_op jit(solution)/shard_map/ppermute | solution.py:189
  64.4 5.5 %collective-permute-start.19 = (f32[128,128]{1,0:T(8,128)S(1)}, f32[128,128]{1,0:T(8,128)S(1)}, u32[]{:S(2)}, u32[]{:S(2)}) collective-permute-start(f32[128,128]{1,0:T(8,128)S(1)} %add.278), channel_id=1, source_target_pairs={{0,8},{1,9},{2,10},{3,11},{4,12},{5,13},{6,14},{7,15},{8,0},{9,1},... | collective-permute-start | bytes 196616 | tf_op jit(solution)/shard_map/ppermute | solution.py:189
  70.0 1.3 %collective-permute-start.20 = (f32[128,128]{1,0:T(8,128)S(1)}, f32[128,128]{1,0:T(8,128)S(1)}, u32[]{:S(2)}, u32[]{:S(2)}) collective-permute-start(f32[128,128]{1,0:T(8,128)S(1)} %add.279), channel_id=1, source_target_pairs={{0,1},{1,0},{2,3},{3,2},{4,5},{5,4},{6,7},{7,6},{8,9},{9,8},{10,11... | collective-permute-start | bytes 196616 | tf_op jit(solution)/shard_map/ppermute | solution.py:189

commit v6 on v5

--- a/solution.py
+++ b/solution.py
@@ -185,8 +185,11 @@
     own = tokens // devices
     me = lax.axis_index("tp")
 
+    def exchange(value, mask):
+        return lax.ppermute(value, "tp", [(i, i ^ mask) for i in range(devices)])
+
     def swap(value, bit):
-        return lax.ppermute(value, "tp", [(i, i ^ (1 << bit)) for i in range(devices)])
+        return exchange(value, 1 << bit)
 
     edges = jnp.sum(
         (seg_ids[None, :] < jnp.arange(SEQS + 1, dtype=jnp.int32)[:, None]).astype(jnp.int32), axis=1
@@ -264,8 +267,10 @@
         grads = grads + swap(grads, last)
         send, keep = group_product(late)
         grads = grads + keep + swap(send, 0)
+    grads = (grads + exchange(grads, 6)) + (exchange(grads, 2) + exchange(grads, 4))
     for b in hops:
-        grads = grads + swap(grads, b)
+        if b > 2:
+            grads = grads + swap(grads, b)
     other = swap(grads, 0)
     even = (me & 1) == 0
     pair = jnp.concatenate([jnp.where(even, grads, other), jnp.where(even, other, grads)], axis=0)

time: 73 us -> 70.3 us (0.963)
  waiting for transfers between devices: 29.2 us -> 22.6 us
  starting transfers between devices: 23.3 us -> 27.2 us
    ppermute x21 -> x22, waiting for transfers between devices: 29.2 us -> 22.6 us  [exchange(): return lax.ppermute(value, 'tp', [(i, i ^ mask) for i in range(devices)])]
    ppermute x21 -> x22, starting transfers between devices: 23.3 us -> 27.2 us  [exchange(): return lax.ppermute(value, 'tp', [(i, i ^ mask) for i in range(devices)])]
  transfers between devices with their start and end apart: 21 -> 22, of which waited for: 13 -> 13; matrix products, arithmetic and copies ran while one was open for 1% -> 1% of each run, Pallas kernels for 0% -> 0%
where the time goes in v6:
time: 70.3 us; the launch traced here: 70.2 us
  starting transfers between devices  27.2 us (39%)
  waiting for transfers between devices  22.6 us (32%)
  Pallas kernels  16.8 us (24%)
  other arithmetic  1.82 us (3%)
  matrix products  1.52 us (2%)
    ppermute x22, starting transfers between devices, exchange(): return lax.ppermute(value, 'tp', [(i, i ^ mask) for i in range(devices)])  27.2 us
    ppermute x22, waiting for transfers between devices, exchange(): return lax.ppermute(value, 'tp', [(i, i ^ mask) for i in range(devices)])  22.6 us
    pallas_call x1, Pallas kernels, project(): pl.pallas_call(functools.partial(project_kernel, bits, tokens >> bits, fi...  15.4 us
    dot_general x1, matrix products, shards(): jnp.dot(pair.reshape(SEQS, rank * rank), queries.T, precision=lax.Precisi...  1.52 us
  transfers between devices with their start and end apart: 22, of which 13 were waited for; matrix products, arithmetic and copies ran while one was open for 1% of the time, Pallas kernels for 0%

profile of v6, /device:TPU:0, one launch (start us, length us, event | category | flops | bytes accessed | tf_op | source)
XLA Modules:
  0.0 70.2 jit_solution(8574155427842027539)
XLA Ops:
  0.0 1.1 %pad_maximum_fusion.w_hbm = bf16[64,2304]{1,0:T(8,128)(2,1)S(1)} fusion(bf16[64,1792]{1,0:T(8,128)(2,1)} %bitcast.116, bf16[64,512]{1,0:T(8,128)(2,1)} %bitcast.125), kind=kLoop, calls=%fused_computation.2 | loop fusion | flops 589824 | bytes 589824 | tf_op jit(solution)/shard_map/concatenate | solution.py:202
  1.1 15.4 %project.1 = (f32[1024,128]{1,0:T(8,128)S(1)}, f32[1024,128]{1,0:T(8,128)S(1)}, f32[1024,128]{1,0:T(8,128)S(1)}, f32[1024,128]{1,0:T(8,128)S(1)}, f32[1024,128]{...) custom-call(bf16[8192,512]{1,0:T(8,128)(2,1)} %a_hbm.1, ...), custom_call_target="tpu_custom_call" | custom-call | flops 1 | bytes 1 | tf_op jit(solution)/shard_map/project/pallas_call | solution.py:102
  18.6 2.9 %collective-permute-start.1 = (f32[512,128]{1,0:T(8,128)S(1)}, f32[512,128]{1,0:T(8,128)S(1)}, u32[]{:S(2)}, u32[]{:S(2)}) collective-permute-start(f32[512,128]{1,0:T(8,128)S(1)} %get-tuple-element.58), channel_id=1, source_target_pairs={{0,2},{1,3},{2,0},{3,1},{4,6},{5,7},{6,4},{7,5},{8,10},{9,11},{10,... | collective-permute-start | bytes 786440 | tf_op jit(solution)/shard_map/ppermute | solution.py:189
  21.6 1.6 %collective-permute-start.8 = (f32[512,128]{1,0:T(8,128)S(1)}, f32[512,128]{1,0:T(8,128)S(1)}, u32[]{:S(2)}, u32[]{:S(2)}) collective-permute-start(f32[512,128]{1,0:T(8,128)S(1)} %bitcast.115), channel_id=1, source_target_pairs={{0,4},{1,5},{2,6},{3,7},{4,0},{5,1},{6,2},{7,3},{8,12},{9,13},{10,... | collective-permute-start | bytes 786440 | tf_op jit(solution)/shard_map/ppermute | solution.py:189
  24.9 3.8 %collective-permute-done.1 = f32[512,128]{1,0:T(8,128)S(1)} collective-permute-done((f32[512,128]{1,0:T(8,128)S(1)}, f32[512,128]{1,0:T(8,128)S(1)}, u32[]{:S(2)}, u32[]{:S(2)}) %collective-permute-start.1) | collective-permute-done | bytes 262176 | tf_op jit(solution)/shard_map/ppermute | solution.py:189
  28.7 2.2 %collective-permute-start.5 = (f32[256,128]{1,0:T(8,128)S(1)}, f32[256,128]{1,0:T(8,128)S(1)}, u32[]{:S(2)}, u32[]{:S(2)}) collective-permute-start(f32[256,128]{1,0:T(8,128)S(1)} %get-tuple-element.66), channel_id=1, source_target_pairs={{0,4},{1,5},{2,6},{3,7},{4,0},{5,1},{6,2},{7,3},{8,12},{9,13},{10,... | collective-permute-start | bytes 393224 | tf_op jit(solution)/shard_map/ppermute | solution.py:189
  30.9 1.6 %collective-permute-start.12 = (f32[256,128]{1,0:T(8,128)S(1)}, f32[256,128]{1,0:T(8,128)S(1)}, u32[]{:S(2)}, u32[]{:S(2)}) collective-permute-start(f32[256,128]{1,0:T(8,128)S(1)} %get-tuple-element.64), channel_id=1, source_target_pairs={{0,2},{1,3},{2,0},{3,1},{4,6},{5,7},{6,4},{7,5},{8,10},{9,11},{10,... | collective-permute-start | bytes 393224 | tf_op jit(solution)/shard_map/ppermute | solution.py:189
  32.5 1.8 %collective-permute-done.7 = f32[512,128]{1,0:T(8,128)S(1)} collective-permute-done((f32[512,128]{1,0:T(8,128)S(1)}, f32[512,128]{1,0:T(8,128)S(1)}, u32[]{:S(2)}, u32[]{:S(2)}) %collective-permute-start.7) | collective-permute-done | bytes 262176 | tf_op jit(solution)/shard_map/ppermute | solution.py:189
  34.3 2.2 %collective-permute-start.11 = (f32[256,128]{1,0:T(8,128)S(1)}, f32[256,128]{1,0:T(8,128)S(1)}, u32[]{:S(2)}, u32[]{:S(2)}) collective-permute-start(f32[256,128]{1,0:T(8,128)S(1)} %get-tuple-element.62), channel_id=1, source_target_pairs={{0,4},{1,5},{2,6},{3,7},{4,0},{5,1},{6,2},{7,3},{8,12},{9,13},{10,... | collective-permute-start | bytes 393224 | tf_op jit(solution)/shard_map/ppermute | solution.py:189
  36.6 1.6 %collective-permute-start.10 = (f32[256,128]{1,0:T(8,128)S(1)}, f32[256,128]{1,0:T(8,128)S(1)}, u32[]{:S(2)}, u32[]{:S(2)}) collective-permute-start(f32[256,128]{1,0:T(8,128)S(1)} %get-tuple-element.60), channel_id=1, source_target_pairs={{0,2},{1,3},{2,0},{3,1},{4,6},{5,7},{6,4},{7,5},{8,10},{9,11},{10,... | collective-permute-start | bytes 393224 | tf_op jit(solution)/shard_map/ppermute | solution.py:189
  38.1 1.2 %collective-permute-done.5 = f32[256,128]{1,0:T(8,128)S(1)} collective-permute-done((f32[256,128]{1,0:T(8,128)S(1)}, f32[256,128]{1,0:T(8,128)S(1)}, u32[]{:S(2)}, u32[]{:S(2)}) %collective-permute-start.5) | collective-permute-done | bytes 131104 | tf_op jit(solution)/shard_map/ppermute | solution.py:189
  39.3 2.7 %collective-permute-start.9 = (f32[128,128]{1,0:T(8,128)S(1)}, f32[128,128]{1,0:T(8,128)S(1)}, u32[]{:S(2)}, u32[]{:S(2)}) collective-permute-start(f32[128,128]{1,0:T(8,128)S(1)} %fusion.19), channel_id=1, source_target_pairs={{0,8},{1,9},{2,10},{3,11},{4,12},{5,13},{6,14},{7,15},{8,0},{9,1},... | collective-permute-start | bytes 196616 | tf_op jit(solution)/shard_map/ppermute | solution.py:189
  42.4 2.7 %collective-permute-start.14 = (f32[128,128]{1,0:T(8,128)S(1)}, f32[128,128]{1,0:T(8,128)S(1)}, u32[]{:S(2)}, u32[]{:S(2)}) collective-permute-start(f32[128,128]{1,0:T(8,128)S(1)} %fusion.17), channel_id=1, source_target_pairs={{0,8},{1,9},{2,10},{3,11},{4,12},{5,13},{6,14},{7,15},{8,0},{9,1},... | collective-permute-start | bytes 196616 | tf_op jit(solution)/shard_map/ppermute | solution.py:189
  45.5 3.9 %collective-permute-done.9 = f32[128,128]{1,0:T(8,128)S(1)} collective-permute-done((f32[128,128]{1,0:T(8,128)S(1)}, f32[128,128]{1,0:T(8,128)S(1)}, u32[]{:S(2)}, u32[]{:S(2)}) %collective-permute-start.9) | collective-permute-done | bytes 65568 | tf_op jit(solution)/shard_map/ppermute | solution.py:189
  49.4 2.1 %collective-permute-done.13 = f32[128,128]{1,0:T(8,128)S(1)} collective-permute-done((f32[128,128]{1,0:T(8,128)S(1)}, f32[128,128]{1,0:T(8,128)S(1)}, u32[]{:S(2)}, u32[]{:S(2)}) %collective-permute-start.13) | collective-permute-done | bytes 65568 | tf_op jit(solution)/shard_map/ppermute | solution.py:189
  53.1 1.4 %product.1 = (f32[128,128]{1,0:T(8,128)S(1)}, f32[128,128]{1,0:T(8,128)S(1)}) custom-call(s32[9]{0:T(128)S(1)} %convert_reduce_fusion.edge_ref, f32[8]{0:T(128)S(1)} %convert_divide_fusion.scale_ref, f32[128,128]{1,0:T(8,128)S(1)} %fusion.21.refs_0_, f32[128,128]{1,0:T(8,128)S(1)} %fusion.15.refs_1_, f32[128,128]{1,0:T(8,128)S(1)} %fusion.13.refs_2_, ...), custom_call_target="tpu_custom_call" | custom-call | tf_op jit(solution)/shard_map/product/pallas_call | solution.py:169
  54.5 1.2 %collective-permute-done.16 = f32[128,128]{1,0:T(8,128)S(1)} collective-permute-done((f32[128,128]{1,0:T(8,128)S(1)}, f32[128,128]{1,0:T(8,128)S(1)}, u32[]{:S(2)}, u32[]{:S(2)}) %collective-permute-start.16) | collective-permute-done | bytes 65568 | tf_op jit(solution)/shard_map/ppermute | solution.py:189
  56.1 1.0 %collective-permute-start.18 = (f32[128,128]{1,0:T(8,128)S(1)}, f32[128,128]{1,0:T(8,128)S(1)}, u32[]{:S(2)}, u32[]{:S(2)}) collective-permute-start(f32[128,128]{1,0:T(8,128)S(1)} %add.279), channel_id=1, source_target_pairs={{0,2},{1,3},{2,0},{3,1},{4,6},{5,7},{6,4},{7,5},{8,10},{9,11},{10,... | collective-permute-start | bytes 196616 | tf_op jit(solution)/shard_map/ppermute | solution.py:189
  57.0 2.3 %collective-permute-start.19 = (f32[128,128]{1,0:T(8,128)S(1)}, f32[128,128]{1,0:T(8,128)S(1)}, u32[]{:S(2)}, u32[]{:S(2)}) collective-permute-start(f32[128,128]{1,0:T(8,128)S(1)} %add.279), channel_id=1, source_target_pairs={{0,4},{1,5},{2,6},{3,7},{4,0},{5,1},{6,2},{7,3},{8,12},{9,13},{10,... | collective-permute-start | bytes 196616 | tf_op jit(solution)/shard_map/ppermute | solution.py:189
  59.3 2.3 %collective-permute-done.17 = f32[128,128]{1,0:T(8,128)S(1)} collective-permute-done((f32[128,128]{1,0:T(8,128)S(1)}, f32[128,128]{1,0:T(8,128)S(1)}, u32[]{:S(2)}, u32[]{:S(2)}) %collective-permute-start.17) | collective-permute-done | bytes 65568 | tf_op jit(solution)/shard_map/ppermute | solution.py:189
  62.0 2.7 %collective-permute-start.20 = (f32[128,128]{1,0:T(8,128)S(1)}, f32[128,128]{1,0:T(8,128)S(1)}, u32[]{:S(2)}, u32[]{:S(2)}) collective-permute-start(f32[128,128]{1,0:T(8,128)S(1)} %add_add_fusion), channel_id=1, source_target_pairs={{0,8},{1,9},{2,10},{3,11},{4,12},{5,13},{6,14},{7,15},{8,0},{9,1},... | collective-permute-start | bytes 196616 | tf_op jit(solution)/shard_map/ppermute | solution.py:189
  64.7 2.5 %collective-permute-done.20 = f32[128,128]{1,0:T(8,128)S(1)} collective-permute-done((f32[128,128]{1,0:T(8,128)S(1)}, f32[128,128]{1,0:T(8,128)S(1)}, u32[]{:S(2)}, u32[]{:S(2)}) %collective-permute-start.20) | collective-permute-done | bytes 65568 | tf_op jit(solution)/shard_map/ppermute | solution.py:189
  67.3 1.2 %collective-permute-done.21 = f32[128,128]{1,0:T(8,128)S(1)} collective-permute-done((f32[128,128]{1,0:T(8,128)S(1)}, f32[128,128]{1,0:T(8,128)S(1)}, u32[]{:S(2)}, u32[]{:S(2)}) %collective-permute-start.21) | collective-permute-done | bytes 65568 | tf_op jit(solution)/shard_map/ppermute | solution.py:189
  68.6 1.5 %fusion.22 = f32[8,64]{1,0:T(8,128)} fusion(f32[8,4096]{1,0:T(8,128)S(1)} %reshape.236, f32[64,4096]{1,0:T(8,128)S(1)} %copy-done), kind=kOutput, calls=%fused_computation.56 | convolution fusion | flops 25165824 | bytes 1181696 | tf_op jit(solution)/shard_map/dot_general | solution.py:277
  (54 shorter events, 7.1 us)
Async XLA Ops:
  0.0 68.6 %copy-start = (f32[64,4096]{1,0:T(8,128)S(1)}, f32[64,4096]{1,0:T(8,128)}, u32[]{:S(2)}) copy-start(f32[64,4096]{1,0:T(8,128)} %param.11) | copy-start | bytes 3145732
  0.0 17.6 %copy-start.1 = (s32[8192]{0:T(1024)S(1)}, s32[8192]{0:T(1024)}, u32[]{:S(2)}) copy-start(s32[8192]{0:T(1024)} %param.10) | copy-start | bytes 98308
  16.5 2.1 %collective-permute-start = (f32[1024,128]{1,0:T(8,128)S(1)}, f32[1024,128]{1,0:T(8,128)S(1)}, u32[]{:S(2)}, u32[]{:S(2)}) collective-permute-start(f32[1024,128]{1,0:T(8,128)S(1)} %get-tuple-element.31), channel_id=1, source_target_pairs={{0,1},{1,0},{2,3},{3,2},{4,5},{5,4},{6,7},{7,6},{8,9},{9,8},{10,11... | collective-permute-start | bytes 1572872 | tf_op jit(solution)/shard_map/ppermute | solution.py:189
  17.1 4.5 %collective-permute-start.4 = (f32[1024,128]{1,0:T(8,128)S(1)}, f32[1024,128]{1,0:T(8,128)S(1)}, u32[]{:S(2)}, u32[]{:S(2)}) collective-permute-start(f32[1024,128]{1,0:T(8,128)S(1)} %get-tuple-element.37), channel_id=1, source_target_pairs={{0,1},{1,0},{2,3},{3,2},{4,5},{5,4},{6,7},{7,6},{8,9},{9,8},{10,11... | collective-permute-start | bytes 1572872 | tf_op jit(solution)/shard_map/ppermute | solution.py:189
  17.1 6.1 %collective-permute-start.3 = (f32[1024,128]{1,0:T(8,128)S(1)}, f32[1024,128]{1,0:T(8,128)S(1)}, u32[]{:S(2)}, u32[]{:S(2)}) collective-permute-start(f32[1024,128]{1,0:T(8,128)S(1)} %get-tuple-element.35), channel_id=1, source_target_pairs={{0,1},{1,0},{2,3},{3,2},{4,5},{5,4},{6,7},{7,6},{8,9},{9,8},{10,11... | collective-permute-start | bytes 1572872 | tf_op jit(solution)/shard_map/ppermute | solution.py:189
  17.6 6.5 %collective-permute-start.2 = (f32[1024,128]{1,0:T(8,128)S(1)}, f32[1024,128]{1,0:T(8,128)S(1)}, u32[]{:S(2)}, u32[]{:S(2)}) collective-permute-start(f32[1024,128]{1,0:T(8,128)S(1)} %get-tuple-element.33), channel_id=1, source_target_pairs={{0,1},{1,0},{2,3},{3,2},{4,5},{5,4},{6,7},{7,6},{8,9},{9,8},{10,11... | collective-permute-start | bytes 1572872 | tf_op jit(solution)/shard_map/ppermute | solution.py:189
  18.6 10.0 %collective-permute-start.1 = (f32[512,128]{1,0:T(8,128)S(1)}, f32[512,128]{1,0:T(8,128)S(1)}, u32[]{:S(2)}, u32[]{:S(2)}) collective-permute-start(f32[512,128]{1,0:T(8,128)S(1)} %get-tuple-element.58), channel_id=1, source_target_pairs={{0,2},{1,3},{2,0},{3,1},{4,6},{5,7},{6,4},{7,5},{8,10},{9,11},{10,... | collective-permute-start | bytes 786440 | tf_op jit(solution)/shard_map/ppermute | solution.py:189
  21.6 9.3 %collective-permute-start.8 = (f32[512,128]{1,0:T(8,128)S(1)}, f32[512,128]{1,0:T(8,128)S(1)}, u32[]{:S(2)}, u32[]{:S(2)}) collective-permute-start(f32[512,128]{1,0:T(8,128)S(1)} %bitcast.115), channel_id=1, source_target_pairs={{0,4},{1,5},{2,6},{3,7},{4,0},{5,1},{6,2},{7,3},{8,12},{9,13},{10,... | collective-permute-start | bytes 786440 | tf_op jit(solution)/shard_map/ppermute | solution.py:189
  23.3 11.0 %collective-permute-start.7 = (f32[512,128]{1,0:T(8,128)S(1)}, f32[512,128]{1,0:T(8,128)S(1)}, u32[]{:S(2)}, u32[]{:S(2)}) collective-permute-start(f32[512,128]{1,0:T(8,128)S(1)} %get-tuple-element.56), channel_id=1, source_target_pairs={{0,2},{1,3},{2,0},{3,1},{4,6},{5,7},{6,4},{7,5},{8,10},{9,11},{10,... | collective-permute-start | bytes 786440 | tf_op jit(solution)/shard_map/ppermute | solution.py:189
  24.1 12.4 %collective-permute-start.6 = (f32[512,128]{1,0:T(8,128)S(1)}, f32[512,128]{1,0:T(8,128)S(1)}, u32[]{:S(2)}, u32[]{:S(2)}) collective-permute-start(f32[512,128]{1,0:T(8,128)S(1)} %bitcast.113), channel_id=1, source_target_pairs={{0,4},{1,5},{2,6},{3,7},{4,0},{5,1},{6,2},{7,3},{8,12},{9,13},{10,... | collective-permute-start | bytes 786440 | tf_op jit(solution)/shard_map/ppermute | solution.py:189
  28.7 10.6 %collective-permute-start.5 = (f32[256,128]{1,0:T(8,128)S(1)}, f32[256,128]{1,0:T(8,128)S(1)}, u32[]{:S(2)}, u32[]{:S(2)}) collective-permute-start(f32[256,128]{1,0:T(8,128)S(1)} %get-tuple-element.66), channel_id=1, source_target_pairs={{0,4},{1,5},{2,6},{3,7},{4,0},{5,1},{6,2},{7,3},{8,12},{9,13},{10,... | collective-permute-start | bytes 393224 | tf_op jit(solution)/shard_map/ppermute | solution.py:189
  30.9 11.1 %collective-permute-start.12 = (f32[256,128]{1,0:T(8,128)S(1)}, f32[256,128]{1,0:T(8,128)S(1)}, u32[]{:S(2)}, u32[]{:S(2)}) collective-permute-start(f32[256,128]{1,0:T(8,128)S(1)} %get-tuple-element.64), channel_id=1, source_target_pairs={{0,2},{1,3},{2,0},{3,1},{4,6},{5,7},{6,4},{7,5},{8,10},{9,11},{10,... | collective-permute-start | bytes 393224 | tf_op jit(solution)/shard_map/ppermute | solution.py:189
  34.3 8.1 %collective-permute-start.11 = (f32[256,128]{1,0:T(8,128)S(1)}, f32[256,128]{1,0:T(8,128)S(1)}, u32[]{:S(2)}, u32[]{:S(2)}) collective-permute-start(f32[256,128]{1,0:T(8,128)S(1)} %get-tuple-element.62), channel_id=1, source_target_pairs={{0,4},{1,5},{2,6},{3,7},{4,0},{5,1},{6,2},{7,3},{8,12},{9,13},{10,... | collective-permute-start | bytes 393224 | tf_op jit(solution)/shard_map/ppermute | solution.py:189
  36.6 8.5 %collective-permute-start.10 = (f32[256,128]{1,0:T(8,128)S(1)}, f32[256,128]{1,0:T(8,128)S(1)}, u32[]{:S(2)}, u32[]{:S(2)}) collective-permute-start(f32[256,128]{1,0:T(8,128)S(1)} %get-tuple-element.60), channel_id=1, source_target_pairs={{0,2},{1,3},{2,0},{3,1},{4,6},{5,7},{6,4},{7,5},{8,10},{9,11},{10,... | collective-permute-start | bytes 393224 | tf_op jit(solution)/shard_map/ppermute | solution.py:189
  39.3 10.1 %collective-permute-start.9 = (f32[128,128]{1,0:T(8,128)S(1)}, f32[128,128]{1,0:T(8,128)S(1)}, u32[]{:S(2)}, u32[]{:S(2)}) collective-permute-start(f32[128,128]{1,0:T(8,128)S(1)} %fusion.19), channel_id=1, source_target_pairs={{0,8},{1,9},{2,10},{3,11},{4,12},{5,13},{6,14},{7,15},{8,0},{9,1},... | collective-permute-start | bytes 196616 | tf_op jit(solution)/shard_map/ppermute | solution.py:189
  42.0 9.5 %collective-permute-start.13 = (f32[128,128]{1,0:T(8,128)S(1)}, f32[128,128]{1,0:T(8,128)S(1)}, u32[]{:S(2)}, u32[]{:S(2)}) collective-permute-start(f32[128,128]{1,0:T(8,128)S(1)} %fusion.18), channel_id=1, source_target_pairs={{0,8},{1,9},{2,10},{3,11},{4,12},{5,13},{6,14},{7,15},{8,0},{9,1},... | collective-permute-start | bytes 196616 | tf_op jit(solution)/shard_map/ppermute | solution.py:189
  42.4 9.9 %collective-permute-start.14 = (f32[128,128]{1,0:T(8,128)S(1)}, f32[128,128]{1,0:T(8,128)S(1)}, u32[]{:S(2)}, u32[]{:S(2)}) collective-permute-start(f32[128,128]{1,0:T(8,128)S(1)} %fusion.17), channel_id=1, source_target_pairs={{0,8},{1,9},{2,10},{3,11},{4,12},{5,13},{6,14},{7,15},{8,0},{9,1},... | collective-permute-start | bytes 196616 | tf_op jit(solution)/shard_map/ppermute | solution.py:189
  45.1 7.9 %collective-permute-start.15 = (f32[128,128]{1,0:T(8,128)S(1)}, f32[128,128]{1,0:T(8,128)S(1)}, u32[]{:S(2)}, u32[]{:S(2)}) collective-permute-start(f32[128,128]{1,0:T(8,128)S(1)} %fusion.16), channel_id=1, source_target_pairs={{0,8},{1,9},{2,10},{3,11},{4,12},{5,13},{6,14},{7,15},{8,0},{9,1},... | collective-permute-start | bytes 196616 | tf_op jit(solution)/shard_map/ppermute | solution.py:189
  54.4 1.3 %collective-permute-start.16 = (f32[128,128]{1,0:T(8,128)S(1)}, f32[128,128]{1,0:T(8,128)S(1)}, u32[]{:S(2)}, u32[]{:S(2)}) collective-permute-start(f32[128,128]{1,0:T(8,128)S(1)} %get-tuple-element.54), channel_id=1, source_target_pairs={{0,1},{1,0},{2,3},{3,2},{4,5},{5,4},{6,7},{7,6},{8,9},{9,8},{10,11... | collective-permute-start | bytes 196616 | tf_op jit(solution)/shard_map/ppermute | solution.py:189
  55.8 5.9 %collective-permute-start.17 = (f32[128,128]{1,0:T(8,128)S(1)}, f32[128,128]{1,0:T(8,128)S(1)}, u32[]{:S(2)}, u32[]{:S(2)}) collective-permute-start(f32[128,128]{1,0:T(8,128)S(1)} %add.279), channel_id=1, source_target_pairs={{0,6},{1,7},{2,4},{3,5},{4,2},{5,3},{6,0},{7,1},{8,14},{9,15},{10,... | collective-permute-start | bytes 196616 | tf_op jit(solution)/shard_map/ppermute | solution.py:189
  56.1 5.5 %collective-permute-start.18 = (f32[128,128]{1,0:T(8,128)S(1)}, f32[128,128]{1,0:T(8,128)S(1)}, u32[]{:S(2)}, u32[]{:S(2)}) collective-permute-start(f32[128,128]{1,0:T(8,128)S(1)} %add.279), channel_id=1, source_target_pairs={{0,2},{1,3},{2,0},{3,1},{4,6},{5,7},{6,4},{7,5},{8,10},{9,11},{10,... | collective-permute-start | bytes 196616 | tf_op jit(solution)/shard_map/ppermute | solution.py:189
  57.0 4.9 %collective-permute-start.19 = (f32[128,128]{1,0:T(8,128)S(1)}, f32[128,128]{1,0:T(8,128)S(1)}, u32[]{:S(2)}, u32[]{:S(2)}) collective-permute-start(f32[128,128]{1,0:T(8,128)S(1)} %add.279), channel_id=1, source_target_pairs={{0,4},{1,5},{2,6},{3,7},{4,0},{5,1},{6,2},{7,3},{8,12},{9,13},{10,... | collective-permute-start | bytes 196616 | tf_op jit(solution)/shard_map/ppermute | solution.py:189
  62.0 5.2 %collective-permute-start.20 = (f32[128,128]{1,0:T(8,128)S(1)}, f32[128,128]{1,0:T(8,128)S(1)}, u32[]{:S(2)}, u32[]{:S(2)}) collective-permute-start(f32[128,128]{1,0:T(8,128)S(1)} %add_add_fusion), channel_id=1, source_target_pairs={{0,8},{1,9},{2,10},{3,11},{4,12},{5,13},{6,14},{7,15},{8,0},{9,1},... | collective-permute-start | bytes 196616 | tf_op jit(solution)/shard_map/ppermute | solution.py:189
  67.2 1.3 %collective-permute-start.21 = (f32[128,128]{1,0:T(8,128)S(1)}, f32[128,128]{1,0:T(8,128)S(1)}, u32[]{:S(2)}, u32[]{:S(2)}) collective-permute-start(f32[128,128]{1,0:T(8,128)S(1)} %add.283), channel_id=1, source_target_pairs={{0,1},{1,0},{2,3},{3,2},{4,5},{5,4},{6,7},{7,6},{8,9},{9,8},{10,11... | collective-permute-start | bytes 196616 | tf_op jit(solution)/shard_map/ppermute | solution.py:189

commit v7 on v6

--- a/solution.py
+++ b/solution.py
@@ -9,7 +9,7 @@
 
 SEQS = 8
 UNITS = 16
-CHUNKS = (4, 4, 4, 4)
+CHUNKS = (4, 4, 5, 3)
 BOTH_SIDES = 0
 RING = 4
 COST = 1

time: 70.3 us -> 70.1 us (level)
  transfers between devices with their start and end apart: 22 -> 22, of which waited for: 13 -> 11; matrix products, arithmetic and copies ran while one was open for 1% -> 1% of each run, Pallas kernels for 0% -> 0%
where the time goes in v7:
time: 70.1 us; the launch traced here: 70 us
  starting transfers between devices  27.1 us (39%)
  waiting for transfers between devices  22.5 us (32%)
  Pallas kernels  16.8 us (24%)
  other arithmetic  1.82 us (3%)
  matrix products  1.52 us (2%)
    ppermute x22, starting transfers between devices, exchange(): return lax.ppermute(value, 'tp', [(i, i ^ mask) for i in range(devices)])  27.1 us
    ppermute x22, waiting for transfers between devices, exchange(): return lax.ppermute(value, 'tp', [(i, i ^ mask) for i in range(devices)])  22.5 us
    pallas_call x1, Pallas kernels, project(): pl.pallas_call(functools.partial(project_kernel, bits, tokens >> bits, fi...  15.4 us
    dot_general x1, matrix products, shards(): jnp.dot(pair.reshape(SEQS, rank * rank), queries.T, precision=lax.Precisi...  1.52 us
  transfers between devices with their start and end apart: 22, of which 11 were waited for; matrix products, arithmetic and copies ran while one was open for 1% of the time, Pallas kernels for 0%

profile of v7, /device:TPU:0, one launch (start us, length us, event | category | flops | bytes accessed | tf_op | source)
XLA Modules:
  0.0 70.0 jit_solution(4336445375210520343)
XLA Ops:
  0.0 1.1 %pad_maximum_fusion.w_hbm = bf16[64,2304]{1,0:T(8,128)(2,1)S(1)} fusion(bf16[64,1792]{1,0:T(8,128)(2,1)} %bitcast.114, bf16[64,512]{1,0:T(8,128)(2,1)} %bitcast.125), kind=kLoop, calls=%fused_computation.5 | loop fusion | flops 589824 | bytes 589824 | tf_op jit(solution)/shard_map/concatenate | solution.py:202
  1.1 15.4 %project.1 = (f32[1024,128]{1,0:T(8,128)S(1)}, f32[1024,128]{1,0:T(8,128)S(1)}, f32[1024,128]{1,0:T(8,128)S(1)}, f32[1024,128]{1,0:T(8,128)S(1)}, f32[1280,128]{...) custom-call(bf16[8192,512]{1,0:T(8,128)(2,1)} %a_hbm.1, ...), custom_call_target="tpu_custom_call" | custom-call | flops 1 | bytes 1 | tf_op jit(solution)/shard_map/project/pallas_call | solution.py:102
  18.6 2.9 %collective-permute-start.1 = (f32[512,128]{1,0:T(8,128)S(1)}, f32[512,128]{1,0:T(8,128)S(1)}, u32[]{:S(2)}, u32[]{:S(2)}) collective-permute-start(f32[512,128]{1,0:T(8,128)S(1)} %get-tuple-element.58), channel_id=1, source_target_pairs={{0,2},{1,3},{2,0},{3,1},{4,6},{5,7},{6,4},{7,5},{8,10},{9,11},{10,... | collective-permute-start | bytes 786440 | tf_op jit(solution)/shard_map/ppermute | solution.py:189
  21.6 1.6 %collective-permute-start.8 = (f32[512,128]{1,0:T(8,128)S(1)}, f32[512,128]{1,0:T(8,128)S(1)}, u32[]{:S(2)}, u32[]{:S(2)}) collective-permute-start(f32[512,128]{1,0:T(8,128)S(1)} %bitcast.113), channel_id=1, source_target_pairs={{0,4},{1,5},{2,6},{3,7},{4,0},{5,1},{6,2},{7,3},{8,12},{9,13},{10,... | collective-permute-start | bytes 786440 | tf_op jit(solution)/shard_map/ppermute | solution.py:189
  24.1 0.9 %collective-permute-start.6 = (f32[384,128]{1,0:T(8,128)S(1)}, f32[384,128]{1,0:T(8,128)S(1)}, u32[]{:S(2)}, u32[]{:S(2)}) collective-permute-start(f32[384,128]{1,0:T(8,128)S(1)} %bitcast.116), channel_id=1, source_target_pairs={{0,4},{1,5},{2,6},{3,7},{4,0},{5,1},{6,2},{7,3},{8,12},{9,13},{10,... | collective-permute-start | bytes 589832 | tf_op jit(solution)/shard_map/ppermute | solution.py:189
  25.0 3.7 %collective-permute-done.1 = f32[512,128]{1,0:T(8,128)S(1)} collective-permute-done((f32[512,128]{1,0:T(8,128)S(1)}, f32[512,128]{1,0:T(8,128)S(1)}, u32[]{:S(2)}, u32[]{:S(2)}) %collective-permute-start.1) | collective-permute-done | bytes 262176 | tf_op jit(solution)/shard_map/ppermute | solution.py:189
  28.7 2.2 %collective-permute-start.5 = (f32[256,128]{1,0:T(8,128)S(1)}, f32[256,128]{1,0:T(8,128)S(1)}, u32[]{:S(2)}, u32[]{:S(2)}) collective-permute-start(f32[256,128]{1,0:T(8,128)S(1)} %get-tuple-element.64), channel_id=1, source_target_pairs={{0,4},{1,5},{2,6},{3,7},{4,0},{5,1},{6,2},{7,3},{8,12},{9,13},{10,... | collective-permute-start | bytes 393224 | tf_op jit(solution)/shard_map/ppermute | solution.py:189
  30.9 1.6 %collective-permute-start.12 = (f32[256,128]{1,0:T(8,128)S(1)}, f32[256,128]{1,0:T(8,128)S(1)}, u32[]{:S(2)}, u32[]{:S(2)}) collective-permute-start(f32[256,128]{1,0:T(8,128)S(1)} %get-tuple-element.62), channel_id=1, source_target_pairs={{0,2},{1,3},{2,0},{3,1},{4,6},{5,7},{6,4},{7,5},{8,10},{9,11},{10,... | collective-permute-start | bytes 393224 | tf_op jit(solution)/shard_map/ppermute | solution.py:189
  32.5 3.2 %collective-permute-done.7 = f32[640,128]{1,0:T(8,128)S(1)} collective-permute-done((f32[640,128]{1,0:T(8,128)S(1)}, f32[640,128]{1,0:T(8,128)S(1)}, u32[]{:S(2)}, u32[]{:S(2)}) %collective-permute-start.7) | collective-permute-done | bytes 327712 | tf_op jit(solution)/shard_map/ppermute | solution.py:189
  35.8 2.2 %collective-permute-start.11 = (f32[320,128]{1,0:T(8,128)S(1)}, f32[320,128]{1,0:T(8,128)S(1)}, u32[]{:S(2)}, u32[]{:S(2)}) collective-permute-start(f32[320,128]{1,0:T(8,128)S(1)} %get-tuple-element.60), channel_id=1, source_target_pairs={{0,4},{1,5},{2,6},{3,7},{4,0},{5,1},{6,2},{7,3},{8,12},{9,13},{10,... | collective-permute-start | bytes 491528 | tf_op jit(solution)/shard_map/ppermute | solution.py:189
  38.0 1.6 %collective-permute-start.10 = (f32[192,128]{1,0:T(8,128)S(1)}, f32[192,128]{1,0:T(8,128)S(1)}, u32[]{:S(2)}, u32[]{:S(2)}) collective-permute-start(f32[192,128]{1,0:T(8,128)S(1)} %get-tuple-element.66), channel_id=1, source_target_pairs={{0,2},{1,3},{2,0},{3,1},{4,6},{5,7},{6,4},{7,5},{8,10},{9,11},{10,... | collective-permute-start | bytes 294920 | tf_op jit(solution)/shard_map/ppermute | solution.py:189
  39.6 2.7 %collective-permute-start.9 = (f32[128,128]{1,0:T(8,128)S(1)}, f32[128,128]{1,0:T(8,128)S(1)}, u32[]{:S(2)}, u32[]{:S(2)}) collective-permute-start(f32[128,128]{1,0:T(8,128)S(1)} %fusion.16), channel_id=1, source_target_pairs={{0,8},{1,9},{2,10},{3,11},{4,12},{5,13},{6,14},{7,15},{8,0},{9,1},... | collective-permute-start | bytes 196616 | tf_op jit(solution)/shard_map/ppermute | solution.py:189
  42.7 2.7 %collective-permute-start.14 = (f32[160,128]{1,0:T(8,128)S(1)}, f32[160,128]{1,0:T(8,128)S(1)}, u32[]{:S(2)}, u32[]{:S(2)}) collective-permute-start(f32[160,128]{1,0:T(8,128)S(1)} %fusion.12), channel_id=1, source_target_pairs={{0,8},{1,9},{2,10},{3,11},{4,12},{5,13},{6,14},{7,15},{8,0},{9,1},... | collective-permute-start | bytes 245768 | tf_op jit(solution)/shard_map/ppermute | solution.py:189
  45.7 3.8 %collective-permute-done.9 = f32[128,128]{1,0:T(8,128)S(1)} collective-permute-done((f32[128,128]{1,0:T(8,128)S(1)}, f32[128,128]{1,0:T(8,128)S(1)}, u32[]{:S(2)}, u32[]{:S(2)}) %collective-permute-start.9) | collective-permute-done | bytes 65568 | tf_op jit(solution)/shard_map/ppermute | solution.py:189
  49.6 1.4 %collective-permute-done.13 = f32[128,128]{1,0:T(8,128)S(1)} collective-permute-done((f32[128,128]{1,0:T(8,128)S(1)}, f32[128,128]{1,0:T(8,128)S(1)}, u32[]{:S(2)}, u32[]{:S(2)}) %collective-permute-start.13) | collective-permute-done | bytes 65568 | tf_op jit(solution)/shard_map/ppermute | solution.py:189
  51.0 1.8 %collective-permute-done.14 = f32[160,128]{1,0:T(8,128)S(1)} collective-permute-done((f32[160,128]{1,0:T(8,128)S(1)}, f32[160,128]{1,0:T(8,128)S(1)}, u32[]{:S(2)}, u32[]{:S(2)}) %collective-permute-start.14) | collective-permute-done | bytes 81952 | tf_op jit(solution)/shard_map/ppermute | solution.py:189
  53.3 1.4 %product.1 = (f32[128,128]{1,0:T(8,128)S(1)}, f32[128,128]{1,0:T(8,128)S(1)}) custom-call(s32[9]{0:T(128)S(1)} %convert_reduce_fusion.edge_ref, f32[8]{0:T(128)S(1)} %convert_divide_fusion.scale_ref, f32[128,128]{1,0:T(8,128)S(1)} %fusion.18.refs_0_, f32[128,128]{1,0:T(8,128)S(1)} %fusion.14.refs_1_, f32[160,128]{1,0:T(8,128)S(1)} %fusion.11.refs_2_, ...), custom_call_target="tpu_custom_call" | custom-call | tf_op jit(solution)/shard_map/product/pallas_call | solution.py:169
  54.7 1.2 %collective-permute-done.16 = f32[128,128]{1,0:T(8,128)S(1)} collective-permute-done((f32[128,128]{1,0:T(8,128)S(1)}, f32[128,128]{1,0:T(8,128)S(1)}, u32[]{:S(2)}, u32[]{:S(2)}) %collective-permute-start.16) | collective-permute-done | bytes 65568 | tf_op jit(solution)/shard_map/ppermute | solution.py:189
  56.6 2.9 %collective-permute-start.19 = (f32[128,128]{1,0:T(8,128)S(1)}, f32[128,128]{1,0:T(8,128)S(1)}, u32[]{:S(2)}, u32[]{:S(2)}) collective-permute-start(f32[128,128]{1,0:T(8,128)S(1)} %add.279), channel_id=1, source_target_pairs={{0,4},{1,5},{2,6},{3,7},{4,0},{5,1},{6,2},{7,3},{8,12},{9,13},{10,... | collective-permute-start | bytes 196616 | tf_op jit(solution)/shard_map/ppermute | solution.py:189
  59.5 2.3 %collective-permute-done.17 = f32[128,128]{1,0:T(8,128)S(1)} collective-permute-done((f32[128,128]{1,0:T(8,128)S(1)}, f32[128,128]{1,0:T(8,128)S(1)}, u32[]{:S(2)}, u32[]{:S(2)}) %collective-permute-start.17) | collective-permute-done | bytes 65568 | tf_op jit(solution)/shard_map/ppermute | solution.py:189
  61.8 2.5 %collective-permute-start.20 = (f32[128,128]{1,0:T(8,128)S(1)}, f32[128,128]{1,0:T(8,128)S(1)}, u32[]{:S(2)}, u32[]{:S(2)}) collective-permute-start(f32[128,128]{1,0:T(8,128)S(1)} %add_add_fusion), channel_id=1, source_target_pairs={{0,8},{1,9},{2,10},{3,11},{4,12},{5,13},{6,14},{7,15},{8,0},{9,1},... | collective-permute-start | bytes 196616 | tf_op jit(solution)/shard_map/ppermute | solution.py:189
  64.3 2.7 %collective-permute-done.20 = f32[128,128]{1,0:T(8,128)S(1)} collective-permute-done((f32[128,128]{1,0:T(8,128)S(1)}, f32[128,128]{1,0:T(8,128)S(1)}, u32[]{:S(2)}, u32[]{:S(2)}) %collective-permute-start.20) | collective-permute-done | bytes 65568 | tf_op jit(solution)/shard_map/ppermute | solution.py:189
  67.1 1.2 %collective-permute-done.21 = f32[128,128]{1,0:T(8,128)S(1)} collective-permute-done((f32[128,128]{1,0:T(8,128)S(1)}, f32[128,128]{1,0:T(8,128)S(1)}, u32[]{:S(2)}, u32[]{:S(2)}) %collective-permute-start.21) | collective-permute-done | bytes 65568 | tf_op jit(solution)/shard_map/ppermute | solution.py:189
  68.5 1.5 %fusion.22 = f32[8,64]{1,0:T(8,128)} fusion(f32[8,4096]{1,0:T(8,128)S(1)} %reshape.236, f32[64,4096]{1,0:T(8,128)S(1)} %copy-done), kind=kOutput, calls=%fused_computation.56 | convolution fusion | flops 25165824 | bytes 1181696 | tf_op jit(solution)/shard_map/dot_general | solution.py:277
  (54 shorter events, 5.4 us)
Async XLA Ops:
  0.0 68.5 %copy-start = (f32[64,4096]{1,0:T(8,128)S(1)}, f32[64,4096]{1,0:T(8,128)}, u32[]{:S(2)}) copy-start(f32[64,4096]{1,0:T(8,128)} %param.11) | copy-start | bytes 3145732
  0.0 17.6 %copy-start.1 = (s32[8192]{0:T(1024)S(1)}, s32[8192]{0:T(1024)}, u32[]{:S(2)}) copy-start(s32[8192]{0:T(1024)} %param.10) | copy-start | bytes 98308
  16.5 2.1 %collective-permute-start = (f32[1024,128]{1,0:T(8,128)S(1)}, f32[1024,128]{1,0:T(8,128)S(1)}, u32[]{:S(2)}, u32[]{:S(2)}) collective-permute-start(f32[1024,128]{1,0:T(8,128)S(1)} %get-tuple-element.31), channel_id=1, source_target_pairs={{0,1},{1,0},{2,3},{3,2},{4,5},{5,4},{6,7},{7,6},{8,9},{9,8},{10,11... | collective-permute-start | bytes 1572872 | tf_op jit(solution)/shard_map/ppermute | solution.py:189
  17.1 4.5 %collective-permute-start.4 = (f32[1024,128]{1,0:T(8,128)S(1)}, f32[1024,128]{1,0:T(8,128)S(1)}, u32[]{:S(2)}, u32[]{:S(2)}) collective-permute-start(f32[1024,128]{1,0:T(8,128)S(1)} %get-tuple-element.37), channel_id=1, source_target_pairs={{0,1},{1,0},{2,3},{3,2},{4,5},{5,4},{6,7},{7,6},{8,9},{9,8},{10,11... | collective-permute-start | bytes 1572872 | tf_op jit(solution)/shard_map/ppermute | solution.py:189
  17.1 6.2 %collective-permute-start.3 = (f32[1280,128]{1,0:T(8,128)S(1)}, f32[1280,128]{1,0:T(8,128)S(1)}, u32[]{:S(2)}, u32[]{:S(2)}) collective-permute-start(f32[1280,128]{1,0:T(8,128)S(1)} %get-tuple-element.35), channel_id=1, source_target_pairs={{0,1},{1,0},{2,3},{3,2},{4,5},{5,4},{6,7},{7,6},{8,9},{9,8},{10,11... | collective-permute-start | bytes 1966088 | tf_op jit(solution)/shard_map/ppermute | solution.py:189
  17.6 6.5 %collective-permute-start.2 = (f32[768,128]{1,0:T(8,128)S(1)}, f32[768,128]{1,0:T(8,128)S(1)}, u32[]{:S(2)}, u32[]{:S(2)}) collective-permute-start(f32[768,128]{1,0:T(8,128)S(1)} %get-tuple-element.33), channel_id=1, source_target_pairs={{0,1},{1,0},{2,3},{3,2},{4,5},{5,4},{6,7},{7,6},{8,9},{9,8},{10,11... | collective-permute-start | bytes 1179656 | tf_op jit(solution)/shard_map/ppermute | solution.py:189
  18.6 10.0 %collective-permute-start.1 = (f32[512,128]{1,0:T(8,128)S(1)}, f32[512,128]{1,0:T(8,128)S(1)}, u32[]{:S(2)}, u32[]{:S(2)}) collective-permute-start(f32[512,128]{1,0:T(8,128)S(1)} %get-tuple-element.58), channel_id=1, source_target_pairs={{0,2},{1,3},{2,0},{3,1},{4,6},{5,7},{6,4},{7,5},{8,10},{9,11},{10,... | collective-permute-start | bytes 786440 | tf_op jit(solution)/shard_map/ppermute | solution.py:189
  21.6 9.3 %collective-permute-start.8 = (f32[512,128]{1,0:T(8,128)S(1)}, f32[512,128]{1,0:T(8,128)S(1)}, u32[]{:S(2)}, u32[]{:S(2)}) collective-permute-start(f32[512,128]{1,0:T(8,128)S(1)} %bitcast.113), channel_id=1, source_target_pairs={{0,4},{1,5},{2,6},{3,7},{4,0},{5,1},{6,2},{7,3},{8,12},{9,13},{10,... | collective-permute-start | bytes 786440 | tf_op jit(solution)/shard_map/ppermute | solution.py:189
  23.4 12.3 %collective-permute-start.7 = (f32[640,128]{1,0:T(8,128)S(1)}, f32[640,128]{1,0:T(8,128)S(1)}, u32[]{:S(2)}, u32[]{:S(2)}) collective-permute-start(f32[640,128]{1,0:T(8,128)S(1)} %get-tuple-element.56), channel_id=1, source_target_pairs={{0,2},{1,3},{2,0},{3,1},{4,6},{5,7},{6,4},{7,5},{8,10},{9,11},{10,... | collective-permute-start | bytes 983048 | tf_op jit(solution)/shard_map/ppermute | solution.py:189
  24.1 13.8 %collective-permute-start.6 = (f32[384,128]{1,0:T(8,128)S(1)}, f32[384,128]{1,0:T(8,128)S(1)}, u32[]{:S(2)}, u32[]{:S(2)}) collective-permute-start(f32[384,128]{1,0:T(8,128)S(1)} %bitcast.116), channel_id=1, source_target_pairs={{0,4},{1,5},{2,6},{3,7},{4,0},{5,1},{6,2},{7,3},{8,12},{9,13},{10,... | collective-permute-start | bytes 589832 | tf_op jit(solution)/shard_map/ppermute | solution.py:189
  28.7 10.8 %collective-permute-start.5 = (f32[256,128]{1,0:T(8,128)S(1)}, f32[256,128]{1,0:T(8,128)S(1)}, u32[]{:S(2)}, u32[]{:S(2)}) collective-permute-start(f32[256,128]{1,0:T(8,128)S(1)} %get-tuple-element.64), channel_id=1, source_target_pairs={{0,4},{1,5},{2,6},{3,7},{4,0},{5,1},{6,2},{7,3},{8,12},{9,13},{10,... | collective-permute-start | bytes 393224 | tf_op jit(solution)/shard_map/ppermute | solution.py:189
  30.9 11.3 %collective-permute-start.12 = (f32[256,128]{1,0:T(8,128)S(1)}, f32[256,128]{1,0:T(8,128)S(1)}, u32[]{:S(2)}, u32[]{:S(2)}) collective-permute-start(f32[256,128]{1,0:T(8,128)S(1)} %get-tuple-element.62), channel_id=1, source_target_pairs={{0,2},{1,3},{2,0},{3,1},{4,6},{5,7},{6,4},{7,5},{8,10},{9,11},{10,... | collective-permute-start | bytes 393224 | tf_op jit(solution)/shard_map/ppermute | solution.py:189
  35.8 6.9 %collective-permute-start.11 = (f32[320,128]{1,0:T(8,128)S(1)}, f32[320,128]{1,0:T(8,128)S(1)}, u32[]{:S(2)}, u32[]{:S(2)}) collective-permute-start(f32[320,128]{1,0:T(8,128)S(1)} %get-tuple-element.60), channel_id=1, source_target_pairs={{0,4},{1,5},{2,6},{3,7},{4,0},{5,1},{6,2},{7,3},{8,12},{9,13},{10,... | collective-permute-start | bytes 491528 | tf_op jit(solution)/shard_map/ppermute | solution.py:189
  38.0 7.4 %collective-permute-start.10 = (f32[192,128]{1,0:T(8,128)S(1)}, f32[192,128]{1,0:T(8,128)S(1)}, u32[]{:S(2)}, u32[]{:S(2)}) collective-permute-start(f32[192,128]{1,0:T(8,128)S(1)} %get-tuple-element.66), channel_id=1, source_target_pairs={{0,2},{1,3},{2,0},{3,1},{4,6},{5,7},{6,4},{7,5},{8,10},{9,11},{10,... | collective-permute-start | bytes 294920 | tf_op jit(solution)/shard_map/ppermute | solution.py:189
  39.6 10.0 %collective-permute-start.9 = (f32[128,128]{1,0:T(8,128)S(1)}, f32[128,128]{1,0:T(8,128)S(1)}, u32[]{:S(2)}, u32[]{:S(2)}) collective-permute-start(f32[128,128]{1,0:T(8,128)S(1)} %fusion.16), channel_id=1, source_target_pairs={{0,8},{1,9},{2,10},{3,11},{4,12},{5,13},{6,14},{7,15},{8,0},{9,1},... | collective-permute-start | bytes 196616 | tf_op jit(solution)/shard_map/ppermute | solution.py:189
  42.2 8.7 %collective-permute-start.13 = (f32[128,128]{1,0:T(8,128)S(1)}, f32[128,128]{1,0:T(8,128)S(1)}, u32[]{:S(2)}, u32[]{:S(2)}) collective-permute-start(f32[128,128]{1,0:T(8,128)S(1)} %fusion.15), channel_id=1, source_target_pairs={{0,8},{1,9},{2,10},{3,11},{4,12},{5,13},{6,14},{7,15},{8,0},{9,1},... | collective-permute-start | bytes 196616 | tf_op jit(solution)/shard_map/ppermute | solution.py:189
  42.7 10.1 %collective-permute-start.14 = (f32[160,128]{1,0:T(8,128)S(1)}, f32[160,128]{1,0:T(8,128)S(1)}, u32[]{:S(2)}, u32[]{:S(2)}) collective-permute-start(f32[160,128]{1,0:T(8,128)S(1)} %fusion.12), channel_id=1, source_target_pairs={{0,8},{1,9},{2,10},{3,11},{4,12},{5,13},{6,14},{7,15},{8,0},{9,1},... | collective-permute-start | bytes 245768 | tf_op jit(solution)/shard_map/ppermute | solution.py:189
  45.3 7.9 %collective-permute-start.15 = (f32[96,128]{1,0:T(8,128)S(1)}, f32[96,128]{1,0:T(8,128)S(1)}, u32[]{:S(2)}, u32[]{:S(2)}) collective-permute-start(f32[96,128]{1,0:T(8,128)S(1)} %fusion.21), channel_id=1, source_target_pairs={{0,8},{1,9},{2,10},{3,11},{4,12},{5,13},{6,14},{7,15},{8,0},{9,1},... | collective-permute-start | bytes 147464 | tf_op jit(solution)/shard_map/ppermute | solution.py:189
  54.6 1.3 %collective-permute-start.16 = (f32[128,128]{1,0:T(8,128)S(1)}, f32[128,128]{1,0:T(8,128)S(1)}, u32[]{:S(2)}, u32[]{:S(2)}) collective-permute-start(f32[128,128]{1,0:T(8,128)S(1)} %get-tuple-element.54), channel_id=1, source_target_pairs={{0,1},{1,0},{2,3},{3,2},{4,5},{5,4},{6,7},{7,6},{8,9},{9,8},{10,11... | collective-permute-start | bytes 196616 | tf_op jit(solution)/shard_map/ppermute | solution.py:189
  56.0 5.8 %collective-permute-start.17 = (f32[128,128]{1,0:T(8,128)S(1)}, f32[128,128]{1,0:T(8,128)S(1)}, u32[]{:S(2)}, u32[]{:S(2)}) collective-permute-start(f32[128,128]{1,0:T(8,128)S(1)} %add.279), channel_id=1, source_target_pairs={{0,6},{1,7},{2,4},{3,5},{4,2},{5,3},{6,0},{7,1},{8,14},{9,15},{10,... | collective-permute-start | bytes 196616 | tf_op jit(solution)/shard_map/ppermute | solution.py:189
  56.0 5.7 %collective-permute-start.18 = (f32[128,128]{1,0:T(8,128)S(1)}, f32[128,128]{1,0:T(8,128)S(1)}, u32[]{:S(2)}, u32[]{:S(2)}) collective-permute-start(f32[128,128]{1,0:T(8,128)S(1)} %add.279), channel_id=1, source_target_pairs={{0,2},{1,3},{2,0},{3,1},{4,6},{5,7},{6,4},{7,5},{8,10},{9,11},{10,... | collective-permute-start | bytes 196616 | tf_op jit(solution)/shard_map/ppermute | solution.py:189
  56.6 5.2 %collective-permute-start.19 = (f32[128,128]{1,0:T(8,128)S(1)}, f32[128,128]{1,0:T(8,128)S(1)}, u32[]{:S(2)}, u32[]{:S(2)}) collective-permute-start(f32[128,128]{1,0:T(8,128)S(1)} %add.279), channel_id=1, source_target_pairs={{0,4},{1,5},{2,6},{3,7},{4,0},{5,1},{6,2},{7,3},{8,12},{9,13},{10,... | collective-permute-start | bytes 196616 | tf_op jit(solution)/shard_map/ppermute | solution.py:189
  61.8 5.2 %collective-permute-start.20 = (f32[128,128]{1,0:T(8,128)S(1)}, f32[128,128]{1,0:T(8,128)S(1)}, u32[]{:S(2)}, u32[]{:S(2)}) collective-permute-start(f32[128,128]{1,0:T(8,128)S(1)} %add_add_fusion), channel_id=1, source_target_pairs={{0,8},{1,9},{2,10},{3,11},{4,12},{5,13},{6,14},{7,15},{8,0},{9,1},... | collective-permute-start | bytes 196616 | tf_op jit(solution)/shard_map/ppermute | solution.py:189
  67.1 1.3 %collective-permute-start.21 = (f32[128,128]{1,0:T(8,128)S(1)}, f32[128,128]{1,0:T(8,128)S(1)}, u32[]{:S(2)}, u32[]{:S(2)}) collective-permute-start(f32[128,128]{1,0:T(8,128)S(1)} %add.283), channel_id=1, source_target_pairs={{0,1},{1,0},{2,3},{3,2},{4,5},{5,4},{6,7},{7,6},{8,9},{9,8},{10,11... | collective-permute-start | bytes 196616 | tf_op jit(solution)/shard_map/ppermute | solution.py:189
